TPU v7x, 32 devices: a whole 2x2x4 slice. The times are simulated.
32 devices in a mesh: dp: 4 (over y, x), seq: 4 (over z), fsdp: 2 (over core).
Axes of the slice: x: 2, y: 2, z: 4, core: 2. Of those that a mesh axis runs over, the one named last changes fastest.
Arguments:
- inputs: bfloat16 [8, 1024, 2048], P('dp', ('seq', 'fsdp')), may hold values from -6 to 6
- block_ids: int32 [8, 1024], P('dp', ('seq', 'fsdp')), may hold values from 0 to 7, never falling along the last dimension, each value on 1 to 256 neighbouring positions
- gain_one: bfloat16 [2048], P(('dp', 'seq', 'fsdp')), may hold values from 0.5 to 1.5
- beta_one: bfloat16 [2048], P(('dp', 'seq', 'fsdp')), may hold values from -3 to 3
- w_qkv: bfloat16 [2048, 6144], P(('dp', 'seq', 'fsdp')), may hold values from -0.125 to 0.125
- bias_query: bfloat16 [2048], P(('dp', 'seq', 'fsdp')), may hold values from -3 to 3
- bias_value: bfloat16 [2048], P(('dp', 'seq', 'fsdp')), may hold values from -3 to 3
- w_out: bfloat16 [2048, 2048], P(('dp', 'seq', 'fsdp')), may hold values from -0.375 to 0.375
- bias_out: bfloat16 [2048], P(('dp', 'seq', 'fsdp')), may hold values from -3 to 3
- gain_two: bfloat16 [2048], P(('dp', 'seq', 'fsdp')), may hold values from 0.5 to 1.5
- beta_two: bfloat16 [2048], P(('dp', 'seq', 'fsdp')), may hold values from -3 to 3
- w_up: bfloat16 [2048, 8192], P(('dp', 'seq', 'fsdp')), may hold values from -0.125 to 0.125
- bias_up: bfloat16 [8192], P(('dp', 'seq', 'fsdp')), may hold values from -3 to 3
- w_down: bfloat16 [8192, 2048], P(('dp', 'seq', 'fsdp')), may hold values from -0.09375 to 0.09375
- bias_down: bfloat16 [2048], P(('dp', 'seq', 'fsdp')), may hold values from -3 to 3
- cotangent: bfloat16 [8, 1024, 2048], P('dp', ('seq', 'fsdp')), may hold values from -6 to 6
Outputs:
- outputs: bfloat16 [8, 1024, 2048], P('dp', ('seq', 'fsdp'))
- grad_inputs: float32 [8, 1024, 2048], P('dp', ('seq', 'fsdp'))
- grad_w_qkv: float32 [2048, 6144], P(('dp', 'seq', 'fsdp'))
- grad_bias_query: float32 [2048], P(('dp', 'seq', 'fsdp'))
- grad_bias_value: float32 [2048], P(('dp', 'seq', 'fsdp'))
- grad_w_out: float32 [2048, 2048], P(('dp', 'seq', 'fsdp'))
- grad_bias_out: float32 [2048], P(('dp', 'seq', 'fsdp'))
- grad_gain_one: float32 [2048], P(('dp', 'seq', 'fsdp'))
- grad_beta_one: float32 [2048], P(('dp', 'seq', 'fsdp'))
- grad_w_up: float32 [2048, 8192], P(('dp', 'seq', 'fsdp'))
- grad_bias_up: float32 [8192], P(('dp', 'seq', 'fsdp'))
- grad_w_down: float32 [8192, 2048], P(('dp', 'seq', 'fsdp'))
- grad_bias_down: float32 [2048], P(('dp', 'seq', 'fsdp'))
- grad_gain_two: float32 [2048], P(('dp', 'seq', 'fsdp'))
- grad_beta_two: float32 [2048], P(('dp', 'seq', 'fsdp'))
Inputs may be any that keep to these rules, and one draw needn't show every extreme that they name: `block_ids`: within each sequence the block ids start at 0 and never fall, rising by at most one from token to token; each block holds 1 to 256 tokens and one block of each sequence holds exactly 256.
All inputs are finite; a program needn't handle non-finite values.
Results may differ from a plain program's by a relative error of at most 0.013.
Values may be sent and summed in bfloat16 or wider, within the bound.
No kernel may reach another device: no remote copies, remote signals or barrier semaphores. Data moves between devices by JAX's collectives and lax.ppermute only.
A program may use at most 512 MiB of HBM per device.

v0:
```python
import jax
import jax.numpy as jnp
from jax import lax
from jax.sharding import PartitionSpec as P

HEADS = 16
HEAD_DIM = 128


EPSILON = 1e-05


def layer_norm(values, gain, shift):
    average = jnp.mean(values, axis=-1, keepdims=True)
    centered = values - average
    variance = jnp.mean(centered * centered, axis=-1, keepdims=True)
    return centered * lax.rsqrt(variance + EPSILON) * gain + shift


def gelu_tanh(values):
    return jax.nn.gelu(values, approximate=True)


def dot_plain(left, right):
    return jnp.dot(left, right, preferred_element_type=jnp.float32)


def dot_right_t(left, right):
    return lax.dot_general(
        left, right, (((1,), (1,)), ((), ())), preferred_element_type=jnp.float32
    )


def dot_left_t(left, right):
    return lax.dot_general(
        left, right, (((0,), (0,)), ((), ())), preferred_element_type=jnp.float32
    )


def softmax_rows(query_head, key_head, slope, distance, allowed, score_scale):
    raw_scores = jnp.einsum(
        "mcd,mld->mcl", query_head, key_head, preferred_element_type=jnp.float32
    )
    scores = raw_scores * score_scale - slope * distance
    scores = jnp.where(allowed, scores, -1e30)
    row_max = jnp.max(scores, axis=-1, keepdims=True)
    exponent = jnp.exp(scores - row_max)
    total = jnp.sum(exponent, axis=-1, keepdims=True)
    return (exponent / total, row_max[..., 0], total[..., 0])


def on_device(
    inputs,
    block_ids,
    gain_one,
    beta_one,
    w_qkv,
    bias_query,
    bias_value,
    w_out,
    bias_out,
    gain_two,
    beta_two,
    w_up,
    bias_up,
    w_down,
    bias_down,
    cotangent,
):
    micro_count, group_len, model_width = inputs.shape
    total_rows = micro_count * group_len
    head_dim = HEAD_DIM
    head_count = HEADS
    score_scale = HEAD_DIM ** (-0.5)
    seq_length = group_len * lax.axis_size(("seq", "fsdp"))
    attention_params = (
        lax.all_gather(w_qkv, ("dp", "seq", "fsdp"), axis=0, tiled=True),
        lax.all_gather(w_out, ("dp", "seq", "fsdp"), axis=0, tiled=True),
        lax.all_gather(bias_query, ("dp", "seq", "fsdp"), axis=0, tiled=True),
        lax.all_gather(bias_value, ("dp", "seq", "fsdp"), axis=0, tiled=True),
        lax.all_gather(bias_out, ("dp", "seq", "fsdp"), axis=0, tiled=True),
        lax.all_gather(gain_one, ("dp", "seq", "fsdp"), axis=0, tiled=True),
        lax.all_gather(beta_one, ("dp", "seq", "fsdp"), axis=0, tiled=True),
    )
    (
        qkv_full,
        out_full,
        query_bias_full,
        value_bias_full,
        out_bias_full,
        gain_one_full,
        beta_one_full,
    ) = attention_params
    first_row = lax.axis_index(("seq", "fsdp")) * group_len
    query_pos = (first_row + jnp.arange(group_len)).astype(jnp.float32)
    key_pos = jnp.arange(seq_length).astype(jnp.float32)
    distance = jnp.abs(query_pos[:, None] - key_pos[None, :])
    slopes = jnp.exp2(-8.0 * (jnp.arange(head_count, dtype=jnp.float32) + 1.0) / head_count)
    tokens_flat = inputs.astype(jnp.float32).reshape(total_rows, model_width)
    normed_f, norm_one_back = jax.vjp(
        layer_norm,
        tokens_flat,
        gain_one_full.astype(jnp.float32),
        beta_one_full.astype(jnp.float32),
    )
    normed_one = normed_f.astype(jnp.bfloat16)
    projected = dot_plain(normed_one, qkv_full)
    query = (projected[:, :model_width] + query_bias_full.astype(jnp.float32)).astype(jnp.bfloat16)
    keys_proj = projected[:, model_width : 2 * model_width].astype(jnp.bfloat16)
    value = (projected[:, 2 * model_width :] + value_bias_full.astype(jnp.float32)).astype(
        jnp.bfloat16
    )
    query_three = query.reshape(micro_count, group_len, model_width)
    keys_three = keys_proj.reshape(micro_count, group_len, model_width)
    values_three = value.reshape(micro_count, group_len, model_width)
    ids_low = block_ids.astype(jnp.bfloat16)
    keys_all, values_all, ids_all = (
        lax.all_gather(keys_three, ("seq", "fsdp"), axis=1, tiled=True),
        lax.all_gather(values_three, ("seq", "fsdp"), axis=1, tiled=True),
        lax.all_gather(ids_low, ("seq", "fsdp"), axis=1, tiled=True),
    )
    ids_all_f = ids_all.astype(jnp.float32)
    ids_local_f = block_ids.astype(jnp.float32)
    allowed = ids_all_f[:, None, :] <= ids_local_f[:, :, None]

    def head_forward(head_index, carried):
        attention, maxima, totals = carried
        columns = head_index * head_dim
        query_head = lax.dynamic_slice_in_dim(query_three, columns, head_dim, 2)
        key_head = lax.dynamic_slice_in_dim(keys_all, columns, head_dim, 2)
        value_head = lax.dynamic_slice_in_dim(values_all, columns, head_dim, 2)
        probs, row_max, row_sum = softmax_rows(
            query_head, key_head, slopes[head_index], distance, allowed, score_scale
        )
        head_out = jnp.einsum(
            "mcl,mld->mcd",
            probs.astype(jnp.bfloat16),
            value_head,
            preferred_element_type=jnp.float32,
        )
        attention = lax.dynamic_update_slice_in_dim(attention, head_out, columns, 2)
        maxima = lax.dynamic_update_slice_in_dim(maxima, row_max[..., None], head_index, 2)
        totals = lax.dynamic_update_slice_in_dim(totals, row_sum[..., None], head_index, 2)
        return (attention, maxima, totals)

    zero_stats = jnp.zeros((micro_count, group_len, head_count), jnp.float32)
    attention, row_maxima, row_sums = lax.fori_loop(
        0,
        head_count,
        head_forward,
        (jnp.zeros((micro_count, group_len, model_width), jnp.float32), zero_stats, zero_stats),
    )
    context = attention.astype(jnp.bfloat16).reshape(total_rows, model_width)
    residual = tokens_flat + dot_plain(context, out_full) + out_bias_full.astype(jnp.float32)
    feed_params = (
        lax.all_gather(w_up, ("dp", "seq", "fsdp"), axis=0, tiled=True),
        lax.all_gather(w_down, ("dp", "seq", "fsdp"), axis=0, tiled=True),
        lax.all_gather(bias_up, ("dp", "seq", "fsdp"), axis=0, tiled=True),
        lax.all_gather(bias_down, ("dp", "seq", "fsdp"), axis=0, tiled=True),
        lax.all_gather(gain_two, ("dp", "seq", "fsdp"), axis=0, tiled=True),
        lax.all_gather(beta_two, ("dp", "seq", "fsdp"), axis=0, tiled=True),
    )
    up_full, down_full, up_bias_full, down_bias_full, gain_two_full, beta_two_full = feed_params
    normed_g, norm_two_back = jax.vjp(
        layer_norm, residual, gain_two_full.astype(jnp.float32), beta_two_full.astype(jnp.float32)
    )
    normed_two = normed_g.astype(jnp.bfloat16)
    hidden = dot_plain(normed_two, up_full) + up_bias_full.astype(jnp.float32)
    activated_f, gelu_back = jax.vjp(gelu_tanh, hidden)
    activated = activated_f.astype(jnp.bfloat16)
    result = residual + dot_plain(activated, down_full) + down_bias_full.astype(jnp.float32)
    outputs = result.astype(jnp.bfloat16).reshape(micro_count, group_len, model_width)
    feed_back = (
        lax.all_gather(w_up, ("dp", "seq", "fsdp"), axis=0, tiled=True),
        lax.all_gather(w_down, ("dp", "seq", "fsdp"), axis=0, tiled=True),
        lax.all_gather(bias_up, ("dp", "seq", "fsdp"), axis=0, tiled=True),
        lax.all_gather(bias_down, ("dp", "seq", "fsdp"), axis=0, tiled=True),
        lax.all_gather(gain_two, ("dp", "seq", "fsdp"), axis=0, tiled=True),
        lax.all_gather(beta_two, ("dp", "seq", "fsdp"), axis=0, tiled=True),
    )
    up_back = feed_back[0]
    down_back = feed_back[1]
    grad_out_flat = cotangent.reshape(total_rows, model_width)
    grad_out_f = grad_out_flat.astype(jnp.float32)
    grad_activated = dot_right_t(grad_out_flat, down_back)
    grad_hidden = gelu_back(grad_activated)[0].astype(jnp.bfloat16)
    grad_w_up = dot_left_t(normed_two, grad_hidden)
    grad_bias_up = jnp.sum(grad_hidden.astype(jnp.float32), axis=0)
    grad_w_down = dot_left_t(activated, grad_out_flat)
    grad_bias_down = jnp.sum(grad_out_f, axis=0)
    grad_normed_two = dot_right_t(grad_hidden, up_back)
    residual_part, grad_gain_two, grad_beta_two = norm_two_back(grad_normed_two)
    grad_residual = grad_out_f + residual_part
    feed_grads = (
        lax.psum_scatter(grad_w_up, ("dp", "seq", "fsdp"), scatter_dimension=0, tiled=True),
        lax.psum_scatter(grad_w_down, ("dp", "seq", "fsdp"), scatter_dimension=0, tiled=True),
        lax.psum_scatter(grad_bias_up, ("dp", "seq", "fsdp"), scatter_dimension=0, tiled=True),
        lax.psum_scatter(grad_bias_down, ("dp", "seq", "fsdp"), scatter_dimension=0, tiled=True),
        lax.psum_scatter(grad_gain_two, ("dp", "seq", "fsdp"), scatter_dimension=0, tiled=True),
        lax.psum_scatter(grad_beta_two, ("dp", "seq", "fsdp"), scatter_dimension=0, tiled=True),
    )
    attention_back = (
        lax.all_gather(w_qkv, ("dp", "seq", "fsdp"), axis=0, tiled=True),
        lax.all_gather(w_out, ("dp", "seq", "fsdp"), axis=0, tiled=True),
        lax.all_gather(bias_query, ("dp", "seq", "fsdp"), axis=0, tiled=True),
        lax.all_gather(bias_value, ("dp", "seq", "fsdp"), axis=0, tiled=True),
        lax.all_gather(bias_out, ("dp", "seq", "fsdp"), axis=0, tiled=True),
        lax.all_gather(gain_one, ("dp", "seq", "fsdp"), axis=0, tiled=True),
        lax.all_gather(beta_one, ("dp", "seq", "fsdp"), axis=0, tiled=True),
    )
    qkv_back = attention_back[0]
    out_back = attention_back[1]
    grad_branch = grad_residual.astype(jnp.bfloat16)
    grad_w_out = dot_left_t(context, grad_branch)
    grad_bias_out = jnp.sum(grad_residual, axis=0)
    grad_context = (
        dot_right_t(grad_branch, out_back)
        .astype(jnp.bfloat16)
        .reshape(micro_count, group_len, model_width)
    )
    keys_again, values_again = (
        lax.all_gather(keys_three, ("seq", "fsdp"), axis=1, tiled=True),
        lax.all_gather(values_three, ("seq", "fsdp"), axis=1, tiled=True),
    )
    zero_local = jnp.zeros((micro_count, group_len, model_width), jnp.float32)

    def head_backward(head_index, carried):
        grad_query, grad_keys, grad_values = carried
        columns = head_index * head_dim
        query_head = lax.dynamic_slice_in_dim(query_three, columns, head_dim, 2)
        key_head = lax.dynamic_slice_in_dim(keys_again, columns, head_dim, 2)
        value_head = lax.dynamic_slice_in_dim(values_again, columns, head_dim, 2)
        grad_head = lax.dynamic_slice_in_dim(grad_context, columns, head_dim, 2)
        probs = softmax_rows(
            query_head, key_head, slopes[head_index], distance, allowed, score_scale
        )[0]
        probs_low = probs.astype(jnp.bfloat16)
        grad_probs = jnp.einsum(
            "mcd,mld->mcl", grad_head, value_head, preferred_element_type=jnp.float32
        )
        grad_value_head = jnp.einsum(
            "mcl,mcd->mld", probs_low, grad_head, preferred_element_type=jnp.float32
        )
        row_total = jnp.sum(probs * grad_probs, axis=-1, keepdims=True)
        grad_scores = (probs * (grad_probs - row_total) * score_scale).astype(jnp.bfloat16)
        grad_query_head = jnp.einsum(
            "mcl,mld->mcd", grad_scores, key_head, preferred_element_type=jnp.float32
        )
        grad_key_head = jnp.einsum(
            "mcl,mcd->mld", grad_scores, query_head, preferred_element_type=jnp.float32
        )
        grad_query = lax.dynamic_update_slice_in_dim(grad_query, grad_query_head, columns, 2)
        grad_keys = lax.dynamic_update_slice_in_dim(grad_keys, grad_key_head, columns, 2)
        grad_values = lax.dynamic_update_slice_in_dim(grad_values, grad_value_head, columns, 2)
        return (grad_query, grad_keys, grad_values)

    zero_whole = jnp.zeros((micro_count, seq_length, model_width), jnp.float32)
    grad_query, grad_keys_all, grad_values_all = lax.fori_loop(
        0, head_count, head_backward, (zero_local, zero_whole, zero_whole)
    )
    grad_keys, grad_values = (
        lax.psum_scatter(
            grad_keys_all.astype(jnp.bfloat16), ("seq", "fsdp"), scatter_dimension=1, tiled=True
        ).astype(jnp.float32),
        lax.psum_scatter(
            grad_values_all.astype(jnp.bfloat16), ("seq", "fsdp"), scatter_dimension=1, tiled=True
        ).astype(jnp.float32),
    )
    grad_query_low = grad_query.astype(jnp.bfloat16).reshape(total_rows, model_width)
    grad_keys_low = grad_keys.astype(jnp.bfloat16).reshape(total_rows, model_width)
    grad_values_low = grad_values.astype(jnp.bfloat16).reshape(total_rows, model_width)
    grad_qkv = jnp.concatenate([grad_query_low, grad_keys_low, grad_values_low], axis=1)
    grad_bias_query = jnp.sum(grad_query_low.astype(jnp.float32), axis=0)
    grad_bias_value = jnp.sum(grad_values_low.astype(jnp.float32), axis=0)
    grad_w_qkv = dot_left_t(normed_one, grad_qkv)
    grad_normed_one = dot_right_t(grad_qkv, qkv_back)
    inputs_part, grad_gain_one, grad_beta_one = norm_one_back(grad_normed_one)
    grad_inputs = (grad_residual + inputs_part).reshape(micro_count, group_len, model_width)
    attention_grads = (
        lax.psum_scatter(grad_w_qkv, ("dp", "seq", "fsdp"), scatter_dimension=0, tiled=True),
        lax.psum_scatter(grad_w_out, ("dp", "seq", "fsdp"), scatter_dimension=0, tiled=True),
        lax.psum_scatter(grad_bias_query, ("dp", "seq", "fsdp"), scatter_dimension=0, tiled=True),
        lax.psum_scatter(grad_bias_value, ("dp", "seq", "fsdp"), scatter_dimension=0, tiled=True),
        lax.psum_scatter(grad_bias_out, ("dp", "seq", "fsdp"), scatter_dimension=0, tiled=True),
        lax.psum_scatter(grad_gain_one, ("dp", "seq", "fsdp"), scatter_dimension=0, tiled=True),
        lax.psum_scatter(grad_beta_one, ("dp", "seq", "fsdp"), scatter_dimension=0, tiled=True),
    )
    return (
        outputs,
        grad_inputs,
        attention_grads[0],
        attention_grads[2],
        attention_grads[3],
        attention_grads[1],
        attention_grads[4],
        attention_grads[5],
        attention_grads[6],
        feed_grads[0],
        feed_grads[2],
        feed_grads[1],
        feed_grads[3],
        feed_grads[4],
        feed_grads[5],
    )


def solution(mesh):
    placed = (
        P("dp", ("seq", "fsdp"), None),
        P("dp", ("seq", "fsdp")),
        P(("dp", "seq", "fsdp")),
        P(("dp", "seq", "fsdp")),
        P(("dp", "seq", "fsdp"), None),
        P(("dp", "seq", "fsdp")),
        P(("dp", "seq", "fsdp")),
        P(("dp", "seq", "fsdp"), None),
        P(("dp", "seq", "fsdp")),
        P(("dp", "seq", "fsdp")),
        P(("dp", "seq", "fsdp")),
        P(("dp", "seq", "fsdp"), None),
        P(("dp", "seq", "fsdp")),
        P(("dp", "seq", "fsdp"), None),
        P(("dp", "seq", "fsdp")),
        P("dp", ("seq", "fsdp"), None),
    )
    return jax.shard_map(
        on_device,
        mesh=mesh,
        in_specs=placed,
        out_specs=(
            P("dp", ("seq", "fsdp"), None),
            P("dp", ("seq", "fsdp"), None),
            P(("dp", "seq", "fsdp"), None),
            P(("dp", "seq", "fsdp")),
            P(("dp", "seq", "fsdp")),
            P(("dp", "seq", "fsdp"), None),
            P(("dp", "seq", "fsdp")),
            P(("dp", "seq", "fsdp")),
            P(("dp", "seq", "fsdp")),
            P(("dp", "seq", "fsdp"), None),
            P(("dp", "seq", "fsdp")),
            P(("dp", "seq", "fsdp"), None),
            P(("dp", "seq", "fsdp")),
            P(("dp", "seq", "fsdp")),
            P(("dp", "seq", "fsdp")),
        ),
        check_vma=False,
    )
```

profile of v0, /device:TPU:0, one launch (start us, length us, event | category | flops | bytes accessed | tf_op | source)
XLA Modules:
  0.0 3511.1 jit_solution(9142961186362723289)
XLA Ops:
  14.8 43.7 %all-reduce.18 = (bf16[2048]{0:T(1024)(128)(2,1)S(1)}, bf16[2048]{0:T(1024)(128)(2,1)S(1)}, bf16[2048]{0:T(1024)(128)(2,1)S(1)}, bf16[2048]{0:T(1024)(128)(2,1)S...) all-reduce(bf16[2048]{0:T(1024)(128)(2,1)S(1)} %dynamic-update-slic, ...), channel_id=1, replica_groups=mesh['dp'=4,'seq'=4,'fsdp'=2] {'dp','seq','fsdp'}, use_global_device_ids=true, to_apply=%add.1 | all-reduce | flops 16384 | bytes 65536
  63.3 106.6 %all-gather.8.cloned.1.call-done = bf16[2048,6144]{1,0:T(8,128)(2,1)} async-done(((bf16[64,6144]{1,0:T(8,128)(2,1)}), bf16[2048,6144]{1,0:T(8,128)(2,1)}) %all-gather.8.cloned.1.call-update) | async-done | bytes 25165840 | tf_op jit(solution)/shard_map/all_gather | solution.py:77
  169.9 11.6 fusion.123
  200.5 38.6 %all-gather = bf16[32,1,256]{2,1,0:T(2,128)(2,1)S(1)} all-gather(bf16[1,1,256]{2,1,0:T(2,128)(2,1)S(1)} %reshape.208), channel_id=1, replica_groups=mesh['dp'=4,'seq'=4,'fsdp'=2] {'dp','seq','fsdp'}, dimensions={0}, use_global_device_ids=true | all-gather | bytes 16896 | tf_op jit(solution)/shard_map/all_gather | solution.py:158
  239.2 26.0 all-gather.10.cloned.1.call-done
  265.1 82.9 %all-gather.12.cloned.1.call-done = bf16[2,1024,2048]{2,1,0:T(8,128)(2,1)} async-done(((bf16[2,128,2048]{2,1,0:T(8,128)(2,1)}), bf16[2,1024,2048]{2,1,0:T(8,128)(2,1)}) %all-gather.12.cloned.1.call-update) | async-done | bytes 8388624 | tf_op jit(solution)/shard_map/all_gather | solution.py:119
  349.1 107.3 %while.32 = (s32[]{:T(128)}, bf16[2,128,2048]{2,1,0:T(8,128)(2,1)}, bf16[2,128,2048]{2,1,0:T(8,128)(2,1)}, bf16[2,1024,2048]{2,1,0:T(8,128)(2,1)}, f32[16]{0:T(1...) while((s32[]{:T(128)}, bf16[2,128,2048]{2,1,0:T(8,128)(2,1)}, ...), condition=%wide.region_5.6_spmd.clone, body=%wide.region_2.5_spmd.clone.sunk | while | flops 205129984 | bytes 6581963 | solution.py:147
  462.9 160.2 %all-gather.18.cloned.1.call-done = bf16[8192,2048]{1,0:T(8,128)(2,1)} async-done(((bf16[256,2048]{1,0:T(8,128)(2,1)}), bf16[8192,2048]{1,0:T(8,128)(2,1)}) %all-gather.18.cloned.1.call-update) | async-done | bytes 33554448 | tf_op jit(solution)/shard_map/all_gather | solution.py:157
  623.2 19.0 fusion.124
  642.1 176.9 %all-gather.16.cloned.1.call-done = bf16[2048,8192]{1,0:T(8,128)(2,1)} async-done(((bf16[64,8192]{1,0:T(8,128)(2,1)}), bf16[2048,8192]{1,0:T(8,128)(2,1)}) %all-gather.16.cloned.1.call-update) | async-done | bytes 33554448 | tf_op jit(solution)/shard_map/all_gather | solution.py:156
  819.0 25.5 convert_reduce_fusion
  844.5 18.3 multiply_reduce_fusion.1
  883.4 251.5 %while.33 = (s32[]{:T(128)}, bf16[2,128,2048]{2,1,0:T(8,128)(2,1)}, bf16[2,1024,2048]{2,1,0:T(8,128)(2,1)}, bf16[2,1024,2048]{2,1,0:T(8,128)(2,1)}, bf16[2,128,2...) while((s32[]{:T(128)}, bf16[2,128,2048]{2,1,0:T(8,128)(2,1)}, ...), condition=%wide.region_14.15_spmd.clone, body=%wide.region_10.14_spmd.clone.sunk | while | flops 410129152 | bytes 16747235 | solution.py:258
  1137.8 85.1 %reduce-scatter.9.cloned.1.call-done = bf16[2,128,2048]{2,1,0:T(8,128)(2,1)} async-done(((bf16[2,1024,2048]{2,1,0:T(8,128)(2,1)}), bf16[2,128,2048]{2,1,0:T(8,128)(2,1)}) %reduce-scatter.9.cloned.1.call-update) | async-done | bytes 1048592 | tf_op jit(solution)/shard_map/reduce_scatter | solution.py:265
  1222.9 90.3 %reduce-scatter.7.cloned.1.call-done = bf16[2,128,2048]{2,1,0:T(8,128)(2,1)} async-done(((bf16[2,1024,2048]{2,1,0:T(8,128)(2,1)}), bf16[2,128,2048]{2,1,0:T(8,128)(2,1)}) %reduce-scatter.7.cloned.1.call-update) | async-done | bytes 1048592 | tf_op jit(solution)/shard_map/reduce_scatter | solution.py:262
  1313.2 16.9 fusion.107
  1344.0 20.8 fusion.95
  1366.4 25.5 fusion.105
  1393.1 27.4 fusion.106
  1421.3 19.6 fusion.92
  1467.4 179.1 %reduce-scatter.13.cloned.1.call-done = f32[64,2048]{1,0:T(8,128)} async-done(((f32[2048,2048]{1,0:T(8,128)}), f32[64,2048]{1,0:T(8,128)}) %reduce-scatter.13.cloned.1.call-update) | async-done | bytes 524304 | tf_op jit(solution)/shard_map/reduce_scatter | solution.py:281
  1646.5 437.3 %reduce-scatter.11.cloned.1.call-done = f32[64,6144]{1,0:T(8,128)} async-done(((f32[2048,6144]{1,0:T(8,128)}), f32[64,6144]{1,0:T(8,128)}) %reduce-scatter.11.cloned.1.call-update) | async-done | bytes 1572880 | tf_op jit(solution)/shard_map/reduce_scatter | solution.py:280
  2083.9 711.3 %reduce-scatter.15.cloned.1.call-done = f32[64,8192]{1,0:T(8,128)} async-done(((f32[2048,8192]{1,0:T(8,128)}), f32[64,8192]{1,0:T(8,128)}) %reduce-scatter.15.cloned.1.call-update) | async-done | bytes 2097168 | tf_op jit(solution)/shard_map/reduce_scatter | solution.py:195
  2795.2 709.0 %reduce-scatter.17.cloned.1.call-done = f32[256,2048]{1,0:T(8,128)} async-done(((f32[8192,2048]{1,0:T(8,128)}), f32[256,2048]{1,0:T(8,128)}) %reduce-scatter.17.cloned.1.call-update) | async-done | bytes 2097168 | tf_op jit(solution)/shard_map/reduce_scatter | solution.py:196
  (353 shorter events, 464.2 us)
Async XLA Ops:
  7.2 162.7 %all-gather.8.cloned.1.call-start = ((), (), s32[]{:S(2)}) async-start(), calls=%async_computation.6 | async-start | bytes 25952256 | tf_op jit(solution)/shard_map/all_gather | solution.py:77
  7.9 257.2 %all-gather.10.cloned.1.call-start = ((), (), s32[]{:S(2)}) async-start(), calls=%async_computation.7 | async-start | bytes 9437184 | tf_op jit(solution)/shard_map/all_gather | solution.py:118
  58.5 1271.7 %copy-start.17 = (f32[2048]{0:T(1024)}, f32[2048]{0:T(1024)S(1)}, u32[]{:S(2)}) copy-start(f32[2048]{0:T(1024)S(1)} %convert_element_type.136) | copy-start | bytes 24580
  59.9 1270.2 %copy-start.19 = (f32[256]{0:T(256)}, f32[256]{0:T(256)S(1)}, u32[]{:S(2)}) copy-start(f32[256]{0:T(256)S(1)} %get-tuple-element.486) | copy-start | bytes 3076
  61.6 119.9 %copy-start.24 = (f32[2,128]{1,0:T(2,128)}, f32[2,128]{1,0:T(2,128)S(1)}, u32[]{:S(2)}) copy-start(f32[2,128]{1,0:T(2,128)S(1)} %multiply_reduce_fusion.6) | copy-start | bytes 3076
  61.6 119.9 %copy-start.21 = (f32[256]{0:T(256)}, f32[256]{0:T(256)S(1)}, u32[]{:S(2)}) copy-start(f32[256]{0:T(256)S(1)} %bitcast_rsqrt_fusion) | copy-start | bytes 3076
  63.3 118.2 %copy-start.12 = (bf16[256,2048]{1,0:T(8,128)(2,1)}, bf16[256,2048]{1,0:T(8,128)(2,1)S(1)}, u32[]{:S(2)}) copy-start(bf16[256,2048]{1,0:T(8,128)(2,1)S(1)} %add_convert_fusion.1) | copy-start | bytes 3145732
  184.6 163.4 %all-gather.12.cloned.1.call-start = ((), (), s32[]{:S(2)}) async-start(), calls=%async_computation.8 | async-start | bytes 9437184 | tf_op jit(solution)/shard_map/all_gather | solution.py:119
  188.7 267.6 %all-gather.14.cloned.1.call-start = ((), (), s32[]{:S(2)}) async-start(), calls=%async_computation.9 | async-start | bytes 8650752 | tf_op jit(solution)/shard_map/all_gather | solution.py:78
  189.3 433.9 %all-gather.18.cloned.1.call-start = ((), (), s32[]{:S(2)}) async-start(), calls=%async_computation.11 | async-start | bytes 34603008 | tf_op jit(solution)/shard_map/all_gather | solution.py:157
  189.9 629.1 %all-gather.16.cloned.1.call-start = ((), (), s32[]{:S(2)}) async-start(), calls=%async_computation.10 | async-start | bytes 34603008 | tf_op jit(solution)/shard_map/all_gather | solution.py:156
  190.5 1032.5 %reduce-scatter.9.cloned.1.call-start = ((), (), s32[]{:S(2)}) async-start(), calls=%async_computation.13 | async-start | bytes 9437184 | tf_op jit(solution)/shard_map/reduce_scatter | solution.py:265
  349.1 107.3 %copy-start = (bf16[2,128,2048]{2,1,0:T(8,128)(2,1)S(1)}, bf16[2,128,2048]{2,1,0:T(8,128)(2,1)}, u32[]{:S(2)}) copy-start(bf16[2,128,2048]{2,1,0:T(8,128)(2,1)} %param.20) | copy-start | bytes 3145732
  462.6 400.3 %copy-start.2 = (f32[256,2048]{1,0:T(8,128)}, f32[256,2048]{1,0:T(8,128)S(1)}, u32[]{:S(2)}) copy-start(f32[256,2048]{1,0:T(8,128)S(1)} %get-tuple-element.489) | copy-start | bytes 6291460
  1135.0 178.3 %reduce-scatter.7.cloned.1.call-start = ((), (), s32[]{:S(2)}) async-start(), calls=%async_computation.12 | async-start | bytes 9437184 | tf_op jit(solution)/shard_map/reduce_scatter | solution.py:262
  1135.7 320.3 %all-reduce.21.cloned.1.call-start = ((), (), s32[]{:S(2)}) async-start(), calls=%async_computation.18 | async-start | bytes 196608
  1332.5 314.0 %reduce-scatter.13.cloned.1.call-start = ((), (), s32[]{:S(2)}) async-start(), calls=%async_computation.15 | async-start | bytes 17301504 | tf_op jit(solution)/shard_map/reduce_scatter | solution.py:281
  1342.2 741.7 %reduce-scatter.11.cloned.1.call-start = ((), (), s32[]{:S(2)}) async-start(), calls=%async_computation.14 | async-start | bytes 51904512 | tf_op jit(solution)/shard_map/reduce_scatter | solution.py:280
  1364.8 1430.4 %reduce-scatter.15.cloned.1.call-start = ((), (), s32[]{:S(2)}) async-start(), calls=%async_computation.16 | async-start | bytes 69206016 | tf_op jit(solution)/shard_map/reduce_scatter | solution.py:195
  1391.9 2112.2 %reduce-scatter.17.cloned.1.call-start = ((), (), s32[]{:S(2)}) async-start(), calls=%async_computation.17 | async-start | bytes 69206016 | tf_op jit(solution)/shard_map/reduce_scatter | solution.py:196
  1421.2 19.7 copy-start.18
  1421.2 19.7 copy-start.20
  1421.2 19.7 copy-start.23
  1421.3 19.7 copy-start.27
  (21 other events, 153.8 us)
Sparse Core Ops, SparseCore 0:
  11.0 158.8 all-gather.7
  184.7 80.3 all-gather.9
  267.3 80.6 all-gather.11
  350.8 76.0 all-gather.13
  429.7 193.3 all-gather.17
  626.0 192.9 all-gather.15
  1135.1 87.7 reduce-scatter.8
  1225.2 87.9 reduce-scatter.6
  1332.6 123.3 all-reduce.20
  1458.8 187.6 reduce-scatter.12
  1654.7 429.1 reduce-scatter.10
  2086.8 708.3 reduce-scatter.14
  2798.2 705.8 reduce-scatter.16
where the time goes:
time: 3520 us; the launch traced here: 3510 us
  waiting for transfers between devices  2780 us (79%)
  matrix products  523 us (15%)
  blocking collectives  92.2 us (3%)
  local copies, waits for them, and re-layouts  56 us (2%)
  other arithmetic  45.2 us (1%)
    reduce_scatter x1, waiting for transfers between devices, on_device(): lax.psum_scatter(grad_w_up, ('dp', 'seq', 'fsdp'), scatter_dimension=0, t...  711 us
    reduce_scatter x1, waiting for transfers between devices, on_device(): lax.psum_scatter(grad_w_down, ('dp', 'seq', 'fsdp'), scatter_dimension=0,...  709 us
    reduce_scatter x1, waiting for transfers between devices, on_device(): lax.psum_scatter(grad_w_qkv, ('dp', 'seq', 'fsdp'), scatter_dimension=0,...  437 us
    reduce_scatter x1, waiting for transfers between devices, on_device(): lax.psum_scatter(grad_w_out, ('dp', 'seq', 'fsdp'), scatter_dimension=0,...  179 us
    all_gather x1, waiting for transfers between devices, on_device(): lax.all_gather(w_up, ('dp', 'seq', 'fsdp'), axis=0, tiled=True)  177 us
    all_gather x1, waiting for transfers between devices, on_device(): lax.all_gather(w_down, ('dp', 'seq', 'fsdp'), axis=0, tiled=True)  160 us
    all_gather x1, waiting for transfers between devices, on_device(): lax.all_gather(w_qkv, ('dp', 'seq', 'fsdp'), axis=0, tiled=True)  107 us
    reduce_scatter x1, waiting for transfers between devices, on_device(): lax.psum_scatter(grad_keys_all.astype(jnp.bfloat16), ('seq', 'fsdp'), sca...  90.3 us
  transfers between devices with their start and end apart: 13, of which 12 were waited for; matrix products, arithmetic and copies ran while one was open for 8% of the time, Pallas kernels for 0%

commit v1 on v0

v1 whole, which is shorter than its diff:
```python
import jax
import jax.numpy as jnp
from jax import lax
from jax.experimental import pallas as pl
from jax.experimental.pallas import tpu as pltpu
from jax.sharding import PartitionSpec as P

HEAD_DIM = 128
EPSILON = 1e-05
ALL = ("dp", "seq", "fsdp")
LINE = ("seq", "fsdp")
f32 = jnp.float32
bf16 = jnp.bfloat16


def dot(left, right, dims):
    return lax.dot_general(left, right, (dims, ((), ())), preferred_element_type=f32)


def norm_parts(values):
    average = jnp.mean(values, axis=-1, keepdims=True)
    centered = values - average
    variance = jnp.mean(centered * centered, axis=-1, keepdims=True)
    scale = lax.rsqrt(variance + EPSILON)
    return centered * scale, scale


def norm_back(grad, gain, normal, scale):
    scaled = grad * gain
    return scale * (
        scaled
        - jnp.mean(scaled, axis=-1, keepdims=True)
        - normal * jnp.mean(scaled * normal, axis=-1, keepdims=True)
    )


def gelu_both(hidden):
    root = (2.0 / jnp.pi) ** 0.5
    square = hidden * hidden
    tanh = jnp.tanh(root * (hidden + 0.044715 * hidden * square))
    half = 0.5 * (1.0 + tanh)
    slope = half + 0.5 * hidden * (1.0 - tanh * tanh) * root * (1.0 + 3 * 0.044715 * square)
    return hidden * half, slope


def permute(value, axis, mask):
    count = lax.axis_size(axis)
    return lax.ppermute(value, axis, [(i, i ^ mask) for i in range(count)])


def gather_dp(block):
    if lax.axis_size("dp") != 4:
        return lax.all_gather(block, "dp", axis=0, tiled=False)
    half = block.shape[0] // 2
    one = permute(block, "dp", 1)
    two = permute(block, "dp", 2)
    top = permute(two[:half], "dp", 1)
    low = permute(one[half:], "dp", 2)
    return jnp.stack([block, one, two, jnp.concatenate([top, low], axis=0)])


def gather_dp_rows(block):
    return lax.all_gather(block, "dp", axis=0, tiled=True)


def scatter_dp(parts):
    if lax.axis_size("dp") != 4:
        return lax.psum_scatter(parts.astype(bf16), "dp", scatter_dimension=0, tiled=False).astype(f32)
    half = parts.shape[1] // 2
    low = parts[3].astype(bf16)
    from_one = permute(low[:half], "dp", 1).astype(f32)
    from_two = permute(low[half:], "dp", 2).astype(f32)
    two = jnp.concatenate([parts[2, :half] + from_one, parts[2, half:]], axis=0)
    one = jnp.concatenate([parts[1, :half], parts[1, half:] + from_two], axis=0)
    return (
        parts[0]
        + permute(one.astype(bf16), "dp", 1).astype(f32)
        + permute(two.astype(bf16), "dp", 2).astype(f32)
    )


BLOCK = 256
LOG2E = 1.4426950408889634
VMEM_BYTES = 56 * 2**20


def call(body, **options):
    return pl.pallas_call(
        body, compiler_params=pltpu.CompilerParams(vmem_limit_bytes=VMEM_BYTES), **options
    )


def norm_project_body(x_ref, gain_ref, beta_ref, w_ref, bias_ref, normed_ref, out_ref):
    normal, _ = norm_parts(x_ref[...].astype(f32))
    normed = (normal * gain_ref[...] + beta_ref[...]).astype(bf16)
    normed_ref[...] = normed
    out_ref[...] = (dot(normed, w_ref[...], ((1,), (0,))) + bias_ref[...]).astype(bf16)


def norm_project(tokens, gain, beta, weight, bias):
    rows, width = tokens.shape
    out = weight.shape[1]
    tile = min(rows, 256)
    whole = lambda shape: pl.BlockSpec(shape, lambda i: (0, 0))
    part = lambda cols: pl.BlockSpec((tile, cols), lambda i: (i, 0))
    return call(
        norm_project_body,
        grid=(rows // tile,),
        in_specs=[part(width), whole((1, width)), whole((1, width)), whole(weight.shape), whole((1, out))],
        out_specs=[part(width), part(out)],
        out_shape=[jax.ShapeDtypeStruct((rows, width), bf16), jax.ShapeDtypeStruct((rows, out), bf16)],
        cost_estimate=pl.CostEstimate(
            flops=2 * rows * width * out, bytes_accessed=4 * rows * width + 2 * out * (rows + width), transcendentals=0
        ),
    )(tokens, gain, beta, weight, bias)


def tile_scores(query, key, slope, first, ids_col, ids_row, score_scale):
    scores = dot(query, key, ((1,), (1,))) * (score_scale * LOG2E)
    shape = scores.shape
    apart = lax.broadcasted_iota(jnp.int32, shape, 0) + first - lax.broadcasted_iota(jnp.int32, shape, 1)
    scores = scores - slope * jnp.abs(apart).astype(f32)
    return jnp.where(ids_row <= ids_col, scores, -1e30)


def attend_body(score_scale, heads, slope_ref, idc_ref, idr_ref, qkv_ref, ctx_ref, lse_ref):
    blocks, _, span, _ = qkv_ref.shape
    length = blocks * span
    cols = heads * HEAD_DIM
    step = BLOCK // span

    def piece(low, high, at):
        return qkv_ref[low:high, 0, :, at : at + HEAD_DIM].reshape((high - low) * span, HEAD_DIM)

    for head in range(heads):
        at = head * HEAD_DIM
        for t in range(length // BLOCK):
            top = min(blocks, (t + 2) * step)
            rows = slice(t * BLOCK, (t + 1) * BLOCK)
            scores = tile_scores(
                piece(t * step, (t + 1) * step, at),
                piece(0, top, cols + at),
                slope_ref[0, head] * LOG2E,
                t * BLOCK,
                idc_ref[0, rows],
                idr_ref[0, :, : top * span],
                score_scale,
            )
            row_max = jnp.max(scores, axis=-1, keepdims=True)
            exponent = jnp.exp2(scores - row_max)
            total = jnp.sum(exponent, axis=-1, keepdims=True)
            probs = (exponent * (1.0 / total)).astype(bf16)
            context = dot(probs, piece(0, top, 2 * cols + at), ((1,), (0,)))
            ctx_ref[t * step : (t + 1) * step, 0, :, at : at + HEAD_DIM] = context.astype(bf16).reshape(
                step, span, HEAD_DIM
            )
            lse_ref[0, rows, head : head + 1] = row_max + jnp.log2(total)


def attend_back_body(score_scale, heads, slope_ref, idc_ref, idr_ref, qkv_ref, grad_ref, lse_ref, out_ref, gk_ref, gv_ref):
    blocks, _, span, _ = qkv_ref.shape
    length = blocks * span
    cols = heads * HEAD_DIM
    step = BLOCK // span

    def piece(ref, low, high, at):
        return ref[low:high, 0, :, at : at + HEAD_DIM].reshape((high - low) * span, HEAD_DIM)

    def put(low, high, at, value):
        out_ref[low:high, 0, :, at : at + HEAD_DIM] = value.astype(bf16).reshape(high - low, span, HEAD_DIM)

    for head in range(heads):
        at = head * HEAD_DIM
        gk_ref[...] = jnp.zeros_like(gk_ref)
        gv_ref[...] = jnp.zeros_like(gv_ref)
        for t in range(length // BLOCK):
            top = min(blocks, (t + 2) * step)
            rows = slice(t * BLOCK, (t + 1) * BLOCK)
            query = piece(qkv_ref, t * step, (t + 1) * step, at)
            key = piece(qkv_ref, 0, top, cols + at)
            grad = piece(grad_ref, t * step, (t + 1) * step, at)
            scores = tile_scores(
                query,
                key,
                slope_ref[0, head] * LOG2E,
                t * BLOCK,
                idc_ref[0, rows],
                idr_ref[0, :, : top * span],
                score_scale,
            )
            probs = jnp.exp2(scores - lse_ref[0, rows, head : head + 1])
            grad_probs = dot(grad, piece(qkv_ref, 0, top, 2 * cols + at), ((1,), (1,)))
            total = jnp.sum(probs * grad_probs, axis=-1, keepdims=True)
            grad_scores = (probs * (grad_probs - total) * score_scale).astype(bf16)
            put(t * step, (t + 1) * step, at, dot(grad_scores, key, ((1,), (0,))))
            gk_ref[: top * span] += dot(grad_scores, query, ((0,), (0,)))
            gv_ref[: top * span] += dot(probs.astype(bf16), grad, ((0,), (0,)))
        put(0, blocks, cols + at, gk_ref[...])
        put(0, blocks, 2 * cols + at, gv_ref[...])


def attention_specs(blocks, span, cols, length, heads):
    split = lambda width: pl.BlockSpec((blocks, 1, span, width), lambda s: (0, s, 0, 0))
    return (
        pl.BlockSpec(memory_space=pltpu.SMEM),
        pl.BlockSpec((1, length, 1), lambda s: (s, 0, 0)),
        pl.BlockSpec((1, 1, length), lambda s: (s, 0, 0)),
        split(3 * cols),
        split(cols),
        pl.BlockSpec((1, length, heads), lambda s: (s, 0, 0)),
    )


def attend(slopes, ids, qkv, score_scale):
    blocks, seqs, span, width = qkv.shape
    length, cols = blocks * span, width // 3
    heads = cols // HEAD_DIM
    smem, idc, idr, three, one, lse = attention_specs(blocks, span, cols, length, heads)
    return call(
        lambda *refs: attend_body(score_scale, heads, *refs),
        grid=(seqs,),
        in_specs=[smem, idc, idr, three],
        out_specs=[one, lse],
        out_shape=[
            jax.ShapeDtypeStruct((blocks, seqs, span, cols), bf16),
            jax.ShapeDtypeStruct((seqs, length, heads), f32),
        ],
        cost_estimate=pl.CostEstimate(
            flops=4 * seqs * cols * length * length,
            bytes_accessed=8 * seqs * length * cols,
            transcendentals=seqs * heads * length * length,
        ),
    )(slopes, ids[:, :, None], ids[:, None, :], qkv)


def attend_back(slopes, ids, qkv, grad, stats, score_scale):
    blocks, seqs, span, width = qkv.shape
    length, cols = blocks * span, width // 3
    heads = cols // HEAD_DIM
    smem, idc, idr, three, one, lse = attention_specs(blocks, span, cols, length, heads)
    return call(
        lambda *refs: attend_back_body(score_scale, heads, *refs),
        grid=(seqs,),
        in_specs=[smem, idc, idr, three, one, lse],
        out_specs=three,
        out_shape=jax.ShapeDtypeStruct(qkv.shape, bf16),
        scratch_shapes=[pltpu.VMEM((length, HEAD_DIM), f32)] * 2,
        cost_estimate=pl.CostEstimate(
            flops=10 * seqs * cols * length * length,
            bytes_accessed=14 * seqs * length * cols,
            transcendentals=seqs * heads * length * length,
        ),
    )(slopes, ids[:, :, None], ids[:, None, :], qkv, grad, stats)


def norm_one_back_body(g_ref, w_ref, x_ref, out_ref, gain_ref, beta_ref):
    grad = dot(g_ref[...], w_ref[...], ((1,), (1,)))
    normal, _ = norm_parts(x_ref[...].astype(f32))
    out_ref[...] = grad.astype(bf16)

    @pl.when(pl.program_id(0) == 0)
    def _():
        gain_ref[...] = jnp.zeros_like(gain_ref)
        beta_ref[...] = jnp.zeros_like(beta_ref)

    gain_ref[...] += jnp.sum(grad * normal, axis=0, keepdims=True)
    beta_ref[...] += jnp.sum(grad, axis=0, keepdims=True)


def norm_one_back(grad_qkv, weight, tokens):
    rows, width = tokens.shape
    inner = weight.shape[1]
    tile = min(rows, 256)
    whole = lambda shape: pl.BlockSpec(shape, lambda i: (0, 0))
    part = lambda cols: pl.BlockSpec((tile, cols), lambda i: (i, 0))
    return call(
        norm_one_back_body,
        grid=(rows // tile,),
        in_specs=[part(inner), whole(weight.shape), part(width)],
        out_specs=[part(width), whole((1, width)), whole((1, width))],
        out_shape=[
            jax.ShapeDtypeStruct((rows, width), bf16),
            jax.ShapeDtypeStruct((1, width), f32),
            jax.ShapeDtypeStruct((1, width), f32),
        ],
        cost_estimate=pl.CostEstimate(
            flops=2 * rows * width * inner, bytes_accessed=4 * rows * width + 2 * inner * (rows + width), transcendentals=0
        ),
    )(grad_qkv, weight, tokens)


def on_device(
    inputs,
    block_ids,
    gain_one,
    beta_one,
    w_qkv,
    bias_query,
    bias_value,
    w_out,
    bias_out,
    gain_two,
    beta_two,
    w_up,
    bias_up,
    w_down,
    bias_down,
    cotangent,
):
    seqs, span, width = inputs.shape
    rows = seqs * span
    n_dp = lax.axis_size("dp")
    n_line = lax.axis_size(LINE)
    length = span * n_line
    share = w_qkv.shape[0]
    feed = w_up.shape[1]
    feed_own = feed // n_dp
    cols = width // n_line
    heads = cols // HEAD_DIM
    score_scale = HEAD_DIM ** (-0.5)
    line_at = lax.axis_index(LINE)

    small = jnp.stack(
        [gain_one, beta_one, bias_query, bias_value, bias_out, gain_two, beta_two, bias_down]
    ).reshape(-1)
    small = jnp.concatenate([small, bias_up])
    small_all = lax.all_gather(small, ALL, axis=0, tiled=False).astype(f32)
    vectors = small_all[:, : 8 * share].reshape(-1, 8, share).transpose(1, 0, 2).reshape(8, width)
    gain1, beta1, biasq, biasv, biaso, gain2, beta2, biasd = [vectors[i][None] for i in range(8)]
    up_bias_all = small_all[:, 8 * share :].reshape(n_dp, 1, feed_own)
    up_bias = lax.dynamic_index_in_dim(up_bias_all, lax.axis_index("dp"), 0, keepdims=False)
    biasq_own = lax.dynamic_slice_in_dim(biasq, line_at * cols, cols, 1)
    biasv_own = lax.dynamic_slice_in_dim(biasv, line_at * cols, cols, 1)

    qkv_send = w_qkv.reshape(share, 3, n_line, cols).transpose(2, 0, 1, 3).reshape(n_line, share, 3 * cols)
    qkv_got = lax.all_to_all(qkv_send, LINE, split_axis=0, concat_axis=0, tiled=True)
    qkv_own = gather_dp_rows(qkv_got.reshape(n_line * share, 3 * cols))
    tokens_line = lax.all_gather(inputs, LINE, axis=0, tiled=False)
    ids_line = lax.all_gather(block_ids.astype(bf16), LINE, axis=0, tiled=False)

    out_full = lax.all_gather(w_out, ALL, axis=0, tiled=True)
    up_send = w_up.reshape(share, n_dp, feed_own).transpose(1, 0, 2)
    up_got = lax.all_to_all(up_send, "dp", split_axis=0, concat_axis=0, tiled=True)
    up_own = (
        lax.all_gather(up_got, LINE, axis=0, tiled=False)
        .transpose(1, 0, 2, 3)
        .reshape(width, feed_own)
    )
    down_own = lax.all_gather(w_down, LINE, axis=0, tiled=True)

    tokens_line = tokens_line.reshape(n_line * rows, width)
    bias_row = jnp.concatenate([biasq_own, jnp.zeros_like(biasq_own), biasv_own], axis=1)
    normed_one, qkv = norm_project(tokens_line, gain1, beta1, qkv_own, bias_row)
    qkv = qkv.reshape(n_line, seqs, span, 3 * cols)
    ids = ids_line.astype(f32).transpose(1, 0, 2).reshape(seqs, length)
    numbers = (line_at * heads + jnp.arange(heads)).astype(f32)
    slopes = jnp.exp2(-8.0 * (numbers + 1.0) / (n_line * heads))[None]
    context_own, stats = attend(slopes, ids, qkv, score_scale)
    context_own = context_own.reshape(n_line, rows, cols)
    context = (
        lax.all_to_all(context_own, LINE, split_axis=0, concat_axis=0, tiled=True)
        .transpose(1, 0, 2)
        .reshape(rows, width)
    )

    tokens = inputs.astype(f32).reshape(rows, width)
    residual = tokens + dot(context, out_full, ((1,), (0,))) + biaso
    normal_two, scale_two = norm_parts(residual)
    normed_two = (normal_two * gain2 + beta2).astype(bf16)

    grad_out = cotangent.reshape(rows, width)
    grad_out_dp = gather_dp(grad_out).reshape(n_dp * rows, width)
    normed_two_dp = gather_dp(normed_two).reshape(n_dp * rows, width)
    hidden = dot(normed_two_dp, up_own, ((1,), (0,))) + up_bias
    activated_f, gelu_slope = gelu_both(hidden)
    activated = activated_f.astype(bf16)
    grad_hidden_f = dot(grad_out_dp, down_own, ((1,), (1,))) * gelu_slope
    grad_hidden = grad_hidden_f.astype(bf16)
    grad_normed_two = scatter_dp(dot(grad_hidden, up_own, ((1,), (1,))).reshape(n_dp, rows, width))
    feed_out = scatter_dp(dot(activated, down_own, ((1,), (0,))).reshape(n_dp, rows, width))
    outputs = (residual + feed_out + biasd).astype(bf16).reshape(seqs, span, width)

    grad_down = dot(activated, grad_out_dp, ((0,), (0,))).astype(bf16)
    grad_w_down = lax.psum_scatter(grad_down, LINE, scatter_dimension=0, tiled=True).astype(f32)
    grad_up = dot(normed_two_dp, grad_hidden, ((0,), (0,))).astype(bf16)
    grad_up = grad_up.reshape(n_dp, n_line, share, feed_own).transpose(1, 0, 2, 3).reshape(width, feed_own)
    grad_up = lax.psum_scatter(grad_up, LINE, scatter_dimension=0, tiled=True).reshape(n_dp, share, feed_own)
    grad_w_up = (
        lax.all_to_all(grad_up, "dp", split_axis=0, concat_axis=0, tiled=True)
        .transpose(1, 0, 2)
        .reshape(share, feed)
        .astype(f32)
    )
    bias_up_part = jnp.sum(grad_hidden.astype(f32), axis=0)

    grad_out_f = grad_out.astype(f32)
    grad_residual = grad_out_f + norm_back(grad_normed_two, gain2, normal_two, scale_two)
    gain2_part = jnp.sum(grad_normed_two * normal_two, axis=0)
    beta2_part = jnp.sum(grad_normed_two, axis=0)
    biasd_part = jnp.sum(grad_out_f, axis=0)
    biaso_part = jnp.sum(grad_residual, axis=0)

    grad_branch = grad_residual.astype(bf16)
    grad_context = dot(grad_branch, out_full, ((1,), (1,))).astype(bf16)
    grad_context = lax.all_to_all(
        grad_context.reshape(rows, n_line, cols).transpose(1, 0, 2), LINE, split_axis=0, concat_axis=0, tiled=True
    ).reshape(n_line, seqs, span, cols)
    grad_out_w = dot(context, grad_branch, ((0,), (0,))).astype(bf16)
    grad_w_out = lax.psum_scatter(grad_out_w, ALL, scatter_dimension=0, tiled=True).astype(f32)

    grad_qkv = attend_back(slopes, ids, qkv, grad_context, stats, score_scale).reshape(n_line * rows, 3 * cols)

    grad_normed_part, gain1_part, beta1_part = norm_one_back(grad_qkv, qkv_own, tokens_line)
    gain1_part, beta1_part = gain1_part[0], beta1_part[0]
    grad_normed_one = lax.psum_scatter(
        grad_normed_part, LINE, scatter_dimension=0, tiled=True
    ).astype(f32)
    normal_one, scale_one = norm_parts(tokens)
    grad_inputs = grad_residual + norm_back(grad_normed_one, gain1, normal_one, scale_one)
    bias_qkv_part = jnp.sum(grad_qkv.astype(f32), axis=0)

    grad_qkv_w = dot(normed_one, grad_qkv, ((0,), (0,))).astype(bf16)
    grad_qkv_w = lax.psum_scatter(grad_qkv_w, "dp", scatter_dimension=0, tiled=True)
    grad_w_qkv = (
        lax.all_to_all(grad_qkv_w.reshape(n_line, share, 3 * cols), LINE, split_axis=0, concat_axis=0, tiled=True)
        .reshape(n_line, share, 3, cols)
        .transpose(1, 2, 0, 3)
        .reshape(share, 3 * width)
        .astype(f32)
    )

    def spread(own, count, at):
        return lax.dynamic_update_slice_in_dim(jnp.zeros((count,) + own.shape, f32), own[None], at, 0)

    biasq_part = spread(bias_qkv_part[:cols], n_line, line_at).reshape(-1)
    biasv_part = spread(bias_qkv_part[2 * cols :], n_line, line_at).reshape(-1)
    bias_up_whole = spread(bias_up_part, n_dp, lax.axis_index("dp")).reshape(-1)
    parts = jnp.stack(
        [biasq_part, biasv_part, biaso_part, gain1_part, beta1_part, biasd_part, gain2_part, beta2_part]
    )
    n_all = n_dp * n_line
    parts = parts.reshape(8, n_all, share).transpose(1, 0, 2).reshape(n_all, 8 * share)
    parts = jnp.concatenate([parts, bias_up_whole.reshape(n_all, -1)], axis=1)
    parts = lax.all_to_all(parts, ALL, split_axis=0, concat_axis=0, tiled=True)
    own = jnp.sum(parts, axis=0)
    vec = own[: 8 * share].reshape(8, share)

    return (
        outputs,
        grad_inputs.reshape(seqs, span, width),
        grad_w_qkv,
        vec[0],
        vec[1],
        grad_w_out,
        vec[2],
        vec[3],
        vec[4],
        grad_w_up,
        own[8 * share :],
        grad_w_down,
        vec[5],
        vec[6],
        vec[7],
    )


def solution(mesh):
    tokens, ids, matrix, vector = P("dp", LINE, None), P("dp", LINE), P(ALL, None), P(ALL)
    placed = (
        tokens,
        ids,
        vector,
        vector,
        matrix,
        vector,
        vector,
        matrix,
        vector,
        vector,
        vector,
        matrix,
        vector,
        matrix,
        vector,
        tokens,
    )
    given = (
        tokens,
        tokens,
        matrix,
        vector,
        vector,
        matrix,
        vector,
        vector,
        vector,
        matrix,
        vector,
        matrix,
        vector,
        vector,
        vector,
    )
    return jax.shard_map(on_device, mesh=mesh, in_specs=placed, out_specs=given, check_vma=False)
```

time: 3520 us -> 1130 us (0.32)
  waiting for transfers between devices: 2780 us -> 645 us
  matrix products: 523 us -> 115 us
  Pallas kernels: 0 us -> 63.5 us
  blocking collectives: 92.2 us -> 142 us
    reduce_scatter x6 -> x5, waiting for transfers between devices: 2210 us -> 343 us  [the longest x1 147 us: on_device(): lax.psum_scatter(grad_out_w, ALL, scatter_dimension=0, tiled=True)]
    all_gather x6 -> x5, waiting for transfers between devices: 552 us -> 188 us  [the longest x1 66.8 us: on_device(): lax.all_gather(up_got, LINE, axis=0, tiled=False).transpose(1, 0, 2, 3)]
    dot_general x108 -> x10, matrix products: 454 us -> 115 us  [dot(): lax.dot_general(left, right, (dims, ((), ())), preferred_element_type=f32)]
    all_to_all x0 -> x4, blocking collectives: none -> 94.2 us  [the longest x1 29.9 us: on_device(): lax.all_to_all(grad_context.reshape(rows, n_line, cols).transpose(1, 0, 2...]
    ppermute x0 -> x16, waiting for transfers between devices: none -> 79.3 us  [permute(): return lax.ppermute(value, axis, [(i, i ^ mask) for i in range(count)])]
    sub x32 -> x0, matrix products: 68.5 us -> none  [softmax_rows(): exponent = jnp.exp(scores - row_max)]
    pallas_call x0 -> x4, Pallas kernels: none -> 63.5 us  [the longest x1 17.8 us: attend_back(): call(lambda *refs: attend_back_body(score_scale, heads, *refs), grid=(seq...]
    unnamed x1 -> x0, blocking collectives: 43.7 us -> none
  transfers between devices with their start and end apart: 13 -> 29, of which waited for: 12 -> 18; matrix products, arithmetic and copies ran while one was open for 8% -> 14% of each run, Pallas kernels for 0% -> 4%
where the time goes in v1:
time: 1130 us; the launch traced here: 1120 us
  waiting for transfers between devices  645 us (57%)
  blocking collectives  142 us (13%)
  matrix products  115 us (10%)
  Pallas kernels  63.5 us (6%)
  local copies, waits for them, and re-layouts  58.5 us (5%)
  other arithmetic  45.1 us (4%)
  starting transfers between devices  32.8 us (3%)
  between operations  15.1 us (1%)
    reduce_scatter x1, waiting for transfers between devices, on_device(): lax.psum_scatter(grad_out_w, ALL, scatter_dimension=0, tiled=True)  147 us
    dot_general x10, matrix products, dot(): lax.dot_general(left, right, (dims, ((), ())), preferred_element_type=f32)  115 us
    reduce_scatter x1, waiting for transfers between devices, on_device(): lax.psum_scatter(grad_normed_part, LINE, scatter_dimension=0, tiled=True)  87.8 us
    reduce_scatter x1, waiting for transfers between devices, on_device(): lax.psum_scatter(grad_down, LINE, scatter_dimension=0, tiled=True)  79.9 us
    ppermute x16, waiting for transfers between devices, permute(): return lax.ppermute(value, axis, [(i, i ^ mask) for i in range(count)])  79.3 us
    all_gather x1, waiting for transfers between devices, on_device(): lax.all_gather(up_got, LINE, axis=0, tiled=False).transpose(1, 0, 2, 3)  66.8 us
    all_gather x1, waiting for transfers between devices, on_device(): tokens_line = lax.all_gather(inputs, LINE, axis=0, tiled=False)  52.3 us
    all_gather x1, waiting for transfers between devices, on_device(): down_own = lax.all_gather(w_down, LINE, axis=0, tiled=True)  40.7 us
  transfers between devices with their start and end apart: 29, of which 18 were waited for; matrix products, arithmetic and copies ran while one was open for 14% of the time, Pallas kernels for 4%

profile of v1, /device:TPU:0, one launch (start us, length us, event | category | flops | bytes accessed | tf_op | source)
XLA Modules:
  0.0 1117.6 jit_solution(6499795691010810352)
XLA Ops:
  10.0 27.2 %all_to_all.39 = bf16[8,64,768]{2,1,0:T(8,128)(2,1)} all-to-all(bf16[8,64,768]{2,1,0:T(8,128)(2,1)S(1)} %reshape.264), channel_id=1, replica_groups=mesh['dp'=4,'seq'=4,'fsdp'=2] {'seq','fsdp'}, dimensions={0} | all-to-all | bytes 1572864 | tf_op jit(solution)/shard_map/all_to_all | solution.py:336
  40.3 25.8 %all_to_all.40 = bf16[4,64,2048]{2,1,0:T(8,128)(2,1)} all-to-all(bf16[4,64,2048]{2,1,0:T(8,128)(2,1)S(1)} %copy.74), channel_id=1, replica_groups=mesh['dp'=4,'seq'=4,'fsdp'=2] {'dp'}, dimensions={0} | all-to-all | bytes 2097152 | tf_op jit(solution)/shard_map/all_to_all | solution.py:343
  66.9 39.3 %all-gather.5 = bf16[32,1,768]{2,1,0:T(2,128)(2,1)S(1)} all-gather(bf16[1,1,768]{2,1,0:T(2,128)(2,1)S(1)} %reshape.299), channel_id=4, replica_groups=mesh['dp'=4,'seq'=4,'fsdp'=2] {'dp','seq','fsdp'}, dimensions={0}, use_global_device_ids=true | all-gather | bytes 50688 | tf_op jit(solution)/shard_map/all_gather | solution.py:327
  120.5 52.3 %all-gather.18.cloned.1.call-done = bf16[16,128,2048]{2,1,0:T(8,128)(2,1)} async-done(((bf16[2,128,2048]{2,1,0:T(8,128)(2,1)}), bf16[16,128,2048]{2,1,0:T(8,128)(2,1)}) %all-gather.18.cloned.1.call-update) | async-done | bytes 8388624 | tf_op jit(solution)/shard_map/all_gather | solution.py:338
  172.8 15.7 %shard_map.271 = (bf16[2048,2048]{1,0:T(8,128)(2,1)}, bf16[2048,768]{1,0:T(8,128)(2,1)}) custom-call(bf16[2048,2048]{1,0:T(8,128)(2,1)} %bitcast.217, f32[1,2048]{1,0:T(1,128)} %slice.168.gain_ref, f32[1,2048]{1,0:T(1,128)} %slice.170.beta_ref, bf16[2048,768]{1,0:T(8,128)(2,1)} %all-gather.12.cloned.1.call-done.w_ref, f32[1,768]{1,0:T(1,128)} %fusion.18.bias_ref), custom_call_target="tpu_custom_call" | custom-call | flops 6442450944 | bytes 23068672 | tf_op jit(solution)/shard_map/pallas_call | solution.py:106
  188.5 13.2 %shard_map.272 = (bf16[8,2,128,256]{3,2,1,0:T(8,128)(2,1)}, f32[2,1024,2]{2,1,0:T(8,128)}) custom-call(f32[1,2]{1,0:T(1,128)} %multiply_exponential_fusion.refs_0_, f32[2,1024,1]{2,1,0:T(8,128)} %copy.72.refs_1_, f32[2,1,1024]{2,1,0:T(1,128)} %bitcast.201, bf16[8,2,128,768]{3,2,1,0:T(8,128)(2,1)} %bitcast.219), custom_call_target="tpu_custom_call" | custom-call | flops 2147483648 | bytes 4194304 | tf_op jit(solution)/shard_map/pallas_call | solution.py:219
  211.1 25.5 %collective-permute-done.8 = bf16[256,2048]{1,0:T(8,128)(2,1)} collective-permute-done((bf16[256,2048]{1,0:T(8,128)(2,1)S(1)}, bf16[256,2048]{1,0:T(8,128)(2,1)}, u32[]{:S(2)}, u32[]{:S(2)}) %collective-permute-start.8) | collective-permute-done | bytes 1048608 | tf_op jit(solution)/shard_map/ppermute | solution.py:48
  244.1 27.8 %all-gather.14.cloned.1.call-done = bf16[2048,2048]{1,0:T(8,128)(2,1)} async-done(((bf16[64,2048]{1,0:T(8,128)(2,1)}), bf16[2048,2048]{1,0:T(8,128)(2,1)}) %all-gather.14.cloned.1.call-update) | async-done | bytes 8388624 | tf_op jit(solution)/shard_map/all_gather | solution.py:341
  287.0 66.8 %all-gather.20.cloned.1.call-done = bf16[32,64,2048]{2,1,0:T(8,128)(2,1)} async-done(((bf16[4,64,2048]{2,1,0:T(8,128)(2,1)}), bf16[32,64,2048]{2,1,0:T(8,128)(2,1)}) %all-gather.20.cloned.1.call-update) | async-done | bytes 8388624 | tf_op jit(solution)/shard_map/all_gather | solution.py:345
  395.2 40.7 %all-gather.16.cloned.1.call-done = bf16[2048,2048]{1,0:T(8,128)(2,1)} async-done(((bf16[256,2048]{1,0:T(8,128)(2,1)}), bf16[2048,2048]{1,0:T(8,128)(2,1)}) %all-gather.16.cloned.1.call-update) | async-done | bytes 8388624 | tf_op jit(solution)/shard_map/all_gather | solution.py:349
  435.8 18.5 %convert_reduce_fusion = (f32[2048]{0:T(1024)}, bf16[1024,2048]{1,0:T(8,128)(2,1)S(1)}) fusion(f32[1024,2048]{1,0:T(8,128)} %fusion.30, f32[2048]{0:T(1024)S(1)} %bitcast.203, bf16[1024,2048]{1,0:T(8,128)(2,1)} %bitcast.174, bf16[2048,2048]{1,0:T(8,128)(2,1)} %all-gather.16.cloned.1.call-done), kind=kOutput, calls=%fused_computation | convolution fusion | flops 8633972736 | bytes 25182208 | tf_op jit(solution)/shard_map/dot_general | solution.py:17
  472.4 16.9 %fusion.29 = (bf16[1024,2048]{1,0:T(8,128)(2,1)}, f32[1024,2048]{1,0:T(8,128)S(1)}) fusion(bf16[2048,2048]{1,0:T(8,128)(2,1)} %all-gather.16.cloned.1.call-done, f32[1024,2048]{1,0:T(8,128)} %fusion.30, f32[2048]{0:T(1024)S(1)} %bitcast.204), kind=kOutput, calls=%fused_computation.103 | convolution fusion | flops 8613003264 | bytes 29368320 | tf_op jit(solution)/shard_map/dot_general | solution.py:17
  515.6 17.5 %collective-permute-done.15 = bf16[256,2048]{1,0:T(8,128)(2,1)} collective-permute-done((bf16[256,2048]{1,0:T(8,128)(2,1)}, bf16[256,2048]{1,0:T(8,128)(2,1)}, u32[]{:S(2)}, u32[]{:S(2)}) %collective-permute-start.15) | collective-permute-done | bytes 1048608 | tf_op jit(solution)/shard_map/ppermute | solution.py:48
  537.3 17.0 %collective-permute-done.7 = bf16[256,2048]{1,0:T(8,128)(2,1)} collective-permute-done((bf16[256,2048]{1,0:T(8,128)(2,1)}, bf16[256,2048]{1,0:T(8,128)(2,1)}, u32[]{:S(2)}, u32[]{:S(2)}) %collective-permute-start.7) | collective-permute-done | bytes 1048608 | tf_op jit(solution)/shard_map/ppermute | solution.py:48
  561.7 29.9 %all_to_all.41 = bf16[8,256,256]{2,1,0:T(8,128)(2,1)} all-to-all(bf16[8,256,256]{2,1,0:T(8,128)(2,1)S(1)} %bitcast.178), channel_id=1, replica_groups=mesh['dp'=4,'seq'=4,'fsdp'=2] {'seq','fsdp'}, dimensions={0} | all-to-all | bytes 2097152 | tf_op jit(solution)/shard_map/all_to_all | solution.py:405
  591.6 17.8 %shard_map.273 = bf16[8,2,128,768]{3,2,1,0:T(8,128)(2,1)} custom-call(f32[1,2]{1,0:T(1,128)} %multiply_exponential_fusion.refs_0_, f32[2,1024,1]{2,1,0:T(8,128)} %copy.72.refs_1_, f32[2,1,1024]{2,1,0:T(1,128)} %bitcast.202, bf16[8,2,128,768]{3,2,1,0:T(8,128)(2,1)} %bitcast.220, bf16[8,2,128,256]{3,2,1,0:T(8,128)(2,1)} %bitcast.189, ...), custom_call_target="tpu_custom_call" | custom-call | flops 5368709120 | bytes 7340032 | tf_op jit(solution)/shard_map/pallas_call | solution.py:241
  620.9 14.4 %convolution_convert_fusion.1 = bf16[2048,2048]{1,0:T(8,128)(2,1)} fusion(bf16[1024,2048]{1,0:T(8,128)(2,1)} %bitcast.177, bf16[1024,2048]{1,0:T(8,128)(2,1)} %copy-done.26), kind=kOutput, calls=%fused_computation.7 | convolution fusion | flops 8594128896 | bytes 16777216 | tf_op jit(solution)/shard_map/dot_general | solution.py:17
  643.8 16.0 %convolution_convert_fusion = bf16[2048,2048]{1,0:T(8,128)(2,1)} fusion(bf16[1024,2048]{1,0:T(8,128)(2,1)} %bitcast.175, f32[1024,2048]{1,0:T(8,128)} %fusion.30, f32[2048]{0:T(1024)S(1)} %bitcast.205), kind=kOutput, calls=%fused_computation.6 | convolution fusion | flops 8615100416 | bytes 20979712 | tf_op jit(solution)/shard_map/dot_general | solution.py:17
  667.4 16.9 %shard_map.274 = (bf16[2048,2048]{1,0:T(8,128)(2,1)}, f32[1,2048]{1,0:T(1,128)}, f32[1,2048]{1,0:T(1,128)}) custom-call(bf16[2048,768]{1,0:T(8,128)(2,1)} %bitcast.182, bf16[2048,768]{1,0:T(8,128)(2,1)} %all-gather.12.cloned.1.call-done.w_ref, bf16[2048,2048]{1,0:T(8,128)(2,1)} %bitcast.218), custom_call_target="tpu_custom_call" | custom-call | flops 6442450944 | bytes 23068672 | tf_op jit(solution)/shard_map/pallas_call | solution.py:276
  707.4 33.7 %all-to-all-done.4 = bf16[8,64,768]{2,1,0:T(8,128)(2,1)} async-done(((bf16[8,64,768]{2,1,0:T(8,128)(2,1)}), bf16[8,64,768]{2,1,0:T(8,128)(2,1)}, u32[]{:S(2)}, u32[]{:S(2)}) %all-to-all-start.4) | async-done | bytes 786464 | tf_op jit(solution)/shard_map/all_to_all | solution.py:425
  741.1 27.9 %reduce-scatter.12.cloned.1.call-done = bf16[256,2048]{1,0:T(8,128)(2,1)} async-done(((bf16[2048,2048]{1,0:T(8,128)(2,1)}), bf16[256,2048]{1,0:T(8,128)(2,1)}) %reduce-scatter.12.cloned.1.call-update) | async-done | bytes 1048592 | tf_op jit(solution)/shard_map/reduce_scatter | solution.py:387
  783.2 79.9 %reduce-scatter.14.cloned.1.call-done = bf16[256,2048]{1,0:T(8,128)(2,1)} async-done(((bf16[2048,2048]{1,0:T(8,128)(2,1)}), bf16[256,2048]{1,0:T(8,128)(2,1)}) %reduce-scatter.14.cloned.1.call-update) | async-done | bytes 1048592 | tf_op jit(solution)/shard_map/reduce_scatter | solution.py:384
  868.8 146.9 %reduce-scatter.10.cloned.1.call-done = bf16[64,2048]{1,0:T(8,128)(2,1)} async-done(((bf16[2048,2048]{1,0:T(8,128)(2,1)}), bf16[64,2048]{1,0:T(8,128)(2,1)}) %reduce-scatter.10.cloned.1.call-update) | async-done | bytes 262160 | tf_op jit(solution)/shard_map/reduce_scatter | solution.py:409
  1017.5 87.8 %reduce-scatter.6.cloned.1.call-done = bf16[256,2048]{1,0:T(8,128)(2,1)} async-done(((bf16[2048,2048]{1,0:T(8,128)(2,1)}), bf16[256,2048]{1,0:T(8,128)(2,1)}) %reduce-scatter.6.cloned.1.call-update) | async-done | bytes 1048592 | tf_op jit(solution)/shard_map/reduce_scatter | solution.py:415
  (238 shorter events, 227.2 us)
Async XLA Ops:
  7.2 113.3 %all-gather.12.cloned.1.call-start = ((), (), s32[]{:S(2)}) async-start(), calls=%async_computation.12 | async-start | bytes 3932160 | tf_op jit(solution)/shard_map/all_gather | solution.py:63
  37.2 135.6 %all-gather.18.cloned.1.call-start = ((), (), s32[]{:S(2)}) async-start(), calls=%async_computation.20 | async-start | bytes 9437184 | tf_op jit(solution)/shard_map/all_gather | solution.py:338
  38.0 234.0 %all-gather.14.cloned.1.call-start = ((), (), s32[]{:S(2)}) async-start(), calls=%async_computation.13 | async-start | bytes 8650752 | tf_op jit(solution)/shard_map/all_gather | solution.py:341
  38.8 314.9 %all-gather.20.cloned.1.call-start = ((), (), s32[]{:S(2)}) async-start(), calls=%async_computation.21 | async-start | bytes 9437184 | tf_op jit(solution)/shard_map/all_gather | solution.py:345
  66.1 369.7 %all-gather.16.cloned.1.call-start = ((), (), s32[]{:S(2)}) async-start(), calls=%async_computation.14 | async-start | bytes 9437184 | tf_op jit(solution)/shard_map/all_gather | solution.py:349
  204.1 67.9 %all-to-all-start.1 = ((bf16[8,256,256]{1,2,0:T(8,128)(2,1)}), bf16[8,256,256]{1,2,0:T(8,128)(2,1)S(1)}, u32[]{:S(2)}, u32[]{:S(2)}) async-start(bf16[8,256,256]{1,2,0:T(8,128)(2,1)} %copy.73), calls=%async_computation.1 | async-start | bytes 2097152 | tf_op jit(solution)/shard_map/all_to_all | solution.py:361
  207.6 495.3 %reduce-scatter.8.cloned.1.call-start = ((), (), s32[]{:S(2)}) async-start(), calls=%async_computation.16 | async-start | bytes 3932160 | tf_op jit(solution)/shard_map/reduce_scatter | solution.py:423
  207.9 28.7 %collective-permute-start.8 = (bf16[256,2048]{1,0:T(8,128)(2,1)S(1)}, bf16[256,2048]{1,0:T(8,128)(2,1)}, u32[]{:S(2)}, u32[]{:S(2)}) collective-permute-start(bf16[256,2048]{1,0:T(8,128)(2,1)S(1)} %bitcast.162), channel_id=1, source_target_pairs={{0,8},{8,0},{16,24},{24,16},{1,9},{9,1},{17,25},{25,17},{2,10},{10... | collective-permute-start | bytes 3145736 | tf_op jit(solution)/shard_map/ppermute | solution.py:48
  209.5 30.3 %collective-permute-start.9 = (bf16[256,2048]{1,0:T(8,128)(2,1)S(1)}, bf16[256,2048]{1,0:T(8,128)(2,1)}, u32[]{:S(2)}, u32[]{:S(2)}) collective-permute-start(bf16[256,2048]{1,0:T(8,128)(2,1)S(1)} %bitcast.163), channel_id=1, source_target_pairs={{0,16},{8,24},{16,0},{24,8},{1,17},{9,25},{17,1},{25,9},{2,18},{10... | collective-permute-start | bytes 3145736 | tf_op jit(solution)/shard_map/ppermute | solution.py:48
  238.5 43.7 %collective-permute-start.11 = (bf16[128,2048]{1,0:T(8,128)(2,1)}, bf16[128,2048]{1,0:T(8,128)(2,1)}, u32[]{:S(2)}, u32[]{:S(2)}) collective-permute-start(bf16[128,2048]{1,0:T(8,128)(2,1)} %slice.229), channel_id=1, source_target_pairs={{0,16},{8,24},{16,0},{24,8},{1,17},{9,25},{17,1},{25,9},{2,18},{10... | collective-permute-start | bytes 1572872 | tf_op jit(solution)/shard_map/ppermute | solution.py:48
  241.7 40.5 %collective-permute-start.10 = (bf16[128,2048]{1,0:T(8,128)(2,1)}, bf16[128,2048]{1,0:T(8,128)(2,1)}, u32[]{:S(2)}, u32[]{:S(2)}) collective-permute-start(bf16[128,2048]{1,0:T(8,128)(2,1)} %slice.228), channel_id=1, source_target_pairs={{0,8},{8,0},{16,24},{24,16},{1,9},{9,1},{17,25},{25,17},{2,10},{10... | collective-permute-start | bytes 1572872 | tf_op jit(solution)/shard_map/ppermute | solution.py:48
  280.9 81.5 %collective-permute-start = (bf16[256,2048]{1,0:T(8,128)(2,1)}, bf16[256,2048]{1,0:T(8,128)(2,1)}, u32[]{:S(2)}, u32[]{:S(2)}) collective-permute-start(bf16[256,2048]{1,0:T(8,128)(2,1)} %add_convert_fusion), channel_id=1, source_target_pairs={{0,8},{8,0},{16,24},{24,16},{1,9},{9,1},{17,25},{25,17},{2,10},{10... | collective-permute-start | bytes 3145736 | tf_op jit(solution)/shard_map/ppermute | solution.py:48
  280.9 84.3 %collective-permute-start.1 = (bf16[256,2048]{1,0:T(8,128)(2,1)}, bf16[256,2048]{1,0:T(8,128)(2,1)}, u32[]{:S(2)}, u32[]{:S(2)}) collective-permute-start(bf16[256,2048]{1,0:T(8,128)(2,1)} %add_convert_fusion), channel_id=1, source_target_pairs={{0,16},{8,24},{16,0},{24,8},{1,17},{9,25},{17,1},{25,9},{2,18},{10... | collective-permute-start | bytes 3145736 | tf_op jit(solution)/shard_map/ppermute | solution.py:48
  469.4 28.4 %collective-permute-start.12 = (bf16[128,2048]{1,0:T(8,128)(2,1)}, bf16[128,2048]{1,0:T(8,128)(2,1)}, u32[]{:S(2)}, u32[]{:S(2)}) collective-permute-start(bf16[128,2048]{1,0:T(8,128)(2,1)} %get-tuple-element.52), channel_id=1, source_target_pairs={{0,16},{8,24},{16,0},{24,8},{1,17},{9,25},{17,1},{25,9},{2,18},{10... | collective-permute-start | bytes 1572872 | tf_op jit(solution)/shard_map/ppermute | solution.py:48
  500.4 32.7 %collective-permute-start.15 = (bf16[256,2048]{1,0:T(8,128)(2,1)}, bf16[256,2048]{1,0:T(8,128)(2,1)}, u32[]{:S(2)}, u32[]{:S(2)}) collective-permute-start(bf16[256,2048]{1,0:T(8,128)(2,1)} %pad_maximum_fusion.5), channel_id=1, source_target_pairs={{0,16},{8,24},{16,0},{24,8},{1,17},{9,25},{17,1},{25,9},{2,18},{10... | collective-permute-start | bytes 3145736 | tf_op jit(solution)/shard_map/ppermute | solution.py:48
  503.0 30.7 %collective-permute-start.13 = (bf16[256,2048]{1,0:T(8,128)(2,1)}, bf16[256,2048]{1,0:T(8,128)(2,1)}, u32[]{:S(2)}, u32[]{:S(2)}) collective-permute-start(bf16[256,2048]{1,0:T(8,128)(2,1)} %pad_maximum_fusion.4), channel_id=1, source_target_pairs={{0,8},{8,0},{16,24},{24,16},{1,9},{9,1},{17,25},{25,17},{2,10},{10... | collective-permute-start | bytes 3145736 | tf_op jit(solution)/shard_map/ppermute | solution.py:48
  512.5 41.8 %collective-permute-start.7 = (bf16[256,2048]{1,0:T(8,128)(2,1)}, bf16[256,2048]{1,0:T(8,128)(2,1)}, u32[]{:S(2)}, u32[]{:S(2)}) collective-permute-start(bf16[256,2048]{1,0:T(8,128)(2,1)} %pad_maximum_fusion.3), channel_id=1, source_target_pairs={{0,16},{8,24},{16,0},{24,8},{1,17},{9,25},{17,1},{25,9},{2,18},{10... | collective-permute-start | bytes 3145736 | tf_op jit(solution)/shard_map/ppermute | solution.py:48
  515.0 39.5 %collective-permute-start.5 = (bf16[256,2048]{1,0:T(8,128)(2,1)}, bf16[256,2048]{1,0:T(8,128)(2,1)}, u32[]{:S(2)}, u32[]{:S(2)}) collective-permute-start(bf16[256,2048]{1,0:T(8,128)(2,1)} %pad_maximum_fusion.2), channel_id=1, source_target_pairs={{0,8},{8,0},{16,24},{24,16},{1,9},{9,1},{17,25},{25,17},{2,10},{10... | collective-permute-start | bytes 3145736 | tf_op jit(solution)/shard_map/ppermute | solution.py:48
  620.8 148.2 %reduce-scatter.12.cloned.1.call-start = ((), (), s32[]{:S(2)}) async-start(), calls=%async_computation.18 | async-start | bytes 9437184 | tf_op jit(solution)/shard_map/reduce_scatter | solution.py:387
  643.8 219.3 %reduce-scatter.14.cloned.1.call-start = ((), (), s32[]{:S(2)}) async-start(), calls=%async_computation.19 | async-start | bytes 9437184 | tf_op jit(solution)/shard_map/reduce_scatter | solution.py:384
  659.8 355.9 %reduce-scatter.10.cloned.1.call-start = ((), (), s32[]{:S(2)}) async-start(), calls=%async_computation.17 | async-start | bytes 8650752 | tf_op jit(solution)/shard_map/reduce_scatter | solution.py:409
  667.3 438.0 %reduce-scatter.6.cloned.1.call-start = ((), (), s32[]{:S(2)}) async-start(), calls=%async_computation.15 | async-start | bytes 9437184 | tf_op jit(solution)/shard_map/reduce_scatter | solution.py:415
  702.9 38.2 %all-to-all-start.4 = ((bf16[8,64,768]{2,1,0:T(8,128)(2,1)}), bf16[8,64,768]{2,1,0:T(8,128)(2,1)}, u32[]{:S(2)}, u32[]{:S(2)}) async-start(bf16[8,64,768]{2,1,0:T(8,128)(2,1)} %bitcast.193), calls=%async_computation.6 | async-start | bytes 1572864 | tf_op jit(solution)/shard_map/all_to_all | solution.py:425
  769.0 96.9 %all-to-all-start.6 = ((bf16[4,64,2048]{2,1,0:T(8,128)(2,1)}), bf16[4,64,2048]{2,1,0:T(8,128)(2,1)}, u32[]{:S(2)}, u32[]{:S(2)}) async-start(bf16[4,64,2048]{2,1,0:T(8,128)(2,1)} %bitcast.188), calls=%async_computation.10 | async-start | bytes 2097152 | tf_op jit(solution)/shard_map/all_to_all | solution.py:389
  (36 other events, 720.3 us)
Sparse Core Ops, SparseCore 0:
  37.3 51.7 all-gather.11
  90.7 82.1 all-gather.17
  175.8 96.0 all-gather.13
  273.4 80.3 all-gather.19
  355.2 80.5 all-gather.15
  620.9 41.8 reduce-scatter.7
  665.1 103.8 reduce-scatter.11
  771.3 91.7 reduce-scatter.13
  865.4 150.2 reduce-scatter.9
  1017.8 87.4 reduce-scatter.5

commit v2 on v1

--- a/solution.py
+++ b/solution.py
@@ -9,6 +9,7 @@
 EPSILON = 1e-05
 ALL = ("dp", "seq", "fsdp")
 LINE = ("seq", "fsdp")
+FAR = ((0, 2), (1, 3))
 f32 = jnp.float32
 bf16 = jnp.bfloat16
 
@@ -43,45 +44,395 @@
     return hidden * half, slope
 
 
-def permute(value, axis, mask):
-    count = lax.axis_size(axis)
-    return lax.ppermute(value, axis, [(i, i ^ mask) for i in range(count)])
-
-
-def gather_dp(block):
-    if lax.axis_size("dp") != 4:
-        return lax.all_gather(block, "dp", axis=0, tiled=False)
-    half = block.shape[0] // 2
-    one = permute(block, "dp", 1)
-    two = permute(block, "dp", 2)
-    top = permute(two[:half], "dp", 1)
-    low = permute(one[half:], "dp", 2)
-    return jnp.stack([block, one, two, jnp.concatenate([top, low], axis=0)])
-
-
-def gather_dp_rows(block):
-    return lax.all_gather(block, "dp", axis=0, tiled=True)
-
-
-def scatter_dp(parts):
-    if lax.axis_size("dp") != 4:
-        return lax.psum_scatter(parts.astype(bf16), "dp", scatter_dimension=0, tiled=False).astype(f32)
-    half = parts.shape[1] // 2
+def swap(value, axis, mask):
+    return lax.ppermute(value, axis, [(i, i ^ mask) for i in range(lax.axis_size(axis))])
+
+
+def hop(value, pairs):
+    return lax.ppermute(value, "seq", list(pairs))
+
+
+def in_plane():
+    return lax.axis_size("dp") == 4 and lax.axis_size("seq") == 4 and lax.axis_size("fsdp") == 2
+
+
+def after(value, *earlier):
+    return lax.optimization_barrier((value,) + earlier)[0]
+
+
+def assemble(shape, parts, copies, scalars):
+    def body(s_ref, *refs):
+        out, sems = refs[len(parts)], refs[len(parts) + 1]
+        flights = []
+        for number, (part, source, target) in enumerate(copies):
+            flight = pltpu.make_async_copy(refs[part].at[source], out.at[target(s_ref)], sems.at[number])
+            flight.start()
+            flights.append(flight)
+        for flight in flights:
+            flight.wait()
+
+    size = 2 * shape[-1]
+    for extent in shape[:-1]:
+        size *= extent
+    return call(
+        body,
+        in_specs=[pl.BlockSpec(memory_space=pltpu.SMEM)] + [pl.BlockSpec(memory_space=pl.ANY)] * len(parts),
+        out_specs=pl.BlockSpec(memory_space=pltpu.VMEM),
+        out_shape=jax.ShapeDtypeStruct(shape, bf16),
+        scratch_shapes=[pltpu.SemaphoreType.DMA((len(copies),))],
+        cost_estimate=cost(flops=0, bytes_accessed=2 * size, transcendentals=0),
+    )(jnp.stack(scalars).astype(jnp.int32), *parts)
+
+
+def pick(whole, at, axis=0):
+    return lax.dynamic_index_in_dim(whole, at, axis, keepdims=False)
+
+
+def unxor(value, axis, at):
+    shape = value.shape
+    bit = 1
+    while bit < shape[axis]:
+        pairs = value.reshape(shape[:axis] + (-1, 2, bit) + shape[axis + 1 :])
+        other = jnp.flip(pairs, axis + 1).reshape(shape)
+        value = jnp.where((at & bit) != 0, other, value)
+        bit *= 2
+    return value
+
+
+def scatter_one(parts):
+    half = parts[0].shape[0] // 2
     low = parts[3].astype(bf16)
-    from_one = permute(low[:half], "dp", 1).astype(f32)
-    from_two = permute(low[half:], "dp", 2).astype(f32)
-    two = jnp.concatenate([parts[2, :half] + from_one, parts[2, half:]], axis=0)
-    one = jnp.concatenate([parts[1, :half], parts[1, half:] + from_two], axis=0)
-    return (
-        parts[0]
-        + permute(one.astype(bf16), "dp", 1).astype(f32)
-        + permute(two.astype(bf16), "dp", 2).astype(f32)
-    )
+    return swap(low[:half], "dp", 1), swap(low[half:], "dp", 2)
+
+
+def scatter_mid(parts, got):
+    half = parts[0].shape[0] // 2
+    one, two = parts[1].astype(f32), parts[2].astype(f32)
+    two = jnp.concatenate([two[:half] + got[0].astype(f32), two[half:]], axis=0).astype(bf16)
+    one = jnp.concatenate([one[:half], one[half:] + got[1].astype(f32)], axis=0).astype(bf16)
+    return one, two
+
+
+def scatter_send(mid):
+    return swap(mid[0], "dp", 1), swap(mid[1], "dp", 2)
+
+
+def scatter_two(parts, got):
+    return scatter_send(scatter_mid(parts, got))
+
+
+def scatter_sum(parts, got):
+    return parts[0].astype(f32) + got[0].astype(f32) + got[1].astype(f32)
+
+
+class Plane:
+    def __init__(self, share, feed, width):
+        self.dp, self.seq, self.core = [lax.axis_index(axis) for axis in ALL]
+        self.near, self.far = self.seq & 1, self.seq >> 1
+        self.share, self.feed_width, self.width = share, feed, width
+        self.block = feed // 32
+
+    def begin(self, send, inputs, weights, dy):
+        w_out, w_up, self.w_down = weights
+        self.dy = dy
+        share, rows = self.share, dy.shape[0]
+        half = rows // 2
+        halves = send.reshape(4, 2, share + 16, -1)
+        got = swap(pick(halves, 1 - self.core, 1), "fsdp", 1)
+        both = jnp.stack([pick(halves, self.core, 1), got], axis=1)
+        dy_one, dy_two = swap(dy, "dp", 1), swap(dy, "dp", 2)
+        whole = w_up.reshape(share, 4, 2, 2, 2 * self.block)
+        split = lambda near: pick(whole, near, 3).transpose(1, 0, 2, 3).reshape(4, share, 4 * self.block)
+        near = swap(split(1 - self.near), "seq", 1)
+        out_line = lax.all_gather(w_out, "seq", axis=0, tiled=False)
+        block = [pick(both, self.seq)] + [swap(pick(both, self.seq ^ k), "seq", k) for k in (1, 2, 3)]
+        block = after(jnp.stack(block), dy_one, dy_two, near)
+        line = lax.all_gather(after(inputs, block), LINE, axis=0, tiled=False)
+
+        one, two = swap(block, "dp", 1), swap(block, "dp", 2)
+        dy_top = swap(after(dy_two[:half], block), "dp", 1)
+        dy_low = swap(after(dy_one[half:], block), "dp", 2)
+        self.dy_first = jnp.concatenate([dy, dy_one, dy_two, dy_top, dy_low], axis=0)
+        one, two, dy_top, dy_low = lax.optimization_barrier((one, two, dy_top, dy_low))
+
+        top, low = swap(two[:2], "dp", 1), swap(one[2:], "dp", 2)
+        columns = jnp.stack([split(self.near), near], axis=1)
+        self.up_rows = jnp.stack(
+            [pick(columns, self.dp)] + [swap(after(pick(columns, self.dp ^ k), one), "dp", k) for k in (1, 2, 3)]
+        )
+        self.out_mine = out_line
+        self.out_one, self.out_two = [swap(after(out_line, top, low), "dp", k) for k in (1, 2)]
+        line = after(line, self.up_rows, self.out_one, self.out_two)
+
+        copies = []
+        for k in range(4):
+            for z in range(4):
+                for f in range(2):
+                    part, at = (k, z) if k < 3 else (3 + z // 2, z % 2)
+                    target = lambda s, k=k, z=z, f=f: (s[0] ^ k, s[1] ^ z, s[2] ^ f)
+                    copies.append((part, (at, f, slice(0, share)), target))
+        parts = [block, one, two, top, low]
+        shape = (4, 4, 2, share, block.shape[3])
+        qkv_own = assemble(shape, parts, copies, [self.dp, self.seq, self.core]).reshape(self.width, -1)
+        small = [block[:, :, share], one[:, :, share], two[:, :, share]]
+        small.append(jnp.concatenate([top[:, :, share], low[:, :, share]], axis=0))
+        small = unxor(unxor(unxor(jnp.stack(small), 0, self.dp), 1, self.seq), 2, self.core).reshape(32, -1)
+        ids = unxor(unxor(block[:, :, share + 1, :rows], 0, self.seq), 1, self.core).reshape(8, rows)
+        return line, qkv_own, small, ids
+
+    def tokens_there(self, tokens):
+        self.dy_near = swap(after(self.dy, tokens), "seq", 1)
+        down = lax.all_gather(after(self.w_down, tokens), "seq", axis=0, tiled=False, axis_index_groups=FAR)
+        up = lax.all_gather(after(self.up_rows, tokens), "seq", axis=0, tiled=False, axis_index_groups=FAR)
+        self.gathered = (up, down)
+
+    def out_start(self, qkv, context):
+        top, low = swap(self.out_two[:2], "dp", 1), swap(self.out_one[2:], "dp", 2)
+        parts = [self.out_mine, self.out_one, self.out_two, jnp.concatenate([top, low], axis=0)]
+        self.out_mine = jnp.stack(parts)
+        self.dy_one, self.dy_two = [swap(after(self.dy_near, context), "dp", k) for k in (1, 2)]
+        return after(context, top, low)
+
+    def out(self, context):
+        mine = self.out_mine
+        other = swap(mine, "fsdp", 1)
+        context = after(context, self.dy_one, self.dy_two, self.gathered[1])
+        copies = [
+            (f, (k, z), lambda s, f=f, k=k, z=z: (s[0] ^ k, z, s[1] ^ f))
+            for f in range(2)
+            for k in range(4)
+            for z in range(4)
+        ]
+        whole = assemble(
+            (4, 4, 2, self.share, self.width), [mine, other], copies, [self.dp, self.core]
+        )
+        return whole.reshape(self.width, self.width), context
+
+    def gather(self, normed):
+        half = normed.shape[0] // 2
+        near, dy_one, dy_two = self.dy_near, self.dy_one, self.dy_two
+        dy_top, dy_low = swap(dy_two[:half], "dp", 1), swap(dy_one[half:], "dp", 2)
+        dy_second = jnp.concatenate([near, dy_one, dy_two, dy_top, dy_low], axis=0)
+        normed = after(normed, dy_top, dy_low)
+        other = swap(normed, "seq", 1)
+        one, two = swap(normed, "dp", 1), swap(normed, "dp", 2)
+        halves = lax.optimization_barrier((two[:half], one[half:]))
+        top, low = swap(halves[0], "dp", 1), swap(halves[1], "dp", 2)
+        up, down = [after(part, *halves) for part in self.gathered]
+        up_other, down_other = swap(up, "fsdp", 1), swap(down, "fsdp", 1)
+        first = jnp.concatenate([normed, one, two, top, low], axis=0)
+        other_one, other_two = [swap(after(other, top, low), "dp", k) for k in (1, 2)]
+        other_top, other_low = swap(other_two[:half], "dp", 1), swap(other_one[half:], "dp", 2)
+        second = jnp.concatenate([other, other_one, other_two, other_top, other_low], axis=0)
+        copies = [(f, (far,), lambda s, far=far, f=f: (far, s[0] ^ f)) for far in range(2) for f in range(2)]
+        shape = (2, 2, self.block, self.width)
+        down = assemble(shape, [down, down_other], copies, [self.core]).reshape(4 * self.block, self.width)
+        copies = [
+            (f, (far, k, n), lambda s, far=far, f=f, k=k, n=n: (s[0] ^ k, far, s[1] ^ n, s[2] ^ f))
+            for far in range(2)
+            for f in range(2)
+            for k in range(4)
+            for n in range(2)
+        ]
+        shape = (4, 2, 2, 2, self.share, 4 * self.block)
+        up = assemble(shape, [up, up_other], copies, [self.dp, self.near, self.core])
+        return [first, second], [self.dy_first, dy_second], up.reshape(self.width, 4 * self.block), down
+
+    def bias(self, table):
+        return pick(pick(table.reshape(4, 2, 2, 2, -1), self.dp).transpose(1, 0, 2, 3), self.near).reshape(1, -1)
+
+    def bias_spread(self, own):
+        whole = jnp.zeros((4, 2, 2, 2, self.block), f32)
+        own = own.reshape(1, 2, 1, 2, self.block)
+        return lax.dynamic_update_slice(whole, own, (self.dp, 0, self.near, 0, 0)).reshape(-1)
+
+    def feed(self, groups, dys, up, down, bias):
+        own_act, own_gh, own_gn = feed_forward(groups[0], dys[0], up, down, bias)
+        own_parts = jnp.split(own_gn, 4)
+        own_one = scatter_one(own_parts)
+        act, gh, gn = feed_forward(after(groups[1], *own_one), dys[1], up, down, bias)
+        own_two = scatter_two(own_parts, own_one)
+        parts = jnp.split(after(gn, *own_two), 4)
+        mid = scatter_mid(parts, scatter_one(parts))
+        two = scatter_send(mid)
+        self.acts = after(jnp.concatenate([own_act, act], axis=0), *mid)
+        ghs = after(jnp.concatenate([own_gh, gh], axis=0), *mid)
+        grad_down = dot(self.acts, jnp.concatenate(dys, axis=0), ((0,), (0,))).astype(bf16)
+        fed = dot(after(self.acts, grad_down), down, ((1,), (0,))).astype(bf16)
+        self.fed = [fed.reshape(2, 4, -1, self.width)[:, k] for k in range(4)]
+        whole = grad_down.reshape(2, 2, self.block, self.width)
+        theirs = swap(pick(whole, 1 - self.core, 1), "fsdp", 1)
+        grad_down = (pick(whole, self.core, 1).astype(f32) + after(theirs, fed).astype(f32)).astype(bf16)
+        ghs = after(ghs, grad_down)
+        grad_up = dot(jnp.concatenate(groups, axis=0), ghs, ((0,), (0,))).astype(bf16)
+        whole = grad_up.reshape(4, 2, 2, 2, self.share, -1)
+        theirs = swap(pick(whole, 1 - self.core, 3), "fsdp", 1)
+        grad_up = (pick(whole, self.core, 3).astype(f32) + theirs.astype(f32)).astype(bf16)
+        grad_up = grad_up.transpose(1, 0, 2, 3, 4)
+        self.grad_down, rows = [
+            lax.psum_scatter(
+                grad.reshape(2 * self.block, self.width) if k == 0 else grad.reshape(self.width // 2, -1),
+                "seq",
+                scatter_dimension=0,
+                tiled=True,
+                axis_index_groups=FAR,
+            )
+            for k, grad in enumerate((grad_down, grad_up))
+        ]
+        self.grad_down = self.grad_down.astype(f32)
+        self.up_rows = rows.reshape(4, 2, self.share, -1)
+        other = scatter_sum(parts, two).astype(bf16)
+        grad = scatter_sum(own_parts, own_two) + swap(other, "seq", 1).astype(f32)
+        self.fed_one = scatter_one([after(part, other) for part in self.fed])
+        self.grad_up = grad_up
+        return after(grad, grad_down), ghs
+
+    def before_exchange(self, grad_context):
+        return after(grad_context, self.grad_up, *self.fed_one)
+
+    def before_attention(self, got, sent, grad_out_w):
+        fed_one = [after(part, sent) for part in self.fed_one]
+        self.fed_two = scatter_two(self.fed, fed_one)
+        whole = grad_out_w.reshape(4, 4, 2, self.share, self.width)
+        theirs = swap(pick(whole, 1 - self.core, 2), "fsdp", 1)
+        whole = (pick(whole, self.core, 2).astype(f32) + theirs.astype(f32)).astype(bf16)
+        self.out_parts = [pick(whole, self.dp ^ k) for k in range(4)]
+        return after(got, whole)
+
+    def before_norm(self, grad_qkv):
+        own, other = scatter_sum(self.fed, self.fed_two)
+        self.feed_out = own + swap(other.astype(bf16), "seq", 1).astype(f32)
+        self.out_one = scatter_one(self.out_parts)
+        return after(grad_qkv, *self.fed_two, *self.out_one)
+
+    def last(self, normed, grad_qkv):
+        grad = dot(normed, grad_qkv, ((0,), (0,))).astype(bf16)
+        out_two = scatter_two(self.out_parts, self.out_one)
+        parts = [pick(grad.reshape(4, -1, grad.shape[1]), self.dp ^ k) for k in range(4)]
+        parts[3] = after(parts[3], *out_two)
+        one = scatter_one(parts)
+        line = scatter_sum(self.out_parts, out_two).reshape(2, 2, self.share, self.width)
+        away = pick(line, 1 - self.far)
+        away = away + hop(away.astype(bf16), ((0, 1), (3, 2))).astype(f32)
+        line = pick(line, self.far) + hop(away.astype(bf16), ((1, 2), (2, 1))).astype(f32)
+        grad_out = pick(line, self.near) + swap(pick(line, 1 - self.near).astype(bf16), "seq", 1).astype(f32)
+        two = scatter_two(parts, one)
+        grad_up = self.up_back_end(after(self.up_rows, *one))
+        return scatter_sum(parts, two), grad_out, grad_up, self.grad_down
+
+    def up_back_end(self, rows):
+        parts = [pick(rows, self.dp)] + [swap(pick(rows, self.dp ^ k), "dp", k) for k in (1, 2, 3)]
+        parts = jnp.stack(parts)
+        pair = [pick(parts, self.near, 1), swap(pick(parts, 1 - self.near, 1), "seq", 1)]
+        wide = 2 * self.block
+
+        def body(s_ref, own_ref, other_ref, out_ref):
+            for n, ref in enumerate((own_ref, other_ref)):
+                for k in range(4):
+                    for far in range(2):
+                        at = ((s_ref[0] ^ k) * 4 + far * 2 + (s_ref[1] ^ n)) * wide
+                        piece = ref[k, :, far * wide : (far + 1) * wide]
+                        out_ref[:, pl.ds(pl.multiple_of(at, wide), wide)] = piece.astype(f32)
+
+        return call(
+            body,
+            in_specs=[pl.BlockSpec(memory_space=pltpu.SMEM)] + [pl.BlockSpec(memory_space=pltpu.VMEM)] * 2,
+            out_specs=pl.BlockSpec(memory_space=pltpu.VMEM),
+            out_shape=jax.ShapeDtypeStruct((self.share, self.feed_width), f32),
+            cost_estimate=cost(flops=0, bytes_accessed=6 * self.share * self.feed_width, transcendentals=0),
+        )(jnp.stack([self.dp, self.near]).astype(jnp.int32), *pair)
+
+
+class General:
+    def __init__(self, share, feed, width):
+        self.dp, self.n_dp, self.line = lax.axis_index("dp"), lax.axis_size("dp"), lax.axis_size(LINE)
+        self.share, self.feed_width = share, feed
+
+    def begin(self, send, inputs, weights, dy):
+        self.w_out, self.w_up, self.w_down = weights
+        self.dy = dy
+        line = lax.all_gather(inputs, LINE, axis=0, tiled=False)
+        got = lax.all_to_all(send, LINE, split_axis=0, concat_axis=0, tiled=True)
+        whole = lax.all_gather(got, "dp", axis=0, tiled=True)
+        share = self.share
+        ids = got[:, share + 1, : dy.shape[0]]
+        return line, whole[:, :share].reshape(-1, got.shape[2]), whole[:, share], ids
+
+    def tokens_there(self, tokens):
+        pass
+
+    def out_start(self, qkv, context):
+        return context
+
+    def out(self, context):
+        return lax.all_gather(self.w_out, ALL, axis=0, tiled=True), context
+
+    def gather(self, normed):
+        groups = [
+            jnp.split(lax.all_gather(block, "dp", axis=0, tiled=True), self.groups()) for block in (normed, self.dy)
+        ]
+        sent = self.w_up.reshape(self.share, self.n_dp, -1).transpose(1, 0, 2)
+        rows = lax.all_to_all(sent, "dp", split_axis=0, concat_axis=0, tiled=True)
+        rows = lax.all_gather(rows, LINE, axis=0, tiled=False).transpose(1, 0, 2, 3)
+        up = rows.reshape(-1, self.feed_width // self.n_dp)
+        return groups[0], groups[1], up, lax.all_gather(self.w_down, LINE, axis=0, tiled=True)
+
+    def bias(self, table):
+        return pick(table.reshape(self.n_dp, 1, -1), self.dp)
+
+    def bias_spread(self, own):
+        whole = jnp.zeros((self.n_dp, own.shape[0]), f32)
+        return lax.dynamic_update_slice_in_dim(whole, own[None], self.dp, 0).reshape(-1)
+
+    def groups(self):
+        return 2 if self.n_dp % 2 == 0 else 1
+
+    def scatter(self, groups):
+        whole = jnp.concatenate(groups, axis=0)
+        return lax.psum_scatter(whole, "dp", scatter_dimension=0, tiled=True).astype(f32)
+
+    def feed(self, groups, dys, up, down, bias):
+        own = self.feed_width // self.n_dp
+        done = [feed_forward(x, dy, up, down, bias) for x, dy in zip(groups, dys)]
+        acts, ghs = [jnp.concatenate([part[k] for part in done], axis=0) for k in range(2)]
+        grad_down = dot(acts, jnp.concatenate(dys, axis=0), ((0,), (0,))).astype(bf16)
+        self.grad_down = lax.psum_scatter(grad_down, LINE, scatter_dimension=0, tiled=True).astype(f32)
+        rows = dot(jnp.concatenate(groups, axis=0), ghs, ((0,), (0,))).astype(bf16)
+        rows = rows.reshape(self.n_dp, self.line, self.share, own).transpose(1, 0, 2, 3).reshape(-1, own)
+        rows = lax.psum_scatter(rows, LINE, scatter_dimension=0, tiled=True).reshape(self.n_dp, self.share, own)
+        rows = lax.all_to_all(rows, "dp", split_axis=0, concat_axis=0, tiled=True)
+        self.grad_up = rows.transpose(1, 0, 2).reshape(self.share, self.feed_width).astype(f32)
+        self.feed_out = self.scatter([dot(part[0], down, ((1,), (0,))).astype(bf16) for part in done])
+        return self.scatter([part[2] for part in done]), ghs
+
+    def before_exchange(self, grad_context):
+        return grad_context
+
+    def before_attention(self, got, sent, grad_out_w):
+        self.grad_out = lax.psum_scatter(grad_out_w, ALL, scatter_dimension=0, tiled=True).astype(f32)
+        return got
+
+    def before_norm(self, grad_qkv):
+        return grad_qkv
+
+    def last(self, normed, grad_qkv):
+        grad = dot(normed, grad_qkv, ((0,), (0,))).astype(bf16)
+        grad = lax.psum_scatter(grad, "dp", scatter_dimension=0, tiled=True)
+        return grad, self.grad_out, self.grad_up, self.grad_down
 
 
 BLOCK = 256
 LOG2E = 1.4426950408889634
 VMEM_BYTES = 56 * 2**20
+
+
+COST = 1000
+
+
+def cost(flops, bytes_accessed, transcendentals):
+    return pl.CostEstimate(
+        flops=flops // COST, bytes_accessed=bytes_accessed // COST, transcendentals=transcendentals // COST
+    )
 
 
 def call(body, **options):
@@ -109,7 +460,7 @@
         in_specs=[part(width), whole((1, width)), whole((1, width)), whole(weight.shape), whole((1, out))],
         out_specs=[part(width), part(out)],
         out_shape=[jax.ShapeDtypeStruct((rows, width), bf16), jax.ShapeDtypeStruct((rows, out), bf16)],
-        cost_estimate=pl.CostEstimate(
+        cost_estimate=cost(
             flops=2 * rows * width * out, bytes_accessed=4 * rows * width + 2 * out * (rows + width), transcendentals=0
         ),
     )(tokens, gain, beta, weight, bias)
@@ -225,7 +576,7 @@
             jax.ShapeDtypeStruct((blocks, seqs, span, cols), bf16),
             jax.ShapeDtypeStruct((seqs, length, heads), f32),
         ],
-        cost_estimate=pl.CostEstimate(
+        cost_estimate=cost(
             flops=4 * seqs * cols * length * length,
             bytes_accessed=8 * seqs * length * cols,
             transcendentals=seqs * heads * length * length,
@@ -245,7 +596,7 @@
         out_specs=three,
         out_shape=jax.ShapeDtypeStruct(qkv.shape, bf16),
         scratch_shapes=[pltpu.VMEM((length, HEAD_DIM), f32)] * 2,
-        cost_estimate=pl.CostEstimate(
+        cost_estimate=cost(
             flops=10 * seqs * cols * length * length,
             bytes_accessed=14 * seqs * length * cols,
             transcendentals=seqs * heads * length * length,
@@ -283,10 +634,41 @@
             jax.ShapeDtypeStruct((1, width), f32),
             jax.ShapeDtypeStruct((1, width), f32),
         ],
-        cost_estimate=pl.CostEstimate(
+        cost_estimate=cost(
             flops=2 * rows * width * inner, bytes_accessed=4 * rows * width + 2 * inner * (rows + width), transcendentals=0
         ),
     )(grad_qkv, weight, tokens)
+
+
+def feed_body(x_ref, dy_ref, up_ref, down_ref, bias_ref, act_ref, gh_ref, gn_ref):
+    up = up_ref[...]
+    hidden = dot(x_ref[...], up, ((1,), (0,))) + bias_ref[...]
+    grad = dot(dy_ref[...], down_ref[...], ((1,), (1,)))
+    activated, slope = gelu_both(hidden)
+    act_ref[...] = activated.astype(bf16)
+    grad = (grad * slope).astype(bf16)
+    gh_ref[...] = grad
+    gn_ref[...] = dot(grad, up, ((1,), (1,))).astype(bf16)
+
+
+def feed_forward(x, dy, up, down, bias):
+    rows, width = x.shape
+    feed = up.shape[1]
+    tile = 256
+    whole = lambda shape: pl.BlockSpec(shape, lambda i: (0, 0), pipeline_mode=pl.Buffered(1))
+    part = lambda cols: pl.BlockSpec((tile, cols), lambda i: (i, 0))
+    return call(
+        feed_body,
+        grid=(rows // tile,),
+        in_specs=[part(width), part(width), whole(up.shape), whole(down.shape), whole(bias.shape)],
+        out_specs=[part(feed), part(feed), part(width)],
+        out_shape=[jax.ShapeDtypeStruct((rows, feed), bf16)] * 2 + [jax.ShapeDtypeStruct((rows, width), bf16)],
+        cost_estimate=cost(
+            flops=6 * rows * width * feed,
+            bytes_accessed=6 * rows * width + 4 * feed * (rows + width),
+            transcendentals=rows * feed,
+        ),
+    )(x, dy, up, down, bias)
 
 
 def on_device(
@@ -314,83 +696,53 @@
     length = span * n_line
     share = w_qkv.shape[0]
     feed = w_up.shape[1]
-    feed_own = feed // n_dp
     cols = width // n_line
     heads = cols // HEAD_DIM
     score_scale = HEAD_DIM ** (-0.5)
     line_at = lax.axis_index(LINE)
 
-    small = jnp.stack(
-        [gain_one, beta_one, bias_query, bias_value, bias_out, gain_two, beta_two, bias_down]
-    ).reshape(-1)
-    small = jnp.concatenate([small, bias_up])
-    small_all = lax.all_gather(small, ALL, axis=0, tiled=False).astype(f32)
+    feeder = (Plane if in_plane() else General)(share, feed, width)
+
+    vectors = jnp.stack([gain_one, beta_one, bias_query, bias_value, bias_out, gain_two, beta_two, bias_down])
+    small = jnp.concatenate([vectors.reshape(-1), bias_up])
+    extra = jnp.zeros((16, 3 * cols), bf16)
+    extra = extra.at[0, : small.shape[0]].set(small)
+    extra = extra.at[1, :rows].set(block_ids.astype(bf16).reshape(-1))
+    qkv_send = w_qkv.reshape(share, 3, n_line, cols).transpose(2, 0, 1, 3).reshape(n_line, share, 3 * cols)
+    extra = jnp.broadcast_to(extra[None], (n_line,) + extra.shape)
+    qkv_send = jnp.concatenate([qkv_send, extra], axis=1)
+    grad_out = cotangent.reshape(rows, width)
+    tokens_line, qkv_own, small_all, ids = feeder.begin(qkv_send, inputs, (w_out, w_up, w_down), grad_out)
+    ids = ids.astype(f32).reshape(n_line, seqs, span).transpose(1, 0, 2).reshape(seqs, length)
+    small_all = small_all[:, : small.shape[0]].astype(f32)
     vectors = small_all[:, : 8 * share].reshape(-1, 8, share).transpose(1, 0, 2).reshape(8, width)
     gain1, beta1, biasq, biasv, biaso, gain2, beta2, biasd = [vectors[i][None] for i in range(8)]
-    up_bias_all = small_all[:, 8 * share :].reshape(n_dp, 1, feed_own)
-    up_bias = lax.dynamic_index_in_dim(up_bias_all, lax.axis_index("dp"), 0, keepdims=False)
+    up_bias = feeder.bias(small_all[:, 8 * share :])
     biasq_own = lax.dynamic_slice_in_dim(biasq, line_at * cols, cols, 1)
     biasv_own = lax.dynamic_slice_in_dim(biasv, line_at * cols, cols, 1)
 
-    qkv_send = w_qkv.reshape(share, 3, n_line, cols).transpose(2, 0, 1, 3).reshape(n_line, share, 3 * cols)
-    qkv_got = lax.all_to_all(qkv_send, LINE, split_axis=0, concat_axis=0, tiled=True)
-    qkv_own = gather_dp_rows(qkv_got.reshape(n_line * share, 3 * cols))
-    tokens_line = lax.all_gather(inputs, LINE, axis=0, tiled=False)
-    ids_line = lax.all_gather(block_ids.astype(bf16), LINE, axis=0, tiled=False)
-
-    out_full = lax.all_gather(w_out, ALL, axis=0, tiled=True)
-    up_send = w_up.reshape(share, n_dp, feed_own).transpose(1, 0, 2)
-    up_got = lax.all_to_all(up_send, "dp", split_axis=0, concat_axis=0, tiled=True)
-    up_own = (
-        lax.all_gather(up_got, LINE, axis=0, tiled=False)
-        .transpose(1, 0, 2, 3)
-        .reshape(width, feed_own)
-    )
-    down_own = lax.all_gather(w_down, LINE, axis=0, tiled=True)
-
     tokens_line = tokens_line.reshape(n_line * rows, width)
+    tokens_line, qkv_own, vectors = lax.optimization_barrier((tokens_line, qkv_own, vectors))
+    feeder.tokens_there(tokens_line)
     bias_row = jnp.concatenate([biasq_own, jnp.zeros_like(biasq_own), biasv_own], axis=1)
     normed_one, qkv = norm_project(tokens_line, gain1, beta1, qkv_own, bias_row)
     qkv = qkv.reshape(n_line, seqs, span, 3 * cols)
-    ids = ids_line.astype(f32).transpose(1, 0, 2).reshape(seqs, length)
     numbers = (line_at * heads + jnp.arange(heads)).astype(f32)
     slopes = jnp.exp2(-8.0 * (numbers + 1.0) / (n_line * heads))[None]
     context_own, stats = attend(slopes, ids, qkv, score_scale)
     context_own = context_own.reshape(n_line, rows, cols)
-    context = (
-        lax.all_to_all(context_own, LINE, split_axis=0, concat_axis=0, tiled=True)
-        .transpose(1, 0, 2)
-        .reshape(rows, width)
-    )
+    context_own = feeder.out_start(qkv, context_own)
+    context = lax.all_to_all(context_own, LINE, split_axis=0, concat_axis=0, tiled=True)
+    out_full, context = feeder.out(context)
+    context = context.transpose(1, 0, 2).reshape(rows, width)
 
     tokens = inputs.astype(f32).reshape(rows, width)
     residual = tokens + dot(context, out_full, ((1,), (0,))) + biaso
     normal_two, scale_two = norm_parts(residual)
     normed_two = (normal_two * gain2 + beta2).astype(bf16)
 
-    grad_out = cotangent.reshape(rows, width)
-    grad_out_dp = gather_dp(grad_out).reshape(n_dp * rows, width)
-    normed_two_dp = gather_dp(normed_two).reshape(n_dp * rows, width)
-    hidden = dot(normed_two_dp, up_own, ((1,), (0,))) + up_bias
-    activated_f, gelu_slope = gelu_both(hidden)
-    activated = activated_f.astype(bf16)
-    grad_hidden_f = dot(grad_out_dp, down_own, ((1,), (1,))) * gelu_slope
-    grad_hidden = grad_hidden_f.astype(bf16)
-    grad_normed_two = scatter_dp(dot(grad_hidden, up_own, ((1,), (1,))).reshape(n_dp, rows, width))
-    feed_out = scatter_dp(dot(activated, down_own, ((1,), (0,))).reshape(n_dp, rows, width))
-    outputs = (residual + feed_out + biasd).astype(bf16).reshape(seqs, span, width)
-
-    grad_down = dot(activated, grad_out_dp, ((0,), (0,))).astype(bf16)
-    grad_w_down = lax.psum_scatter(grad_down, LINE, scatter_dimension=0, tiled=True).astype(f32)
-    grad_up = dot(normed_two_dp, grad_hidden, ((0,), (0,))).astype(bf16)
-    grad_up = grad_up.reshape(n_dp, n_line, share, feed_own).transpose(1, 0, 2, 3).reshape(width, feed_own)
-    grad_up = lax.psum_scatter(grad_up, LINE, scatter_dimension=0, tiled=True).reshape(n_dp, share, feed_own)
-    grad_w_up = (
-        lax.all_to_all(grad_up, "dp", split_axis=0, concat_axis=0, tiled=True)
-        .transpose(1, 0, 2)
-        .reshape(share, feed)
-        .astype(f32)
-    )
+    normed_groups, grad_out_groups, up_own, down_own = feeder.gather(normed_two)
+    grad_normed_two, grad_hidden = feeder.feed(normed_groups, grad_out_groups, up_own, down_own, up_bias)
     bias_up_part = jnp.sum(grad_hidden.astype(f32), axis=0)
 
     grad_out_f = grad_out.astype(f32)
@@ -402,14 +754,15 @@
 
     grad_branch = grad_residual.astype(bf16)
     grad_context = dot(grad_branch, out_full, ((1,), (1,))).astype(bf16)
-    grad_context = lax.all_to_all(
-        grad_context.reshape(rows, n_line, cols).transpose(1, 0, 2), LINE, split_axis=0, concat_axis=0, tiled=True
-    ).reshape(n_line, seqs, span, cols)
+    grad_context = grad_context.reshape(rows, n_line, cols).transpose(1, 0, 2)
+    grad_context = feeder.before_exchange(grad_context)
+    grad_branch = after(grad_branch, grad_context)
+    sent = grad_context
+    grad_context = lax.all_to_all(grad_context, LINE, split_axis=0, concat_axis=0, tiled=True)
     grad_out_w = dot(context, grad_branch, ((0,), (0,))).astype(bf16)
-    grad_w_out = lax.psum_scatter(grad_out_w, ALL, scatter_dimension=0, tiled=True).astype(f32)
-
+    grad_context = feeder.before_attention(grad_context, sent, grad_out_w).reshape(n_line, seqs, span, cols)
     grad_qkv = attend_back(slopes, ids, qkv, grad_context, stats, score_scale).reshape(n_line * rows, 3 * cols)
-
+    grad_qkv = feeder.before_norm(grad_qkv)
     grad_normed_part, gain1_part, beta1_part = norm_one_back(grad_qkv, qkv_own, tokens_line)
     gain1_part, beta1_part = gain1_part[0], beta1_part[0]
     grad_normed_one = lax.psum_scatter(
@@ -419,8 +772,9 @@
     grad_inputs = grad_residual + norm_back(grad_normed_one, gain1, normal_one, scale_one)
     bias_qkv_part = jnp.sum(grad_qkv.astype(f32), axis=0)
 
-    grad_qkv_w = dot(normed_one, grad_qkv, ((0,), (0,))).astype(bf16)
-    grad_qkv_w = lax.psum_scatter(grad_qkv_w, "dp", scatter_dimension=0, tiled=True)
+    grad_qkv_w, grad_w_out, grad_w_up, grad_w_down = feeder.last(normed_one, grad_qkv)
+    grad_qkv_w = grad_qkv_w.astype(bf16)
+    outputs = (residual + feeder.feed_out + biasd).astype(bf16).reshape(seqs, span, width)
     grad_w_qkv = (
         lax.all_to_all(grad_qkv_w.reshape(n_line, share, 3 * cols), LINE, split_axis=0, concat_axis=0, tiled=True)
         .reshape(n_line, share, 3, cols)
@@ -434,7 +788,7 @@
 
     biasq_part = spread(bias_qkv_part[:cols], n_line, line_at).reshape(-1)
     biasv_part = spread(bias_qkv_part[2 * cols :], n_line, line_at).reshape(-1)
-    bias_up_whole = spread(bias_up_part, n_dp, lax.axis_index("dp")).reshape(-1)
+    bias_up_whole = feeder.bias_spread(bias_up_part)
     parts = jnp.stack(
         [biasq_part, biasv_part, biaso_part, gain1_part, beta1_part, biasd_part, gain2_part, beta2_part]
     )

time: 1130 us -> 845 us (0.75)
  waiting for transfers between devices: 645 us -> 316 us
  blocking collectives: 142 us -> 0 us
  local copies, waits for them, and re-layouts: 58.5 us -> 129 us
  Pallas kernels: 63.5 us -> 127 us
  starting transfers between devices: 32.8 us -> 95.7 us
  matrix products: 115 us -> 58.9 us
  other arithmetic: 45.1 us -> 92.4 us
    reduce_scatter x4 -> x2, waiting for transfers between devices: 255 us -> 0.01 us  [feed(): lax.psum_scatter(grad.reshape(2 * self.block, self.width) if k == 0 else...]
    all_gather x5 -> x4, waiting for transfers between devices: 188 us -> 27.2 us  [the longest x1 27.2 us: tokens_there(): lax.all_gather(after(self.up_rows, tokens), 'seq', axis=0, tiled=False, a...]
    ppermute x16 -> x69, waiting for transfers between devices: 79.3 us -> 239 us  [the longest x67 231 us: swap(): lax.ppermute(value, axis, [(i, i ^ mask) for i in range(lax.axis_size(axi...]
    all_to_all x4 -> x0, blocking collectives: 94.2 us -> none  [the longest x1 29.9 us: on_device(): lax.all_to_all(grad_context.reshape(rows, n_line, cols).transpose(1, 0, 2...]
    reduce_scatter x1, waiting for transfers between devices: 87.8 us -> 0.01 us  [on_device(): lax.psum_scatter(grad_normed_part, LINE, scatter_dimension=0, tiled=True)]
    pallas_call x0 -> x7, Pallas kernels: none -> 62.6 us  [the longest x2 38.1 us: feed_forward(): call(feed_body, grid=(rows // tile,), in_specs=[part(width), part(width),...]
    dot_general x10 -> x7, matrix products: 115 us -> 58.9 us  [dot(): lax.dot_general(left, right, (dims, ((), ())), preferred_element_type=f32)]
    ppermute x16 -> x69, starting transfers between devices: 20 us -> 74.6 us  [the longest x67 71 us: swap(): lax.ppermute(value, axis, [(i, i ^ mask) for i in range(lax.axis_size(axi...]
  transfers between devices with their start and end apart: 29 -> 80, of which waited for: 18 -> 32; matrix products, arithmetic and copies ran while one was open for 14% -> 29% of each run, Pallas kernels for 4% -> 15%
where the time goes in v2:
time: 845 us; the launch traced here: 835 us
  waiting for transfers between devices  316 us (37%)
  local copies, waits for them, and re-layouts  129 us (15%)
  Pallas kernels  127 us (15%)
  starting transfers between devices  95.7 us (11%)
  other arithmetic  92.4 us (11%)
  matrix products  58.9 us (7%)
  between operations  16.1 us (2%)
    ppermute x67, waiting for transfers between devices, swap(): lax.ppermute(value, axis, [(i, i ^ mask) for i in range(lax.axis_size(axi...  231 us
    ppermute x67, starting transfers between devices, swap(): lax.ppermute(value, axis, [(i, i ^ mask) for i in range(lax.axis_size(axi...  71 us
    dot_general x7, matrix products, dot(): lax.dot_general(left, right, (dims, ((), ())), preferred_element_type=f32)  58.9 us
    unnamed x136, local copies, waits for them, and re-layouts  56.1 us
    pallas_call x2, Pallas kernels, feed_forward(): call(feed_body, grid=(rows // tile,), in_specs=[part(width), part(width),...  38.1 us
    all_to_all x1, waiting for transfers between devices, on_device(): lax.all_to_all(grad_context, LINE, split_axis=0, concat_axis=0, tiled=True)  27.9 us
    all_gather x1, waiting for transfers between devices, tokens_there(): lax.all_gather(after(self.up_rows, tokens), 'seq', axis=0, tiled=False, a...  27.2 us
    pallas_call x4, Pallas kernels, assemble(): call(body, in_specs=[pl.BlockSpec(memory_space=pltpu.SMEM)] + [pl.BlockSp...  21.8 us
  transfers between devices with their start and end apart: 80, of which 32 were waited for; matrix products, arithmetic and copies ran while one was open for 29% of the time, Pallas kernels for 15%

profile of v2, /device:TPU:0, one launch (start us, length us, event | category | flops | bytes accessed | tf_op | source)
XLA Modules:
  0.0 834.9 jit_solution(12580035871525993060)
XLA Ops:
  28.6 18.4 %collective-permute-done.1 = bf16[2,80,768]{2,1,0:T(8,128)(2,1)S(1)} collective-permute-done((bf16[2,80,768]{2,1,0:T(8,128)(2,1)S(1)}, bf16[2,80,768]{2,1,0:T(8,128)(2,1)S(1)}, u32[]{:S(2)}, u32[]{:S(2)}) %collective-permute-start.1) | collective-permute-done | bytes 245792 | tf_op jit(solution)/shard_map/ppermute | solution.py:48
  49.9 9.4 %collective-permute-done.2 = bf16[2,80,768]{2,1,0:T(8,128)(2,1)S(1)} collective-permute-done((bf16[2,80,768]{2,1,0:T(8,128)(2,1)S(1)}, bf16[2,80,768]{2,1,0:T(8,128)(2,1)S(1)}, u32[]{:S(2)}, u32[]{:S(2)}) %collective-permute-start.2) | collective-permute-done | bytes 245792 | tf_op jit(solution)/shard_map/ppermute | solution.py:48
  75.7 28.3 %collective-permute-done.10 = bf16[128,2048]{1,0:T(8,128)(2,1)S(1)} collective-permute-done((bf16[128,2048]{1,0:T(8,128)(2,1)S(1)}, bf16[128,2048]{1,0:T(8,128)(2,1)S(1)}, u32[]{:S(2)}, u32[]{:S(2)}) %collective-permute-start.10) | collective-permute-done | bytes 524320 | tf_op jit(solution)/shard_map/ppermute | solution.py:48
  110.8 10.0 %collective-permute-done.15.refs_4_ = bf16[2,2,80,768]{3,2,1,0:T(8,128)(2,1)} collective-permute-done((bf16[2,2,80,768]{3,2,1,0:T(8,128)(2,1)}, bf16[2,2,80,768]{3,2,1,0:T(8,128)(2,1)}, u32[]{:S(2)}, u32[]{:S(2)}) %collective-permute-start.15) | collective-permute-done | bytes 491552 | tf_op jit(solution)/shard_map/ppermute | solution.py:48
  128.0 16.2 %collective-permute-done.17 = bf16[4,64,2048]{2,1,0:T(8,128)(2,1)} collective-permute-done((bf16[4,64,2048]{2,1,0:T(8,128)(2,1)}, bf16[4,64,2048]{2,1,0:T(8,128)(2,1)}, u32[]{:S(2)}, u32[]{:S(2)}) %collective-permute-start.17) | collective-permute-done | bytes 1048608 | tf_op jit(solution)/shard_map/ppermute | solution.py:48
  186.1 16.1 %shard_map.272 = (bf16[2048,2048]{1,0:T(8,128)(2,1)}, bf16[2048,768]{1,0:T(8,128)(2,1)}) custom-call(bf16[2048,2048]{1,0:T(8,128)(2,1)} %bitcast.347, f32[1,2048]{1,0:T(1,128)} %slice.391.gain_ref, f32[1,2048]{1,0:T(1,128)} %slice.393.beta_ref, bf16[2048,768]{1,0:T(8,128)(2,1)} %bitcast.349, f32[1,768]{1,0:T(1,128)} %fusion.40.bias_ref), custom_call_target="tpu_custom_call" | custom-call | flops 6442450 | bytes 23068 | tf_op jit(solution)/shard_map/pallas_call | solution.py:457
  202.1 13.1 %shard_map.273 = (bf16[8,2,128,256]{3,2,1,0:T(8,128)(2,1)}, f32[2,1024,2]{2,1,0:T(8,128)}) custom-call(f32[1,2]{1,0:T(1,128)} %multiply_exponential_fusion.refs_0_, f32[2,1024,1]{2,1,0:T(8,128)} %copy.177.refs_1_, f32[2,1,1024]{2,1,0:T(1,128)} %bitcast.433, bf16[8,2,128,768]{3,2,1,0:T(8,128)(2,1)} %bitcast.356), custom_call_target="tpu_custom_call" | custom-call | flops 2147483 | bytes 4194 | tf_op jit(solution)/shard_map/pallas_call | solution.py:570
  239.2 9.6 %collective-permute-done.22 = bf16[256,2048]{1,0:T(8,128)(2,1)S(1)} collective-permute-done((bf16[256,2048]{1,0:T(8,128)(2,1)}, bf16[256,2048]{1,0:T(8,128)(2,1)S(1)}, u32[]{:S(2)}, u32[]{:S(2)}) %collective-permute-start.22) | collective-permute-done | bytes 1048608 | tf_op jit(solution)/shard_map/ppermute | solution.py:48
  285.8 27.2 %all-gather.15.cloned.1.call-done = bf16[8,2,64,1024]{3,2,0,1:T(8,128)(2,1)} async-done(((bf16[4,2,64,1024]{3,2,0,1:T(8,128)(2,1)}), bf16[8,2,64,1024]{3,2,0,1:T(8,128)(2,1)}) %all-gather.15.cloned.1.call-update) | async-done | bytes 2097168 | tf_op jit(solution)/shard_map/all_gather | solution.py:186
  335.0 13.1 %collective-permute-done.32 = bf16[256,2048]{1,0:T(8,128)(2,1)} collective-permute-done((bf16[256,2048]{1,0:T(8,128)(2,1)}, bf16[256,2048]{1,0:T(8,128)(2,1)}, u32[]{:S(2)}, u32[]{:S(2)}) %collective-permute-start.32) | collective-permute-done | bytes 1048608 | tf_op jit(solution)/shard_map/ppermute | solution.py:48
  365.6 19.1 %shard_map.277 = (bf16[1024,1024]{1,0:T(8,128)(2,1)}, bf16[1024,1024]{1,0:T(8,128)(2,1)}, bf16[1024,2048]{1,0:T(8,128)(2,1)}) custom-call(bf16[1024,2048]{1,0:T(8,128)(2,1)} %get-tuple-element.248.x_ref, bf16[1024,2048]{1,0:T(8,128)(2,1)} %get-tuple-element.256.dy_ref, bf16[2048,1024]{1,0:T(8,128)(2,1)} %bitcast.344, bf16[1024,2048]{1,0:T(8,128)(2,1)} %bitcast.341, ...), custom_call_target="tpu_custom_call" | custom-call | flops 12884901 | bytes 25165 | tf_op jit(solution)/shard_map/pallas_call | solution.py:660
  417.0 19.1 %shard_map.278 = (bf16[1024,1024]{1,0:T(8,128)(2,1)}, bf16[1024,1024]{1,0:T(8,128)(2,1)}, bf16[1024,2048]{1,0:T(8,128)(2,1)}) custom-call(bf16[1024,2048]{1,0:T(8,128)(2,1)} %copy-done.19, bf16[1024,2048]{1,0:T(8,128)(2,1)} %get-tuple-element.252.dy_ref, bf16[2048,1024]{1,0:T(8,128)(2,1)} %bitcast.345, bf16[1024,2048]{1,0:T(8,128)(2,1)} %bitcast.342, ...), custom_call_target="tpu_custom_call" | custom-call | flops 12884901 | bytes 25165 | tf_op jit(solution)/shard_map/pallas_call | solution.py:660
  451.9 11.6 %convolution_convert_fusion.2 = bf16[1024,2048]{1,0:T(8,128)(2,1)S(1)} fusion(bf16[2048,1024]{1,0:T(8,128)(2,1)S(1)} %pad_maximum_fusion.1, bf16[2048,2048]{1,0:T(8,128)(2,1)} %get-tuple-element.251), kind=kOutput, calls=%fused_computation.16 | convolution fusion | flops 8592031744 | bytes 16777216 | tf_op jit(solution)/shard_map/dot_general | solution.py:18
  470.1 10.6 %convolution_convert_fusion.1 = bf16[2048,2048]{1,0:T(8,128)(2,1)S(1)} fusion(bf16[2048,1024]{1,0:T(8,128)(2,1)} %copy-done.20, bf16[1024,2048]{1,0:T(8,128)(2,1)S(1)} %bitcast.343), kind=kOutput, calls=%fused_computation.4 | convolution fusion | flops 8594128896 | bytes 16777216 | tf_op jit(solution)/shard_map/dot_general | solution.py:18
  483.4 12.2 %convolution_convert_fusion.3 = bf16[2048,1024]{1,0:T(8,128)(2,1)S(1)} fusion(bf16[2048,2048]{1,0:T(8,128)(2,1)} %get-tuple-element.243, bf16[2048,1024]{1,0:T(8,128)(2,1)S(1)} %pad_maximum_fusion.2), kind=kOutput, calls=%fused_computation.17 | convolution fusion | flops 8592031744 | bytes 16777216 | tf_op jit(solution)/shard_map/dot_general | solution.py:18
  503.2 20.7 %collective-permute-done.46 = bf16[256,2048]{1,0:T(8,128)(2,1)S(1)} collective-permute-done((bf16[256,2048]{1,0:T(8,128)(2,1)S(1)}, bf16[256,2048]{1,0:T(8,128)(2,1)S(1)}, u32[]{:S(2)}, u32[]{:S(2)}) %collective-permute-start.46) | collective-permute-done | bytes 1048608 | tf_op jit(solution)/shard_map/ppermute | solution.py:48
  574.8 27.9 %all-to-all-done.1 = bf16[8,256,256]{2,1,0:T(8,128)(2,1)} async-done(((bf16[8,256,256]{2,1,0:T(8,128)(2,1)}), bf16[8,256,256]{2,1,0:T(8,128)(2,1)}, u32[]{:S(2)}, u32[]{:S(2)}) %all-to-all-start.1) | async-done | bytes 1048608 | tf_op jit(solution)/shard_map/all_to_all | solution.py:761
  602.7 17.8 %shard_map.279 = bf16[8,2,128,768]{3,2,1,0:T(8,128)(2,1)} custom-call(f32[1,2]{1,0:T(1,128)} %multiply_exponential_fusion.refs_0_, f32[2,1024,1]{2,1,0:T(8,128)} %copy.177.refs_1_, f32[2,1,1024]{2,1,0:T(1,128)} %bitcast.434, bf16[8,2,128,768]{3,2,1,0:T(8,128)(2,1)} %bitcast.357, bf16[8,2,128,256]{3,2,1,0:T(8,128)(2,1)} %bitcast.102.refs_4_, ...), custom_call_target="tpu_custom_call" | custom-call | flops 5368709 | bytes 7340 | tf_op jit(solution)/shard_map/pallas_call | solution.py:592
  620.5 17.1 %shard_map.280 = (bf16[2048,2048]{1,0:T(8,128)(2,1)}, f32[1,2048]{1,0:T(1,128)}, f32[1,2048]{1,0:T(1,128)}) custom-call(bf16[2048,768]{1,0:T(8,128)(2,1)} %bitcast.351, bf16[2048,768]{1,0:T(8,128)(2,1)} %bitcast.350, bf16[2048,2048]{1,0:T(8,128)(2,1)} %bitcast.348), custom_call_target="tpu_custom_call" | custom-call | flops 6442450 | bytes 23068 | tf_op jit(solution)/shard_map/pallas_call | solution.py:627
  665.2 13.2 %collective-permute-done.56 = bf16[4,64,2048]{2,1,0:T(8,128)(2,1)S(1)} collective-permute-done((bf16[4,64,2048]{2,1,0:T(8,128)(2,1)S(1)}, bf16[4,64,2048]{2,1,0:T(8,128)(2,1)S(1)}, u32[]{:S(2)}, u32[]{:S(2)}) %collective-permute-start.56) | collective-permute-done | bytes 1048608 | tf_op jit(solution)/shard_map/ppermute | solution.py:48
  734.2 12.2 %all-to-all-done.3 = f32[32,1,768]{2,1,0:T(1,128)S(1)} async-done(((f32[32,1,768]{2,1,0:T(1,128)}), f32[32,1,768]{2,1,0:T(1,128)S(1)}, u32[]{:S(2)}, u32[]{:S(2)}) %all-to-all-start.3) | async-done | bytes 98336 | tf_op jit(solution)/shard_map/all_to_all | solution.py:798
  756.5 22.6 %collective-permute-done.52 = bf16[256,2048]{1,0:T(8,128)(2,1)} collective-permute-done((bf16[256,2048]{1,0:T(8,128)(2,1)}, bf16[256,2048]{1,0:T(8,128)(2,1)}, u32[]{:S(2)}, u32[]{:S(2)}) %collective-permute-start.52) | collective-permute-done | bytes 1048608 | tf_op jit(solution)/shard_map/ppermute | solution.py:48
  786.6 12.7 %collective-permute-done.68.other_ref = bf16[4,64,1024]{2,1,0:T(8,128)(2,1)} collective-permute-done((bf16[4,64,1024]{2,1,0:T(8,128)(2,1)}, bf16[4,64,1024]{2,1,0:T(8,128)(2,1)}, u32[]{:S(2)}, u32[]{:S(2)}) %collective-permute-start.68) | collective-permute-done | bytes 524320 | tf_op jit(solution)/shard_map/ppermute | solution.py:48
  802.0 11.7 %collective-permute-done.64 = bf16[64,2048]{1,0:T(8,128)(2,1)S(1)} collective-permute-done((bf16[64,2048]{1,0:T(8,128)(2,1)}, bf16[64,2048]{1,0:T(8,128)(2,1)S(1)}, u32[]{:S(2)}, u32[]{:S(2)}) %collective-permute-start.64) | collective-permute-done | bytes 262176 | tf_op jit(solution)/shard_map/ppermute | solution.py:48
  (499 shorter events, 429.2 us)
Async XLA Ops:
  7.2 103.6 %all-gather.11.cloned.1.call-start = ((), (), s32[]{:S(2)}) async-start(), calls=%async_computation.11 | async-start | bytes 1310720 | tf_op jit(solution)/shard_map/all_gather | solution.py:147
  7.9 174.7 %all-gather.9.cloned.1.call-start = ((), (), s32[]{:S(2)}) async-start(), calls=%async_computation.10 | async-start | bytes 9437184 | tf_op jit(solution)/shard_map/all_gather | solution.py:150
  14.5 54.0 %collective-permute-start.5 = (bf16[256,2048]{1,0:T(8,128)(2,1)S(1)}, bf16[256,2048]{1,0:T(8,128)(2,1)}, u32[]{:S(2)}, u32[]{:S(2)}) collective-permute-start(bf16[256,2048]{1,0:T(8,128)(2,1)S(1)} %bitcast.361), channel_id=1, source_target_pairs={{0,16},{8,24},{16,0},{24,8},{1,17},{9,25},{17,1},{25,9},{2,18},{10... | collective-permute-start | bytes 3145736 | tf_op jit(solution)/shard_map/ppermute | solution.py:48
  17.0 52.3 %collective-permute-start.4 = (bf16[256,2048]{1,0:T(8,128)(2,1)S(1)}, bf16[256,2048]{1,0:T(8,128)(2,1)}, u32[]{:S(2)}, u32[]{:S(2)}) collective-permute-start(bf16[256,2048]{1,0:T(8,128)(2,1)S(1)} %bitcast.362), channel_id=1, source_target_pairs={{0,8},{8,0},{16,24},{24,16},{1,9},{9,1},{17,25},{25,17},{2,10},{10... | collective-permute-start | bytes 3145736 | tf_op jit(solution)/shard_map/ppermute | solution.py:48
  25.5 42.9 %collective-permute-start.6 = (bf16[4,64,1024]{2,1,0:T(8,128)(2,1)S(1)}, bf16[4,64,1024]{2,1,0:T(8,128)(2,1)S(1)}, u32[]{:S(2)}, u32[]{:S(2)}) collective-permute-start(bf16[4,64,1024]{2,1,0:T(8,128)(2,1)S(1)} %bitcast.409), channel_id=1, source_target_pairs={{0,2},{2,0},{4,6},{6,4},{1,3},{3,1},{5,7},{7,5},{8,10},{10,8},{12,... | collective-permute-start | bytes 1572872 | tf_op jit(solution)/shard_map/ppermute | solution.py:48
  69.3 189.6 %all-gather.13.cloned.1.call-start = ((), (), s32[]{:S(2)}) async-start(), calls=%async_computation.12 | async-start | bytes 3145728 | tf_op jit(solution)/shard_map/all_gather | solution.py:185
  168.6 62.3 %collective-permute-start.23 = (bf16[4,4,64,2048]{3,2,1,0:T(8,128)(2,1)}, bf16[4,4,64,2048]{3,2,1,0:T(8,128)(2,1)}, u32[]{:S(2)}, u32[]{:S(2)}) collective-permute-start(bf16[4,4,64,2048]{3,2,1,0:T(8,128)(2,1)} %pad_maximum_fusion.refs_0_), channel_id=1, source_target_pairs={{0,1},{1,0},{2,3},{3,2},{4,5},{5,4},{6,7},{7,6},{8,9},{9,8},{10,11... | collective-permute-start | bytes 12582920 | tf_op jit(solution)/shard_map/ppermute | solution.py:48
  221.1 92.0 %all-gather.15.cloned.1.call-start = ((), (), s32[]{:S(2)}) async-start(), calls=%async_computation.13 | async-start | bytes 3145728 | tf_op jit(solution)/shard_map/all_gather | solution.py:186
  238.7 457.0 %reduce-scatter.6.cloned.1.call-start = ((), (), s32[]{:S(2)}) async-start(), calls=%async_computation.8 | async-start | bytes 3145728 | tf_op jit(solution)/shard_map/reduce_scatter | solution.py:273
  317.6 42.7 %collective-permute-start.30 = (bf16[2,4,2,64,1024]{4,3,2,1,0:T(8,128)(2,1)S(1)}, bf16[2,4,2,64,1024]{4,3,2,1,0:T(8,128)(2,1)}, u32[]{:S(2)}, u32[]{:S(2)}) collective-permute-start(bf16[2,4,2,64,1024]{4,3,2,1,0:T(8,128)(2,1)S(1)} %bitcast.372), channel_id=1, source_target_pairs={{0,1},{1,0},{2,3},{3,2},{4,5},{5,4},{6,7},{7,6},{8,9},{9,8},{10,11... | collective-permute-start | bytes 6291464 | tf_op jit(solution)/shard_map/ppermute | solution.py:48
  348.1 43.1 %collective-permute-start.34 = (bf16[256,2048]{1,0:T(8,128)(2,1)}, bf16[256,2048]{1,0:T(8,128)(2,1)}, u32[]{:S(2)}, u32[]{:S(2)}) collective-permute-start(bf16[256,2048]{1,0:T(8,128)(2,1)} %collective-permute-done.32), channel_id=1, source_target_pairs={{0,16},{8,24},{16,0},{24,8},{1,17},{9,25},{17,1},{25,9},{2,18},{10... | collective-permute-start | bytes 3145736 | tf_op jit(solution)/shard_map/ppermute | solution.py:48
  349.6 44.2 %collective-permute-start.33 = (bf16[256,2048]{1,0:T(8,128)(2,1)}, bf16[256,2048]{1,0:T(8,128)(2,1)}, u32[]{:S(2)}, u32[]{:S(2)}) collective-permute-start(bf16[256,2048]{1,0:T(8,128)(2,1)} %collective-permute-done.32), channel_id=1, source_target_pairs={{0,8},{8,0},{16,24},{24,16},{1,9},{9,1},{17,25},{25,17},{2,10},{10... | collective-permute-start | bytes 3145736 | tf_op jit(solution)/shard_map/ppermute | solution.py:48
  500.6 42.2 %collective-permute-start.45 = (bf16[1,256,2048]{2,1,0:T(8,128)(2,1)}, bf16[1,256,2048]{2,1,0:T(8,128)(2,1)}, u32[]{:S(2)}, u32[]{:S(2)}) collective-permute-start(bf16[1,256,2048]{2,1,0:T(8,128)(2,1)} %get-tuple-element.195), channel_id=1, source_target_pairs={{0,16},{8,24},{16,0},{24,8},{1,17},{9,25},{17,1},{25,9},{2,18},{10... | collective-permute-start | bytes 3145736 | tf_op jit(solution)/shard_map/ppermute | solution.py:48
  530.1 252.4 %reduce-scatter.8.cloned.1.call-start = ((), (), s32[]{:S(2)}) async-start(), calls=%async_computation.9 | async-start | bytes 3145728 | tf_op jit(solution)/shard_map/reduce_scatter | solution.py:273
  556.1 64.4 %collective-permute-start.51 = (bf16[2,256,2048]{2,1,0:T(8,128)(2,1)}, bf16[2,256,2048]{2,1,0:T(8,128)(2,1)}, u32[]{:S(2)}, u32[]{:S(2)}) collective-permute-start(bf16[2,256,2048]{2,1,0:T(8,128)(2,1)} %pad_maximum_fusion.4), channel_id=1, source_target_pairs={{0,16},{8,24},{16,0},{24,8},{1,17},{9,25},{17,1},{25,9},{2,18},{10... | collective-permute-start | bytes 6291464 | tf_op jit(solution)/shard_map/ppermute | solution.py:48
  558.9 61.6 %collective-permute-start.50 = (bf16[2,256,2048]{2,1,0:T(8,128)(2,1)}, bf16[2,256,2048]{2,1,0:T(8,128)(2,1)}, u32[]{:S(2)}, u32[]{:S(2)}) collective-permute-start(bf16[2,256,2048]{2,1,0:T(8,128)(2,1)} %pad_maximum_fusion.3), channel_id=1, source_target_pairs={{0,8},{8,0},{16,24},{24,16},{1,9},{9,1},{17,25},{25,17},{2,10},{10... | collective-permute-start | bytes 6291464 | tf_op jit(solution)/shard_map/ppermute | solution.py:48
  560.3 42.4 %all-to-all-start.1 = ((bf16[8,256,256]{2,1,0:T(8,128)(2,1)}), bf16[8,256,256]{2,1,0:T(8,128)(2,1)}, u32[]{:S(2)}, u32[]{:S(2)}) async-start(bf16[8,256,256]{2,1,0:T(8,128)(2,1)} %bitcast.379), calls=%async_computation.1 | async-start | bytes 2097152 | tf_op jit(solution)/shard_map/all_to_all | solution.py:761
  564.6 257.8 %reduce-scatter.4.cloned.1.call-start = ((), (), s32[]{:S(2)}) async-start(), calls=%async_computation.7 | async-start | bytes 9437184 | tf_op jit(solution)/shard_map/reduce_scatter | solution.py:768
  573.6 46.9 %collective-permute-start.54 = (bf16[2,64,2048]{2,1,0:T(8,128)(2,1)}, bf16[2,64,2048]{2,1,0:T(8,128)(2,1)}, u32[]{:S(2)}, u32[]{:S(2)}) collective-permute-start(bf16[2,64,2048]{2,1,0:T(8,128)(2,1)} %get-tuple-element.177), channel_id=1, source_target_pairs={{0,8},{8,0},{16,24},{24,16},{1,9},{9,1},{17,25},{25,17},{2,10},{10... | collective-permute-start | bytes 1572872 | tf_op jit(solution)/shard_map/ppermute | solution.py:48
  574.1 46.4 %collective-permute-start.55 = (bf16[2,64,2048]{2,1,0:T(8,128)(2,1)}, bf16[2,64,2048]{2,1,0:T(8,128)(2,1)}, u32[]{:S(2)}, u32[]{:S(2)}) collective-permute-start(bf16[2,64,2048]{2,1,0:T(8,128)(2,1)} %get-tuple-element.178), channel_id=1, source_target_pairs={{0,16},{8,24},{16,0},{24,8},{1,17},{9,25},{17,1},{25,9},{2,18},{10... | collective-permute-start | bytes 1572872 | tf_op jit(solution)/shard_map/ppermute | solution.py:48
  723.2 55.9 %collective-permute-start.52 = (bf16[256,2048]{1,0:T(8,128)(2,1)}, bf16[256,2048]{1,0:T(8,128)(2,1)}, u32[]{:S(2)}, u32[]{:S(2)}) collective-permute-start(bf16[256,2048]{1,0:T(8,128)(2,1)} %fusion.16), channel_id=1, source_target_pairs={{0,2},{2,0},{4,6},{6,4},{1,3},{3,1},{5,7},{7,5},{8,10},{10,8},{12,... | collective-permute-start | bytes 3145736 | tf_op jit(solution)/shard_map/ppermute | solution.py:48
  725.8 73.5 %collective-permute-start.68 = (bf16[4,64,1024]{2,1,0:T(8,128)(2,1)}, bf16[4,64,1024]{2,1,0:T(8,128)(2,1)}, u32[]{:S(2)}, u32[]{:S(2)}) collective-permute-start(bf16[4,64,1024]{2,1,0:T(8,128)(2,1)} %get-tuple-element.197), channel_id=1, source_target_pairs={{0,2},{2,0},{4,6},{6,4},{1,3},{3,1},{5,7},{7,5},{8,10},{10,8},{12,... | collective-permute-start | bytes 1572872 | tf_op jit(solution)/shard_map/ppermute | solution.py:48
  746.3 68.2 %all-to-all-start.2 = ((bf16[8,64,768]{2,1,0:T(8,128)(2,1)}), bf16[8,64,768]{2,1,0:T(8,128)(2,1)}, u32[]{:S(2)}, u32[]{:S(2)}) async-start(bf16[8,64,768]{2,1,0:T(8,128)(2,1)} %bitcast.385), calls=%async_computation.3 | async-start | bytes 1572864 | tf_op jit(solution)/shard_map/all_to_all | solution.py:779
  753.7 60.0 %collective-permute-start.64 = (bf16[64,2048]{1,0:T(8,128)(2,1)}, bf16[64,2048]{1,0:T(8,128)(2,1)S(1)}, u32[]{:S(2)}, u32[]{:S(2)}) collective-permute-start(bf16[64,2048]{1,0:T(8,128)(2,1)} %fusion.25), channel_id=1, source_target_pairs={{0,2},{2,0},{4,6},{6,4},{1,3},{3,1},{5,7},{7,5},{8,10},{10,8},{12,... | collective-permute-start | bytes 786440 | tf_op jit(solution)/shard_map/ppermute | solution.py:48
  (109 other events, 1845.4 us)
Sparse Core Ops, SparseCore 0:
  9.6 43.6 all-gather.10
  69.4 79.8 all-gather.8
  182.8 73.6 all-gather.12
  257.9 55.0 all-gather.14
  530.2 76.3 reduce-scatter.5
  608.8 54.2 reduce-scatter.7
  665.3 137.1 reduce-scatter.3

commit v3 on v2

--- a/solution.py
+++ b/solution.py
@@ -160,10 +160,6 @@
         self.up_rows = jnp.stack(
             [pick(columns, self.dp)] + [swap(after(pick(columns, self.dp ^ k), one), "dp", k) for k in (1, 2, 3)]
         )
-        self.out_mine = out_line
-        self.out_one, self.out_two = [swap(after(out_line, top, low), "dp", k) for k in (1, 2)]
-        line = after(line, self.up_rows, self.out_one, self.out_two)
-
         copies = []
         for k in range(4):
             for z in range(4):
@@ -174,6 +170,11 @@
         parts = [block, one, two, top, low]
         shape = (4, 4, 2, share, block.shape[3])
         qkv_own = assemble(shape, parts, copies, [self.dp, self.seq, self.core]).reshape(self.width, -1)
+        self.out_mine = out_line
+        self.out_one, self.out_two = [swap(after(out_line, self.up_rows, qkv_own), "dp", k) for k in (1, 2)]
+        self.dy_near = swap(after(dy, self.up_rows, qkv_own), "seq", 1)
+        line = after(line, self.out_one, self.out_two, self.dy_near)
+
         small = [block[:, :, share], one[:, :, share], two[:, :, share]]
         small.append(jnp.concatenate([top[:, :, share], low[:, :, share]], axis=0))
         small = unxor(unxor(unxor(jnp.stack(small), 0, self.dp), 1, self.seq), 2, self.core).reshape(32, -1)
@@ -181,22 +182,30 @@
         return line, qkv_own, small, ids
 
     def tokens_there(self, tokens):
-        self.dy_near = swap(after(self.dy, tokens), "seq", 1)
-        down = lax.all_gather(after(self.w_down, tokens), "seq", axis=0, tiled=False, axis_index_groups=FAR)
-        up = lax.all_gather(after(self.up_rows, tokens), "seq", axis=0, tiled=False, axis_index_groups=FAR)
-        self.gathered = (up, down)
-
-    def out_start(self, qkv, context):
-        top, low = swap(self.out_two[:2], "dp", 1), swap(self.out_one[2:], "dp", 2)
-        parts = [self.out_mine, self.out_one, self.out_two, jnp.concatenate([top, low], axis=0)]
-        self.out_mine = jnp.stack(parts)
-        self.dy_one, self.dy_two = [swap(after(self.dy_near, context), "dp", k) for k in (1, 2)]
-        return after(context, top, low)
+        self.down_line = lax.all_gather(
+            after(self.w_down, tokens), "seq", axis=0, tiled=False, axis_index_groups=FAR
+        )
+
+    def before_scores(self, qkv):
+        top = swap(after(self.out_two[:2], qkv), "dp", 1)
+        low = swap(after(self.out_one[2:], qkv), "dp", 2)
+        self.out_mine = [self.out_mine, self.out_one, self.out_two, jnp.concatenate([top, low], axis=0)]
+        self.dy_one, self.dy_two = [swap(after(self.dy_near, qkv), "dp", k) for k in (1, 2)]
+        return after(qkv, self.down_line, top, low, self.dy_one, self.dy_two)
+
+    def out_start(self, context):
+        self.out_mine = after(jnp.stack(self.out_mine), context)
+        half = self.dy.shape[0] // 2
+        self.dy_top = swap(after(self.dy_two[:half], context), "dp", 1)
+        self.dy_low = swap(after(self.dy_one[half:], context), "dp", 2)
+        return context
 
     def out(self, context):
         mine = self.out_mine
         other = swap(mine, "fsdp", 1)
-        context = after(context, self.dy_one, self.dy_two, self.gathered[1])
+        up = lax.all_gather(after(self.up_rows, context), "seq", axis=0, tiled=False, axis_index_groups=FAR)
+        self.gathered = (up, self.down_line)
+        context = after(context, self.dy_top, self.dy_low)
         copies = [
             (f, (k, z), lambda s, f=f, k=k, z=z: (s[0] ^ k, z, s[1] ^ f))
             for f in range(2)
@@ -210,18 +219,16 @@
 
     def gather(self, normed):
         half = normed.shape[0] // 2
-        near, dy_one, dy_two = self.dy_near, self.dy_one, self.dy_two
-        dy_top, dy_low = swap(dy_two[:half], "dp", 1), swap(dy_one[half:], "dp", 2)
-        dy_second = jnp.concatenate([near, dy_one, dy_two, dy_top, dy_low], axis=0)
-        normed = after(normed, dy_top, dy_low)
+        parts = [self.dy_near, self.dy_one, self.dy_two, self.dy_top, self.dy_low]
+        dy_second = jnp.concatenate(parts, axis=0)
         other = swap(normed, "seq", 1)
         one, two = swap(normed, "dp", 1), swap(normed, "dp", 2)
-        halves = lax.optimization_barrier((two[:half], one[half:]))
+        halves = lax.optimization_barrier((two[:half], one[half:], other))
         top, low = swap(halves[0], "dp", 1), swap(halves[1], "dp", 2)
         up, down = [after(part, *halves) for part in self.gathered]
         up_other, down_other = swap(up, "fsdp", 1), swap(down, "fsdp", 1)
         first = jnp.concatenate([normed, one, two, top, low], axis=0)
-        other_one, other_two = [swap(after(other, top, low), "dp", k) for k in (1, 2)]
+        other_one, other_two = [swap(after(other, one, two), "dp", k) for k in (1, 2)]
         other_top, other_low = swap(other_two[:half], "dp", 1), swap(other_one[half:], "dp", 2)
         second = jnp.concatenate([other, other_one, other_two, other_top, other_low], axis=0)
         copies = [(f, (far,), lambda s, far=far, f=f: (far, s[0] ^ f)) for far in range(2) for f in range(2)]
@@ -253,36 +260,31 @@
         act, gh, gn = feed_forward(after(groups[1], *own_one), dys[1], up, down, bias)
         own_two = scatter_two(own_parts, own_one)
         parts = jnp.split(after(gn, *own_two), 4)
-        mid = scatter_mid(parts, scatter_one(parts))
+        one = scatter_one(parts)
+        acts, ghs = jnp.concatenate([own_act, act], axis=0), jnp.concatenate([own_gh, gh], axis=0)
+        grad_down = dot(acts, jnp.concatenate(dys, axis=0), ((0,), (0,))).astype(bf16)
+        mid = scatter_mid(parts, [after(part, grad_down) for part in one])
         two = scatter_send(mid)
-        self.acts = after(jnp.concatenate([own_act, act], axis=0), *mid)
-        ghs = after(jnp.concatenate([own_gh, gh], axis=0), *mid)
-        grad_down = dot(self.acts, jnp.concatenate(dys, axis=0), ((0,), (0,))).astype(bf16)
-        fed = dot(after(self.acts, grad_down), down, ((1,), (0,))).astype(bf16)
-        self.fed = [fed.reshape(2, 4, -1, self.width)[:, k] for k in range(4)]
+        grad_up = dot(jnp.concatenate(groups, axis=0), after(ghs, *mid), ((0,), (0,))).astype(bf16)
+        fed = dot(after(acts, *mid), down, ((1,), (0,))).astype(bf16)
+        fed, raw = lax.optimization_barrier((fed, grad_up))
+        other = after(scatter_sum(parts, two).astype(bf16), fed, raw)
         whole = grad_down.reshape(2, 2, self.block, self.width)
         theirs = swap(pick(whole, 1 - self.core, 1), "fsdp", 1)
-        grad_down = (pick(whole, self.core, 1).astype(f32) + after(theirs, fed).astype(f32)).astype(bf16)
-        ghs = after(ghs, grad_down)
-        grad_up = dot(jnp.concatenate(groups, axis=0), ghs, ((0,), (0,))).astype(bf16)
-        whole = grad_up.reshape(4, 2, 2, 2, self.share, -1)
+        grad_down = (pick(whole, self.core, 1).astype(f32) + theirs.astype(f32)).astype(bf16)
+        whole = raw.reshape(4, 2, 2, 2, self.share, -1)
         theirs = swap(pick(whole, 1 - self.core, 3), "fsdp", 1)
         grad_up = (pick(whole, self.core, 3).astype(f32) + theirs.astype(f32)).astype(bf16)
         grad_up = grad_up.transpose(1, 0, 2, 3, 4)
-        self.grad_down, rows = [
-            lax.psum_scatter(
-                grad.reshape(2 * self.block, self.width) if k == 0 else grad.reshape(self.width // 2, -1),
-                "seq",
-                scatter_dimension=0,
-                tiled=True,
-                axis_index_groups=FAR,
-            )
-            for k, grad in enumerate((grad_down, grad_up))
+        grad_down = grad_down.reshape(2 * self.block, self.width)
+        owned = [
+            lax.psum_scatter(grad, "seq", scatter_dimension=0, tiled=True, axis_index_groups=FAR)
+            for grad in (grad_down, grad_up.reshape(self.width // 2, -1))
         ]
-        self.grad_down = self.grad_down.astype(f32)
-        self.up_rows = rows.reshape(4, 2, self.share, -1)
-        other = scatter_sum(parts, two).astype(bf16)
+        self.grad_down = owned[0]
+        self.up_rows = owned[1].reshape(4, 2, self.share, -1)
         grad = scatter_sum(own_parts, own_two) + swap(other, "seq", 1).astype(f32)
+        self.fed = [fed.reshape(2, 4, -1, self.width)[:, k] for k in range(4)]
         self.fed_one = scatter_one([after(part, other) for part in self.fed])
         self.grad_up = grad_up
         return after(grad, grad_down), ghs
@@ -291,8 +293,7 @@
         return after(grad_context, self.grad_up, *self.fed_one)
 
     def before_attention(self, got, sent, grad_out_w):
-        fed_one = [after(part, sent) for part in self.fed_one]
-        self.fed_two = scatter_two(self.fed, fed_one)
+        self.fed_two = scatter_two(self.fed, [after(part, sent) for part in self.fed_one])
         whole = grad_out_w.reshape(4, 4, 2, self.share, self.width)
         theirs = swap(pick(whole, 1 - self.core, 2), "fsdp", 1)
         whole = (pick(whole, self.core, 2).astype(f32) + theirs.astype(f32)).astype(bf16)
@@ -301,24 +302,27 @@
 
     def before_norm(self, grad_qkv):
         own, other = scatter_sum(self.fed, self.fed_two)
-        self.feed_out = own + swap(other.astype(bf16), "seq", 1).astype(f32)
-        self.out_one = scatter_one(self.out_parts)
-        return after(grad_qkv, *self.fed_two, *self.out_one)
+        other = swap(other.astype(bf16), "seq", 1)
+        self.feed_out = own + other.astype(f32)
+        self.out_two = scatter_two(self.out_parts, scatter_one(self.out_parts))
+        return after(grad_qkv, other, *self.out_two)
 
     def last(self, normed, grad_qkv):
+        out_parts, out_two = self.out_parts, self.out_two
         grad = dot(normed, grad_qkv, ((0,), (0,))).astype(bf16)
-        out_two = scatter_two(self.out_parts, self.out_one)
         parts = [pick(grad.reshape(4, -1, grad.shape[1]), self.dp ^ k) for k in range(4)]
-        parts[3] = after(parts[3], *out_two)
-        one = scatter_one(parts)
-        line = scatter_sum(self.out_parts, out_two).reshape(2, 2, self.share, self.width)
+        two = scatter_two(parts, scatter_one(parts))
+        line = scatter_sum(out_parts, out_two).reshape(2, 2, self.share, self.width)
         away = pick(line, 1 - self.far)
         away = away + hop(away.astype(bf16), ((0, 1), (3, 2))).astype(f32)
-        line = pick(line, self.far) + hop(away.astype(bf16), ((1, 2), (2, 1))).astype(f32)
-        grad_out = pick(line, self.near) + swap(pick(line, 1 - self.near).astype(bf16), "seq", 1).astype(f32)
-        two = scatter_two(parts, one)
-        grad_up = self.up_back_end(after(self.up_rows, *one))
-        return scatter_sum(parts, two), grad_out, grad_up, self.grad_down
+        self.line = pick(line, self.far)
+        self.across = hop(away.astype(bf16), ((1, 2), (2, 1)))
+        grad_up = self.up_back_end(after(self.up_rows, *two))
+        return scatter_sum(parts, two), grad_up, self.grad_down
+
+    def out_end(self, home):
+        line = self.line + after(self.across, home).astype(f32)
+        return pick(line, self.near) + swap(pick(line, 1 - self.near).astype(bf16), "seq", 1).astype(f32)
 
     def up_back_end(self, rows):
         parts = [pick(rows, self.dp)] + [swap(pick(rows, self.dp ^ k), "dp", k) for k in (1, 2, 3)]
@@ -361,7 +365,10 @@
     def tokens_there(self, tokens):
         pass
 
-    def out_start(self, qkv, context):
+    def before_scores(self, qkv):
+        return qkv
+
+    def out_start(self, context):
         return context
 
     def out(self, context):
@@ -418,7 +425,10 @@
     def last(self, normed, grad_qkv):
         grad = dot(normed, grad_qkv, ((0,), (0,))).astype(bf16)
         grad = lax.psum_scatter(grad, "dp", scatter_dimension=0, tiled=True)
-        return grad, self.grad_out, self.grad_up, self.grad_down
+        return grad, self.grad_up, self.grad_down
+
+    def out_end(self, home):
+        return self.grad_out
 
 
 BLOCK = 256
@@ -727,11 +737,12 @@
     bias_row = jnp.concatenate([biasq_own, jnp.zeros_like(biasq_own), biasv_own], axis=1)
     normed_one, qkv = norm_project(tokens_line, gain1, beta1, qkv_own, bias_row)
     qkv = qkv.reshape(n_line, seqs, span, 3 * cols)
+    qkv = feeder.before_scores(qkv)
     numbers = (line_at * heads + jnp.arange(heads)).astype(f32)
     slopes = jnp.exp2(-8.0 * (numbers + 1.0) / (n_line * heads))[None]
     context_own, stats = attend(slopes, ids, qkv, score_scale)
     context_own = context_own.reshape(n_line, rows, cols)
-    context_own = feeder.out_start(qkv, context_own)
+    context_own = feeder.out_start(context_own)
     context = lax.all_to_all(context_own, LINE, split_axis=0, concat_axis=0, tiled=True)
     out_full, context = feeder.out(context)
     context = context.transpose(1, 0, 2).reshape(rows, width)
@@ -743,21 +754,15 @@
 
     normed_groups, grad_out_groups, up_own, down_own = feeder.gather(normed_two)
     grad_normed_two, grad_hidden = feeder.feed(normed_groups, grad_out_groups, up_own, down_own, up_bias)
-    bias_up_part = jnp.sum(grad_hidden.astype(f32), axis=0)
-
     grad_out_f = grad_out.astype(f32)
     grad_residual = grad_out_f + norm_back(grad_normed_two, gain2, normal_two, scale_two)
-    gain2_part = jnp.sum(grad_normed_two * normal_two, axis=0)
-    beta2_part = jnp.sum(grad_normed_two, axis=0)
-    biasd_part = jnp.sum(grad_out_f, axis=0)
-    biaso_part = jnp.sum(grad_residual, axis=0)
 
     grad_branch = grad_residual.astype(bf16)
     grad_context = dot(grad_branch, out_full, ((1,), (1,))).astype(bf16)
     grad_context = grad_context.reshape(rows, n_line, cols).transpose(1, 0, 2)
     grad_context = feeder.before_exchange(grad_context)
-    grad_branch = after(grad_branch, grad_context)
     sent = grad_context
+    grad_branch = after(grad_branch, sent)
     grad_context = lax.all_to_all(grad_context, LINE, split_axis=0, concat_axis=0, tiled=True)
     grad_out_w = dot(context, grad_branch, ((0,), (0,))).astype(bf16)
     grad_context = feeder.before_attention(grad_context, sent, grad_out_w).reshape(n_line, seqs, span, cols)
@@ -770,14 +775,28 @@
     ).astype(f32)
     normal_one, scale_one = norm_parts(tokens)
     grad_inputs = grad_residual + norm_back(grad_normed_one, gain1, normal_one, scale_one)
-    bias_qkv_part = jnp.sum(grad_qkv.astype(f32), axis=0)
-
-    grad_qkv_w, grad_w_out, grad_w_up, grad_w_down = feeder.last(normed_one, grad_qkv)
+    grad_qkv_w, grad_w_up, grad_w_down = feeder.last(normed_one, grad_qkv)
     grad_qkv_w = grad_qkv_w.astype(bf16)
+
+    grad_normed_late, grad_residual_late, grad_hidden_late, grad_qkv_late, gain1_part, beta1_part, grad_w_down = (
+        lax.optimization_barrier(
+            (grad_normed_two, grad_residual, grad_hidden, grad_qkv, gain1_part, beta1_part, grad_w_down, grad_qkv_w)
+        )[:7]
+    )
+    grad_w_down = grad_w_down.astype(f32)
+    gain2_part = jnp.sum(grad_normed_late * normal_two, axis=0)
+    beta2_part = jnp.sum(grad_normed_late, axis=0)
+    biasd_part = jnp.sum(grad_out_f, axis=0)
+    biaso_part = jnp.sum(grad_residual_late, axis=0)
+    bias_up_part = jnp.sum(grad_hidden_late.astype(f32), axis=0)
+    bias_qkv_part = jnp.sum(grad_qkv_late.astype(f32), axis=0)
     outputs = (residual + feeder.feed_out + biasd).astype(bf16).reshape(seqs, span, width)
+    qkv_home = lax.all_to_all(
+        grad_qkv_w.reshape(n_line, share, 3 * cols), LINE, split_axis=0, concat_axis=0, tiled=True
+    )
+    grad_w_out = feeder.out_end(qkv_home)
     grad_w_qkv = (
-        lax.all_to_all(grad_qkv_w.reshape(n_line, share, 3 * cols), LINE, split_axis=0, concat_axis=0, tiled=True)
-        .reshape(n_line, share, 3, cols)
+        qkv_home.reshape(n_line, share, 3, cols)
         .transpose(1, 2, 0, 3)
         .reshape(share, 3 * width)
         .astype(f32)
@@ -795,7 +814,7 @@
     n_all = n_dp * n_line
     parts = parts.reshape(8, n_all, share).transpose(1, 0, 2).reshape(n_all, 8 * share)
     parts = jnp.concatenate([parts, bias_up_whole.reshape(n_all, -1)], axis=1)
-    parts = lax.all_to_all(parts, ALL, split_axis=0, concat_axis=0, tiled=True)
+    parts = lax.all_to_all(after(parts, qkv_home), ALL, split_axis=0, concat_axis=0, tiled=True)
     own = jnp.sum(parts, axis=0)
     vec = own[: 8 * share].reshape(8, share)
 

time: 845 us -> 838 us (level)
  waiting for transfers between devices: 316 us -> 304 us
    all_to_all x1, waiting for transfers between devices: 27.9 us -> 0.01 us  [on_device(): lax.all_to_all(grad_context, LINE, split_axis=0, concat_axis=0, tiled=True)]
    all_to_all x1, waiting for transfers between devices: 0.01 us -> 21 us  [on_device(): lax.all_to_all(grad_qkv_w.reshape(n_line, share, 3 * cols), LINE, split_a...]
    all_to_all x1, waiting for transfers between devices: 12.2 us -> 0.01 us  [on_device(): lax.all_to_all(after(parts, qkv_home), ALL, split_axis=0, concat_axis=0,...]
    unnamed x136 -> x142, local copies, waits for them, and re-layouts: 56.1 us -> 52.9 us
  transfers between devices with their start and end apart: 80 -> 80, of which waited for: 32 -> 30; matrix products, arithmetic and copies ran while one was open for 29% -> 33% of each run, Pallas kernels for 15% -> 14%
where the time goes in v3:
time: 838 us; the launch traced here: 828 us
  waiting for transfers between devices  304 us (36%)
  local copies, waits for them, and re-layouts  134 us (16%)
  Pallas kernels  128 us (15%)
  other arithmetic  95.4 us (11%)
  starting transfers between devices  90.9 us (11%)
  matrix products  60 us (7%)
  between operations  15.9 us (2%)
    ppermute x67, waiting for transfers between devices, swap(): lax.ppermute(value, axis, [(i, i ^ mask) for i in range(lax.axis_size(axi...  227 us
    ppermute x67, starting transfers between devices, swap(): lax.ppermute(value, axis, [(i, i ^ mask) for i in range(lax.axis_size(axi...  68.3 us
    dot_general x7, matrix products, dot(): lax.dot_general(left, right, (dims, ((), ())), preferred_element_type=f32)  60 us
    unnamed x142, local copies, waits for them, and re-layouts  52.9 us
    pallas_call x2, Pallas kernels, feed_forward(): call(feed_body, grid=(rows // tile,), in_specs=[part(width), part(width),...  38.7 us
    all_gather x1, waiting for transfers between devices, out(): lax.all_gather(after(self.up_rows, context), 'seq', axis=0, tiled=False,...  25.2 us
    pallas_call x4, Pallas kernels, assemble(): call(body, in_specs=[pl.BlockSpec(memory_space=pltpu.SMEM)] + [pl.BlockSp...  22.1 us
    all_to_all x1, waiting for transfers between devices, on_device(): lax.all_to_all(grad_qkv_w.reshape(n_line, share, 3 * cols), LINE, split_a...  21 us
  transfers between devices with their start and end apart: 80, of which 30 were waited for; matrix products, arithmetic and copies ran while one was open for 33% of the time, Pallas kernels for 14%

profile of v3, /device:TPU:0, one launch (start us, length us, event | category | flops | bytes accessed | tf_op | source)
XLA Modules:
  0.0 827.8 jit_solution(9148123270329453210)
XLA Ops:
  28.6 18.4 %collective-permute-done.1 = bf16[2,80,768]{2,1,0:T(8,128)(2,1)S(1)} collective-permute-done((bf16[2,80,768]{2,1,0:T(8,128)(2,1)S(1)}, bf16[2,80,768]{2,1,0:T(8,128)(2,1)S(1)}, u32[]{:S(2)}, u32[]{:S(2)}) %collective-permute-start.1) | collective-permute-done | bytes 245792 | tf_op jit(solution)/shard_map/ppermute | solution.py:48
  49.9 9.4 %collective-permute-done.2 = bf16[2,80,768]{2,1,0:T(8,128)(2,1)S(1)} collective-permute-done((bf16[2,80,768]{2,1,0:T(8,128)(2,1)S(1)}, bf16[2,80,768]{2,1,0:T(8,128)(2,1)S(1)}, u32[]{:S(2)}, u32[]{:S(2)}) %collective-permute-start.2) | collective-permute-done | bytes 245792 | tf_op jit(solution)/shard_map/ppermute | solution.py:48
  59.3 8.9 %collective-permute-done.3 = bf16[2,80,768]{2,1,0:T(8,128)(2,1)S(1)} collective-permute-done((bf16[2,80,768]{2,1,0:T(8,128)(2,1)S(1)}, bf16[2,80,768]{2,1,0:T(8,128)(2,1)S(1)}, u32[]{:S(2)}, u32[]{:S(2)}) %collective-permute-start.3) | collective-permute-done | bytes 245792 | tf_op jit(solution)/shard_map/ppermute | solution.py:48
  79.2 24.8 %collective-permute-done.10 = bf16[128,2048]{1,0:T(8,128)(2,1)} collective-permute-done((bf16[128,2048]{1,0:T(8,128)(2,1)}, bf16[128,2048]{1,0:T(8,128)(2,1)}, u32[]{:S(2)}, u32[]{:S(2)}) %collective-permute-start.10) | collective-permute-done | bytes 524320 | tf_op jit(solution)/shard_map/ppermute | solution.py:48
  118.2 11.3 %collective-permute-done.11 = bf16[2,64,1024]{2,1,0:T(8,128)(2,1)S(1)} collective-permute-done((bf16[2,64,1024]{2,1,0:T(8,128)(2,1)}, bf16[2,64,1024]{2,1,0:T(8,128)(2,1)S(1)}, u32[]{:S(2)}, u32[]{:S(2)}) %collective-permute-start.11) | collective-permute-done | bytes 262176 | tf_op jit(solution)/shard_map/ppermute | solution.py:48
  148.1 15.3 %collective-permute-done.17 = bf16[4,64,2048]{2,1,0:T(8,128)(2,1)S(1)} collective-permute-done((bf16[4,64,2048]{2,1,0:T(8,128)(2,1)}, bf16[4,64,2048]{2,1,0:T(8,128)(2,1)S(1)}, u32[]{:S(2)}, u32[]{:S(2)}) %collective-permute-start.17) | collective-permute-done | bytes 1048608 | tf_op jit(solution)/shard_map/ppermute | solution.py:48
  177.1 16.0 %shard_map.272 = (bf16[2048,2048]{1,0:T(8,128)(2,1)}, bf16[2048,768]{1,0:T(8,128)(2,1)}) custom-call(bf16[2048,2048]{1,0:T(8,128)(2,1)} %bitcast.350, f32[1,2048]{1,0:T(1,128)} %slice.397.gain_ref, f32[1,2048]{1,0:T(1,128)} %slice.399.beta_ref, bf16[2048,768]{1,0:T(8,128)(2,1)} %bitcast.352, f32[1,768]{1,0:T(1,128)} %fusion.40.bias_ref), custom_call_target="tpu_custom_call" | custom-call | flops 6442450 | bytes 23068 | tf_op jit(solution)/shard_map/pallas_call | solution.py:467
  199.4 8.9 %collective-permute-done.19 = bf16[2,64,2048]{2,1,0:T(8,128)(2,1)} collective-permute-done((bf16[2,64,2048]{2,1,0:T(8,128)(2,1)}, bf16[2,64,2048]{2,1,0:T(8,128)(2,1)}, u32[]{:S(2)}, u32[]{:S(2)}) %collective-permute-start.19) | collective-permute-done | bytes 524320 | tf_op jit(solution)/shard_map/ppermute | solution.py:48
  213.9 15.6 %collective-permute-done.22 = bf16[256,2048]{1,0:T(8,128)(2,1)S(1)} collective-permute-done((bf16[256,2048]{1,0:T(8,128)(2,1)}, bf16[256,2048]{1,0:T(8,128)(2,1)S(1)}, u32[]{:S(2)}, u32[]{:S(2)}) %collective-permute-start.22) | collective-permute-done | bytes 1048608 | tf_op jit(solution)/shard_map/ppermute | solution.py:48
  229.6 13.9 %shard_map.273 = (bf16[8,2,128,256]{3,2,1,0:T(8,128)(2,1)}, f32[2,1024,2]{2,1,0:T(8,128)}) custom-call(f32[1,2]{1,0:T(1,128)} %multiply_exponential_fusion.refs_0_, f32[2,1024,1]{2,1,0:T(8,128)} %copy.167.refs_1_, f32[2,1,1024]{2,1,0:T(1,128)} %bitcast.440, bf16[8,2,128,768]{3,2,1,0:T(8,128)(2,1)} %bitcast.359), custom_call_target="tpu_custom_call" | custom-call | flops 2147483 | bytes 4194 | tf_op jit(solution)/shard_map/pallas_call | solution.py:580
  260.8 15.9 %all-to-all-done = bf16[8,256,256]{1,2,0:T(8,128)(2,1)S(1)} async-done(((bf16[8,256,256]{1,2,0:T(8,128)(2,1)}), bf16[8,256,256]{1,2,0:T(8,128)(2,1)S(1)}, u32[]{:S(2)}, u32[]{:S(2)}) %all-to-all-start) | async-done | bytes 1048608 | tf_op jit(solution)/shard_map/all_to_all | solution.py:746
  306.3 25.2 %all-gather.15.cloned.1.call-done = bf16[8,2,64,1024]{3,2,0,1:T(8,128)(2,1)} async-done(((bf16[4,2,64,1024]{3,2,0,1:T(8,128)(2,1)}), bf16[8,2,64,1024]{3,2,0,1:T(8,128)(2,1)}) %all-gather.15.cloned.1.call-update) | async-done | bytes 2097168 | tf_op jit(solution)/shard_map/all_gather | solution.py:206
  374.7 19.6 %shard_map.277 = (bf16[1024,1024]{1,0:T(8,128)(2,1)}, bf16[1024,1024]{1,0:T(8,128)(2,1)}, bf16[1024,2048]{1,0:T(8,128)(2,1)}) custom-call(bf16[1024,2048]{1,0:T(8,128)(2,1)} %get-tuple-element.279.x_ref, bf16[1024,2048]{1,0:T(8,128)(2,1)} %get-tuple-element.287.dy_ref, bf16[2048,1024]{1,0:T(8,128)(2,1)} %bitcast.347, bf16[1024,2048]{1,0:T(8,128)(2,1)} %bitcast.344, ...), custom_call_target="tpu_custom_call" | custom-call | flops 12884901 | bytes 25165 | tf_op jit(solution)/shard_map/pallas_call | solution.py:670
  427.5 19.1 %shard_map.278 = (bf16[1024,1024]{1,0:T(8,128)(2,1)}, bf16[1024,1024]{1,0:T(8,128)(2,1)}, bf16[1024,2048]{1,0:T(8,128)(2,1)}) custom-call(bf16[1024,2048]{1,0:T(8,128)(2,1)} %get-tuple-element.143.x_ref, bf16[1024,2048]{1,0:T(8,128)(2,1)} %get-tuple-element.283.dy_ref, bf16[2048,1024]{1,0:T(8,128)(2,1)} %bitcast.348, bf16[1024,2048]{1,0:T(8,128)(2,1)} %bitcast.345, ...), custom_call_target="tpu_custom_call" | custom-call | flops 12884901 | bytes 25165 | tf_op jit(solution)/shard_map/pallas_call | solution.py:670
  452.0 11.9 %convolution_convert_fusion.2 = bf16[1024,2048]{1,0:T(8,128)(2,1)S(1)} fusion(bf16[2048,1024]{1,0:T(8,128)(2,1)S(1)} %copy-done.33, bf16[2048,2048]{1,0:T(8,128)(2,1)} %get-tuple-element.282), kind=kOutput, calls=%fused_computation.14 | convolution fusion | flops 8592031744 | bytes 16777216 | tf_op jit(solution)/shard_map/dot_general | solution.py:18
  471.1 10.7 %convolution_convert_fusion.1 = bf16[2048,2048]{1,0:T(8,128)(2,1)S(1)} fusion(bf16[2048,1024]{1,0:T(8,128)(2,1)} %constant_dynamic-update-slice_fusion.20, bf16[1024,2048]{1,0:T(8,128)(2,1)S(1)} %bitcast.346), kind=kOutput, calls=%fused_computation.4 | convolution fusion | flops 8594128896 | bytes 16777216 | tf_op jit(solution)/shard_map/dot_general | solution.py:18
  481.9 16.1 %convolution_convert_fusion.3 = bf16[2048,1024]{1,0:T(8,128)(2,1)} fusion(bf16[2048,2048]{1,0:T(8,128)(2,1)} %get-tuple-element.274, bf16[2048,1024]{1,0:T(8,128)(2,1)S(1)} %constant_dynamic-update-slice_fusion.42), kind=kOutput, calls=%fused_computation.15 | convolution fusion | flops 8592031744 | bytes 16777216 | tf_op jit(solution)/shard_map/dot_general | solution.py:18
  509.8 29.7 %collective-permute-done.46 = bf16[256,2048]{1,0:T(8,128)(2,1)} collective-permute-done((bf16[256,2048]{1,0:T(8,128)(2,1)}, bf16[256,2048]{1,0:T(8,128)(2,1)}, u32[]{:S(2)}, u32[]{:S(2)}) %collective-permute-start.46) | collective-permute-done | bytes 1048608 | tf_op jit(solution)/shard_map/ppermute | solution.py:48
  578.9 35.4 %collective-permute-done.51 = bf16[2,256,2048]{2,1,0:T(8,128)(2,1)} collective-permute-done((bf16[2,256,2048]{2,1,0:T(8,128)(2,1)}, bf16[2,256,2048]{2,1,0:T(8,128)(2,1)}, u32[]{:S(2)}, u32[]{:S(2)}) %collective-permute-start.51) | collective-permute-done | bytes 2097184 | tf_op jit(solution)/shard_map/ppermute | solution.py:48
  645.6 17.9 %shard_map.279 = bf16[8,2,128,768]{3,2,1,0:T(8,128)(2,1)} custom-call(f32[1,2]{1,0:T(1,128)} %multiply_exponential_fusion.refs_0_, f32[2,1024,1]{2,1,0:T(8,128)} %copy.167.refs_1_, f32[2,1,1024]{2,1,0:T(1,128)} %bitcast.441, bf16[8,2,128,768]{3,2,1,0:T(8,128)(2,1)} %bitcast.360, bf16[8,2,128,256]{3,2,1,0:T(8,128)(2,1)} %bitcast.103.refs_4_, ...), custom_call_target="tpu_custom_call" | custom-call | flops 5368709 | bytes 7340 | tf_op jit(solution)/shard_map/pallas_call | solution.py:602
  668.1 16.9 %shard_map.280 = (bf16[2048,2048]{1,0:T(8,128)(2,1)}, f32[1,2048]{1,0:T(1,128)}, f32[1,2048]{1,0:T(1,128)}) custom-call(bf16[2048,768]{1,0:T(8,128)(2,1)} %bitcast.354, bf16[2048,768]{1,0:T(8,128)(2,1)} %bitcast.353, bf16[2048,2048]{1,0:T(8,128)(2,1)} %bitcast.351), custom_call_target="tpu_custom_call" | custom-call | flops 6442450 | bytes 23068 | tf_op jit(solution)/shard_map/pallas_call | solution.py:637
  686.2 10.5 %convolution_convert_fusion.4 = bf16[2048,768]{1,0:T(8,128)(2,1)S(1)} fusion(bf16[2048,2048]{1,0:T(8,128)(2,1)} %get-tuple-element.166, bf16[2048,768]{1,0:T(8,128)(2,1)} %bitcast.355), kind=kOutput, calls=%fused_computation.16 | convolution fusion | flops 6444023808 | bytes 14680064 | tf_op jit(solution)/shard_map/dot_general | solution.py:18
  715.2 14.4 %collective-permute-done.62 = bf16[2,64,2048]{2,1,0:T(8,128)(2,1)} collective-permute-done((bf16[2,64,2048]{2,1,0:T(8,128)(2,1)}, bf16[2,64,2048]{2,1,0:T(8,128)(2,1)}, u32[]{:S(2)}, u32[]{:S(2)}) %collective-permute-start.62) | collective-permute-done | bytes 524320 | tf_op jit(solution)/shard_map/ppermute | solution.py:52
  771.6 21.0 %all-to-all-done.2 = bf16[8,64,768]{2,1,0:T(8,128)(2,1)} async-done(((bf16[8,64,768]{2,1,0:T(8,128)(2,1)}), bf16[8,64,768]{2,1,0:T(8,128)(2,1)}, u32[]{:S(2)}, u32[]{:S(2)}) %all-to-all-start.2) | async-done | bytes 786464 | tf_op jit(solution)/shard_map/all_to_all | solution.py:794
  (502 shorter events, 405.4 us)
Async XLA Ops:
  7.2 133.5 %all-gather.11.cloned.1.call-start = ((), (), s32[]{:S(2)}) async-start(), calls=%async_computation.11 | async-start | bytes 1310720 | tf_op jit(solution)/shard_map/all_gather | solution.py:147
  7.9 160.3 %all-gather.9.cloned.1.call-start = ((), (), s32[]{:S(2)}) async-start(), calls=%async_computation.10 | async-start | bytes 9437184 | tf_op jit(solution)/shard_map/all_gather | solution.py:150
  14.5 54.0 %collective-permute-start.5 = (bf16[256,2048]{1,0:T(8,128)(2,1)S(1)}, bf16[256,2048]{1,0:T(8,128)(2,1)}, u32[]{:S(2)}, u32[]{:S(2)}) collective-permute-start(bf16[256,2048]{1,0:T(8,128)(2,1)S(1)} %bitcast.364), channel_id=1, source_target_pairs={{0,16},{8,24},{16,0},{24,8},{1,17},{9,25},{17,1},{25,9},{2,18},{10... | collective-permute-start | bytes 3145736 | tf_op jit(solution)/shard_map/ppermute | solution.py:48
  17.0 52.3 %collective-permute-start.4 = (bf16[256,2048]{1,0:T(8,128)(2,1)S(1)}, bf16[256,2048]{1,0:T(8,128)(2,1)}, u32[]{:S(2)}, u32[]{:S(2)}) collective-permute-start(bf16[256,2048]{1,0:T(8,128)(2,1)S(1)} %bitcast.365), channel_id=1, source_target_pairs={{0,8},{8,0},{16,24},{24,16},{1,9},{9,1},{17,25},{25,17},{2,10},{10... | collective-permute-start | bytes 3145736 | tf_op jit(solution)/shard_map/ppermute | solution.py:48
  25.5 42.9 %collective-permute-start.6 = (bf16[4,64,1024]{2,1,0:T(8,128)(2,1)S(1)}, bf16[4,64,1024]{2,1,0:T(8,128)(2,1)S(1)}, u32[]{:S(2)}, u32[]{:S(2)}) collective-permute-start(bf16[4,64,1024]{2,1,0:T(8,128)(2,1)S(1)} %bitcast.414), channel_id=1, source_target_pairs={{0,2},{2,0},{4,6},{6,4},{1,3},{3,1},{5,7},{7,5},{8,10},{10,8},{12,... | collective-permute-start | bytes 1572872 | tf_op jit(solution)/shard_map/ppermute | solution.py:48
  69.3 160.3 %all-gather.13.cloned.1.call-start = ((), (), s32[]{:S(2)}) async-start(), calls=%async_computation.12 | async-start | bytes 3145728 | tf_op jit(solution)/shard_map/all_gather | solution.py:185
  250.1 81.4 %all-gather.15.cloned.1.call-start = ((), (), s32[]{:S(2)}) async-start(), calls=%async_computation.13 | async-start | bytes 3145728 | tf_op jit(solution)/shard_map/all_gather | solution.py:206
  276.8 459.5 %reduce-scatter.6.cloned.1.call-start = ((), (), s32[]{:S(2)}) async-start(), calls=%async_computation.8 | async-start | bytes 3145728 | tf_op jit(solution)/shard_map/reduce_scatter | solution.py:281
  293.6 46.4 %collective-permute-start.28 = (bf16[256,2048]{1,0:T(8,128)(2,1)}, bf16[256,2048]{1,0:T(8,128)(2,1)}, u32[]{:S(2)}, u32[]{:S(2)}) collective-permute-start(bf16[256,2048]{1,0:T(8,128)(2,1)} %get-tuple-element.196), channel_id=1, source_target_pairs={{0,2},{2,0},{4,6},{6,4},{1,3},{3,1},{5,7},{7,5},{8,10},{10,8},{12,... | collective-permute-start | bytes 3145736 | tf_op jit(solution)/shard_map/ppermute | solution.py:48
  293.6 40.0 %collective-permute-start.27 = (bf16[256,2048]{1,0:T(8,128)(2,1)}, bf16[256,2048]{1,0:T(8,128)(2,1)}, u32[]{:S(2)}, u32[]{:S(2)}) collective-permute-start(bf16[256,2048]{1,0:T(8,128)(2,1)} %get-tuple-element.196), channel_id=1, source_target_pairs={{0,16},{8,24},{16,0},{24,8},{1,17},{9,25},{17,1},{25,9},{2,18},{10... | collective-permute-start | bytes 3145736 | tf_op jit(solution)/shard_map/ppermute | solution.py:48
  295.1 40.0 %collective-permute-start.26 = (bf16[256,2048]{1,0:T(8,128)(2,1)}, bf16[256,2048]{1,0:T(8,128)(2,1)}, u32[]{:S(2)}, u32[]{:S(2)}) collective-permute-start(bf16[256,2048]{1,0:T(8,128)(2,1)} %get-tuple-element.196), channel_id=1, source_target_pairs={{0,8},{8,0},{16,24},{24,16},{1,9},{9,1},{17,25},{25,17},{2,10},{10... | collective-permute-start | bytes 3145736 | tf_op jit(solution)/shard_map/ppermute | solution.py:48
  350.7 51.0 %collective-permute-start.34 = (bf16[256,2048]{1,0:T(8,128)(2,1)}, bf16[256,2048]{1,0:T(8,128)(2,1)S(1)}, u32[]{:S(2)}, u32[]{:S(2)}) collective-permute-start(bf16[256,2048]{1,0:T(8,128)(2,1)} %collective-permute-done.28), channel_id=1, source_target_pairs={{0,16},{8,24},{16,0},{24,8},{1,17},{9,25},{17,1},{25,9},{2,18},{10... | collective-permute-start | bytes 3145736 | tf_op jit(solution)/shard_map/ppermute | solution.py:48
  362.3 40.2 %collective-permute-start.33 = (bf16[256,2048]{1,0:T(8,128)(2,1)}, bf16[256,2048]{1,0:T(8,128)(2,1)S(1)}, u32[]{:S(2)}, u32[]{:S(2)}) collective-permute-start(bf16[256,2048]{1,0:T(8,128)(2,1)} %collective-permute-done.28), channel_id=1, source_target_pairs={{0,8},{8,0},{16,24},{24,16},{1,9},{9,1},{17,25},{25,17},{2,10},{10... | collective-permute-start | bytes 3145736 | tf_op jit(solution)/shard_map/ppermute | solution.py:48
  502.3 37.2 %collective-permute-start.46 = (bf16[256,2048]{1,0:T(8,128)(2,1)}, bf16[256,2048]{1,0:T(8,128)(2,1)}, u32[]{:S(2)}, u32[]{:S(2)}) collective-permute-start(bf16[256,2048]{1,0:T(8,128)(2,1)} %add_convert_fusion), channel_id=1, source_target_pairs={{0,2},{2,0},{4,6},{6,4},{1,3},{3,1},{5,7},{7,5},{8,10},{10,8},{12,... | collective-permute-start | bytes 3145736 | tf_op jit(solution)/shard_map/ppermute | solution.py:48
  507.8 41.9 %collective-permute-start.45 = (bf16[1,256,2048]{2,1,0:T(8,128)(2,1)S(1)}, bf16[1,256,2048]{2,1,0:T(8,128)(2,1)S(1)}, u32[]{:S(2)}, u32[]{:S(2)}) collective-permute-start(bf16[1,256,2048]{2,1,0:T(8,128)(2,1)S(1)} %get-tuple-element.230), channel_id=1, source_target_pairs={{0,16},{8,24},{16,0},{24,8},{1,17},{9,25},{17,1},{25,9},{2,18},{10... | collective-permute-start | bytes 3145736 | tf_op jit(solution)/shard_map/ppermute | solution.py:48
  509.1 40.6 %collective-permute-start.49 = (bf16[1,256,2048]{2,1,0:T(8,128)(2,1)S(1)}, bf16[1,256,2048]{2,1,0:T(8,128)(2,1)S(1)}, u32[]{:S(2)}, u32[]{:S(2)}) collective-permute-start(bf16[1,256,2048]{2,1,0:T(8,128)(2,1)S(1)} %get-tuple-element.231), channel_id=1, source_target_pairs={{0,8},{8,0},{16,24},{24,16},{1,9},{9,1},{17,25},{25,17},{2,10},{10... | collective-permute-start | bytes 3145736 | tf_op jit(solution)/shard_map/ppermute | solution.py:48
  558.0 63.2 %collective-permute-start.53 = (bf16[4,4,64,2048]{3,2,1,0:T(8,128)(2,1)}, bf16[4,4,64,2048]{3,2,1,0:T(8,128)(2,1)}, u32[]{:S(2)}, u32[]{:S(2)}) collective-permute-start(bf16[4,4,64,2048]{3,2,1,0:T(8,128)(2,1)} %dynamic-slice_bitcast_fusion), channel_id=1, source_target_pairs={{0,1},{1,0},{2,3},{3,2},{4,5},{5,4},{6,7},{7,6},{8,9},{9,8},{10,11... | collective-permute-start | bytes 12582920 | tf_op jit(solution)/shard_map/ppermute | solution.py:48
  566.6 47.7 %collective-permute-start.51 = (bf16[2,256,2048]{2,1,0:T(8,128)(2,1)}, bf16[2,256,2048]{2,1,0:T(8,128)(2,1)}, u32[]{:S(2)}, u32[]{:S(2)}) collective-permute-start(bf16[2,256,2048]{2,1,0:T(8,128)(2,1)} %pad_maximum_fusion.2), channel_id=1, source_target_pairs={{0,16},{8,24},{16,0},{24,8},{1,17},{9,25},{17,1},{25,9},{2,18},{10... | collective-permute-start | bytes 6291464 | tf_op jit(solution)/shard_map/ppermute | solution.py:48
  569.8 47.4 %collective-permute-start.50 = (bf16[2,256,2048]{2,1,0:T(8,128)(2,1)}, bf16[2,256,2048]{2,1,0:T(8,128)(2,1)}, u32[]{:S(2)}, u32[]{:S(2)}) collective-permute-start(bf16[2,256,2048]{2,1,0:T(8,128)(2,1)} %pad_maximum_fusion.1), channel_id=1, source_target_pairs={{0,8},{8,0},{16,24},{24,16},{1,9},{9,1},{17,25},{25,17},{2,10},{10... | collective-permute-start | bytes 6291464 | tf_op jit(solution)/shard_map/ppermute | solution.py:48
  569.8 75.8 %all-to-all-start.1 = ((bf16[8,256,256]{2,1,0:T(8,128)(2,1)}), bf16[8,256,256]{2,1,0:T(8,128)(2,1)}, u32[]{:S(2)}, u32[]{:S(2)}) async-start(bf16[8,256,256]{2,1,0:T(8,128)(2,1)} %bitcast.384), calls=%async_computation.1 | async-start | bytes 2097152 | tf_op jit(solution)/shard_map/all_to_all | solution.py:766
  574.0 162.2 %reduce-scatter.8.cloned.1.call-start = ((), (), s32[]{:S(2)}) async-start(), calls=%async_computation.9 | async-start | bytes 3145728 | tf_op jit(solution)/shard_map/reduce_scatter | solution.py:281
  578.9 236.4 %reduce-scatter.4.cloned.1.call-start = ((), (), s32[]{:S(2)}) async-start(), calls=%async_computation.7 | async-start | bytes 9437184 | tf_op jit(solution)/shard_map/reduce_scatter | solution.py:773
  731.9 39.7 %collective-permute-start.63 = (bf16[2,64,2048]{2,1,0:T(8,128)(2,1)}, bf16[2,64,2048]{2,1,0:T(8,128)(2,1)}, u32[]{:S(2)}, u32[]{:S(2)}) collective-permute-start(bf16[2,64,2048]{2,1,0:T(8,128)(2,1)} %fusion.19), channel_id=1, source_target_pairs={{2,4},{4,2},{3,5},{5,3},{10,12},{12,10},{11,13},{13,11},{18,20},{2... | collective-permute-start | bytes 1572872 | tf_op jit(solution)/shard_map/ppermute | solution.py:52
  739.2 53.3 %all-to-all-start.2 = ((bf16[8,64,768]{2,1,0:T(8,128)(2,1)}), bf16[8,64,768]{2,1,0:T(8,128)(2,1)}, u32[]{:S(2)}, u32[]{:S(2)}) async-start(bf16[8,64,768]{2,1,0:T(8,128)(2,1)} %bitcast.389), calls=%async_computation.3 | async-start | bytes 1572864 | tf_op jit(solution)/shard_map/all_to_all | solution.py:794
  (111 other events, 1856.7 us)
Sparse Core Ops, SparseCore 0:
  9.6 43.6 all-gather.10
  69.4 79.4 all-gather.8
  168.4 56.9 all-gather.12
  276.9 54.5 all-gather.14
  506.2 55.1 reduce-scatter.5
  579.0 67.9 reduce-scatter.7
  685.1 129.4 reduce-scatter.3

commit v4 on v3

--- a/solution.py
+++ b/solution.py
@@ -223,9 +223,9 @@
         dy_second = jnp.concatenate(parts, axis=0)
         other = swap(normed, "seq", 1)
         one, two = swap(normed, "dp", 1), swap(normed, "dp", 2)
-        halves = lax.optimization_barrier((two[:half], one[half:], other))
+        halves = lax.optimization_barrier((two[:half], one[half:]))
         top, low = swap(halves[0], "dp", 1), swap(halves[1], "dp", 2)
-        up, down = [after(part, *halves) for part in self.gathered]
+        up, down = [after(part, top, low, other) for part in self.gathered]
         up_other, down_other = swap(up, "fsdp", 1), swap(down, "fsdp", 1)
         first = jnp.concatenate([normed, one, two, top, low], axis=0)
         other_one, other_two = [swap(after(other, one, two), "dp", k) for k in (1, 2)]

time: 838 us -> 836 us (level)
    all_gather x1, waiting for transfers between devices: 25.2 us -> 1.8 us  [out(): lax.all_gather(after(self.up_rows, context), 'seq', axis=0, tiled=False,...]
    ppermute x67, waiting for transfers between devices: 227 us -> 238 us  [swap(): lax.ppermute(value, axis, [(i, i ^ mask) for i in range(lax.axis_size(axi...]
    unnamed x142 -> x150, local copies, waits for them, and re-layouts: 52.9 us -> 58.7 us
where the time goes in v4:
time: 836 us; the launch traced here: 826 us
  waiting for transfers between devices  299 us (36%)
  local copies, waits for them, and re-layouts  139 us (17%)
  Pallas kernels  128 us (15%)
  other arithmetic  94.4 us (11%)
  starting transfers between devices  89.8 us (11%)
  matrix products  60 us (7%)
  between operations  15.9 us (2%)
    ppermute x67, waiting for transfers between devices, swap(): lax.ppermute(value, axis, [(i, i ^ mask) for i in range(lax.axis_size(axi...  238 us
    ppermute x67, starting transfers between devices, swap(): lax.ppermute(value, axis, [(i, i ^ mask) for i in range(lax.axis_size(axi...  67.7 us
    dot_general x7, matrix products, dot(): lax.dot_general(left, right, (dims, ((), ())), preferred_element_type=f32)  60 us
    unnamed x150, local copies, waits for them, and re-layouts  58.7 us
    pallas_call x2, Pallas kernels, feed_forward(): call(feed_body, grid=(rows // tile,), in_specs=[part(width), part(width),...  38.7 us
    pallas_call x4, Pallas kernels, assemble(): call(body, in_specs=[pl.BlockSpec(memory_space=pltpu.SMEM)] + [pl.BlockSp...  22 us
    all_to_all x1, waiting for transfers between devices, on_device(): lax.all_to_all(context_own, LINE, split_axis=0, concat_axis=0, tiled=True)  21.4 us
    all_to_all x1, waiting for transfers between devices, on_device(): lax.all_to_all(grad_qkv_w.reshape(n_line, share, 3 * cols), LINE, split_a...  21.2 us
  transfers between devices with their start and end apart: 80, of which 30 were waited for; matrix products, arithmetic and copies ran while one was open for 33% of the time, Pallas kernels for 14%

profile of v4, /device:TPU:0, one launch (start us, length us, event | category | flops | bytes accessed | tf_op | source)
XLA Modules:
  0.0 825.7 jit_solution(103965682346474847)
XLA Ops:
  28.6 18.4 %collective-permute-done.1 = bf16[2,80,768]{2,1,0:T(8,128)(2,1)S(1)} collective-permute-done((bf16[2,80,768]{2,1,0:T(8,128)(2,1)S(1)}, bf16[2,80,768]{2,1,0:T(8,128)(2,1)S(1)}, u32[]{:S(2)}, u32[]{:S(2)}) %collective-permute-start.1) | collective-permute-done | bytes 245792 | tf_op jit(solution)/shard_map/ppermute | solution.py:48
  49.9 9.4 %collective-permute-done.2 = bf16[2,80,768]{2,1,0:T(8,128)(2,1)S(1)} collective-permute-done((bf16[2,80,768]{2,1,0:T(8,128)(2,1)S(1)}, bf16[2,80,768]{2,1,0:T(8,128)(2,1)S(1)}, u32[]{:S(2)}, u32[]{:S(2)}) %collective-permute-start.2) | collective-permute-done | bytes 245792 | tf_op jit(solution)/shard_map/ppermute | solution.py:48
  59.3 8.9 %collective-permute-done.3 = bf16[2,80,768]{2,1,0:T(8,128)(2,1)S(1)} collective-permute-done((bf16[2,80,768]{2,1,0:T(8,128)(2,1)S(1)}, bf16[2,80,768]{2,1,0:T(8,128)(2,1)S(1)}, u32[]{:S(2)}, u32[]{:S(2)}) %collective-permute-start.3) | collective-permute-done | bytes 245792 | tf_op jit(solution)/shard_map/ppermute | solution.py:48
  79.2 24.8 %collective-permute-done.10 = bf16[128,2048]{1,0:T(8,128)(2,1)} collective-permute-done((bf16[128,2048]{1,0:T(8,128)(2,1)}, bf16[128,2048]{1,0:T(8,128)(2,1)}, u32[]{:S(2)}, u32[]{:S(2)}) %collective-permute-start.10) | collective-permute-done | bytes 524320 | tf_op jit(solution)/shard_map/ppermute | solution.py:48
  118.2 11.3 %collective-permute-done.11 = bf16[2,64,1024]{2,1,0:T(8,128)(2,1)S(1)} collective-permute-done((bf16[2,64,1024]{2,1,0:T(8,128)(2,1)}, bf16[2,64,1024]{2,1,0:T(8,128)(2,1)S(1)}, u32[]{:S(2)}, u32[]{:S(2)}) %collective-permute-start.11) | collective-permute-done | bytes 262176 | tf_op jit(solution)/shard_map/ppermute | solution.py:48
  148.1 15.3 %collective-permute-done.17 = bf16[4,64,2048]{2,1,0:T(8,128)(2,1)S(1)} collective-permute-done((bf16[4,64,2048]{2,1,0:T(8,128)(2,1)}, bf16[4,64,2048]{2,1,0:T(8,128)(2,1)S(1)}, u32[]{:S(2)}, u32[]{:S(2)}) %collective-permute-start.17) | collective-permute-done | bytes 1048608 | tf_op jit(solution)/shard_map/ppermute | solution.py:48
  175.1 16.1 %shard_map.272 = (bf16[2048,2048]{1,0:T(8,128)(2,1)}, bf16[2048,768]{1,0:T(8,128)(2,1)}) custom-call(bf16[2048,2048]{1,0:T(8,128)(2,1)} %bitcast.350, f32[1,2048]{1,0:T(1,128)} %slice.397.gain_ref, f32[1,2048]{1,0:T(1,128)} %slice.399.beta_ref, bf16[2048,768]{1,0:T(8,128)(2,1)} %bitcast.352, f32[1,768]{1,0:T(1,128)} %fusion.40.bias_ref), custom_call_target="tpu_custom_call" | custom-call | flops 6442450 | bytes 23068 | tf_op jit(solution)/shard_map/pallas_call | solution.py:467
  212.6 15.8 %collective-permute-done.22 = bf16[256,2048]{1,0:T(8,128)(2,1)S(1)} collective-permute-done((bf16[256,2048]{1,0:T(8,128)(2,1)}, bf16[256,2048]{1,0:T(8,128)(2,1)S(1)}, u32[]{:S(2)}, u32[]{:S(2)}) %collective-permute-start.22) | collective-permute-done | bytes 1048608 | tf_op jit(solution)/shard_map/ppermute | solution.py:48
  228.4 13.8 %shard_map.273 = (bf16[8,2,128,256]{3,2,1,0:T(8,128)(2,1)}, f32[2,1024,2]{2,1,0:T(8,128)}) custom-call(f32[1,2]{1,0:T(1,128)} %multiply_exponential_fusion.refs_0_, f32[2,1024,1]{2,1,0:T(8,128)} %copy.167.refs_1_, f32[2,1,1024]{2,1,0:T(1,128)} %bitcast.440, bf16[8,2,128,768]{3,2,1,0:T(8,128)(2,1)} %bitcast.359), custom_call_target="tpu_custom_call" | custom-call | flops 2147483 | bytes 4194 | tf_op jit(solution)/shard_map/pallas_call | solution.py:580
  253.3 21.4 %all-to-all-done = bf16[8,256,256]{1,2,0:T(8,128)(2,1)S(1)} async-done(((bf16[8,256,256]{1,2,0:T(8,128)(2,1)}), bf16[8,256,256]{1,2,0:T(8,128)(2,1)S(1)}, u32[]{:S(2)}, u32[]{:S(2)}) %all-to-all-start) | async-done | bytes 1048608 | tf_op jit(solution)/shard_map/all_to_all | solution.py:746
  304.0 13.3 %collective-permute-done.27 = bf16[256,2048]{1,0:T(8,128)(2,1)S(1)} collective-permute-done((bf16[256,2048]{1,0:T(8,128)(2,1)}, bf16[256,2048]{1,0:T(8,128)(2,1)S(1)}, u32[]{:S(2)}, u32[]{:S(2)}) %collective-permute-start.27) | collective-permute-done | bytes 1048608 | tf_op jit(solution)/shard_map/ppermute | solution.py:48
  332.6 12.5 %collective-permute-done.30 = bf16[256,2048]{1,0:T(8,128)(2,1)} collective-permute-done((bf16[256,2048]{1,0:T(8,128)(2,1)}, bf16[256,2048]{1,0:T(8,128)(2,1)}, u32[]{:S(2)}, u32[]{:S(2)}) %collective-permute-start.30) | collective-permute-done | bytes 1048608 | tf_op jit(solution)/shard_map/ppermute | solution.py:48
  372.4 19.6 %shard_map.277 = (bf16[1024,1024]{1,0:T(8,128)(2,1)}, bf16[1024,1024]{1,0:T(8,128)(2,1)}, bf16[1024,2048]{1,0:T(8,128)(2,1)}) custom-call(bf16[1024,2048]{1,0:T(8,128)(2,1)} %get-tuple-element.277.x_ref, bf16[1024,2048]{1,0:T(8,128)(2,1)} %get-tuple-element.285.dy_ref, bf16[2048,1024]{1,0:T(8,128)(2,1)} %bitcast.347, bf16[1024,2048]{1,0:T(8,128)(2,1)} %bitcast.344, ...), custom_call_target="tpu_custom_call" | custom-call | flops 12884901 | bytes 25165 | tf_op jit(solution)/shard_map/pallas_call | solution.py:670
  425.3 19.1 %shard_map.278 = (bf16[1024,1024]{1,0:T(8,128)(2,1)}, bf16[1024,1024]{1,0:T(8,128)(2,1)}, bf16[1024,2048]{1,0:T(8,128)(2,1)}) custom-call(bf16[1024,2048]{1,0:T(8,128)(2,1)} %get-tuple-element.141.x_ref, bf16[1024,2048]{1,0:T(8,128)(2,1)} %get-tuple-element.281.dy_ref, bf16[2048,1024]{1,0:T(8,128)(2,1)} %bitcast.348, bf16[1024,2048]{1,0:T(8,128)(2,1)} %bitcast.345, ...), custom_call_target="tpu_custom_call" | custom-call | flops 12884901 | bytes 25165 | tf_op jit(solution)/shard_map/pallas_call | solution.py:670
  449.9 11.9 %convolution_convert_fusion.2 = bf16[1024,2048]{1,0:T(8,128)(2,1)S(1)} fusion(bf16[2048,1024]{1,0:T(8,128)(2,1)S(1)} %copy-done.37, bf16[2048,2048]{1,0:T(8,128)(2,1)} %get-tuple-element.280), kind=kOutput, calls=%fused_computation.14 | convolution fusion | flops 8592031744 | bytes 16777216 | tf_op jit(solution)/shard_map/dot_general | solution.py:18
  469.0 10.7 %convolution_convert_fusion.1 = bf16[2048,2048]{1,0:T(8,128)(2,1)S(1)} fusion(bf16[2048,1024]{1,0:T(8,128)(2,1)} %constant_dynamic-update-slice_fusion.20, bf16[1024,2048]{1,0:T(8,128)(2,1)S(1)} %bitcast.346), kind=kOutput, calls=%fused_computation.4 | convolution fusion | flops 8594128896 | bytes 16777216 | tf_op jit(solution)/shard_map/dot_general | solution.py:18
  479.8 16.1 %convolution_convert_fusion.3 = bf16[2048,1024]{1,0:T(8,128)(2,1)} fusion(bf16[2048,2048]{1,0:T(8,128)(2,1)} %get-tuple-element.272, bf16[2048,1024]{1,0:T(8,128)(2,1)S(1)} %constant_dynamic-update-slice_fusion.42), kind=kOutput, calls=%fused_computation.15 | convolution fusion | flops 8592031744 | bytes 16777216 | tf_op jit(solution)/shard_map/dot_general | solution.py:18
  507.7 29.7 %collective-permute-done.46 = bf16[256,2048]{1,0:T(8,128)(2,1)} collective-permute-done((bf16[256,2048]{1,0:T(8,128)(2,1)}, bf16[256,2048]{1,0:T(8,128)(2,1)}, u32[]{:S(2)}, u32[]{:S(2)}) %collective-permute-start.46) | collective-permute-done | bytes 1048608 | tf_op jit(solution)/shard_map/ppermute | solution.py:48
  576.8 35.4 %collective-permute-done.51 = bf16[2,256,2048]{2,1,0:T(8,128)(2,1)} collective-permute-done((bf16[2,256,2048]{2,1,0:T(8,128)(2,1)}, bf16[2,256,2048]{2,1,0:T(8,128)(2,1)}, u32[]{:S(2)}, u32[]{:S(2)}) %collective-permute-start.51) | collective-permute-done | bytes 2097184 | tf_op jit(solution)/shard_map/ppermute | solution.py:48
  643.6 17.8 %shard_map.279 = bf16[8,2,128,768]{3,2,1,0:T(8,128)(2,1)} custom-call(f32[1,2]{1,0:T(1,128)} %multiply_exponential_fusion.refs_0_, f32[2,1024,1]{2,1,0:T(8,128)} %copy.167.refs_1_, f32[2,1,1024]{2,1,0:T(1,128)} %bitcast.441, bf16[8,2,128,768]{3,2,1,0:T(8,128)(2,1)} %bitcast.360, bf16[8,2,128,256]{3,2,1,0:T(8,128)(2,1)} %bitcast.103.refs_4_, ...), custom_call_target="tpu_custom_call" | custom-call | flops 5368709 | bytes 7340 | tf_op jit(solution)/shard_map/pallas_call | solution.py:602
  665.9 16.9 %shard_map.280 = (bf16[2048,2048]{1,0:T(8,128)(2,1)}, f32[1,2048]{1,0:T(1,128)}, f32[1,2048]{1,0:T(1,128)}) custom-call(bf16[2048,768]{1,0:T(8,128)(2,1)} %bitcast.354, bf16[2048,768]{1,0:T(8,128)(2,1)} %bitcast.353, bf16[2048,2048]{1,0:T(8,128)(2,1)} %bitcast.351), custom_call_target="tpu_custom_call" | custom-call | flops 6442450 | bytes 23068 | tf_op jit(solution)/shard_map/pallas_call | solution.py:637
  684.0 10.5 %convolution_convert_fusion.4 = bf16[2048,768]{1,0:T(8,128)(2,1)S(1)} fusion(bf16[2048,2048]{1,0:T(8,128)(2,1)} %get-tuple-element.164, bf16[2048,768]{1,0:T(8,128)(2,1)} %bitcast.355), kind=kOutput, calls=%fused_computation.16 | convolution fusion | flops 6444023808 | bytes 14680064 | tf_op jit(solution)/shard_map/dot_general | solution.py:18
  711.9 15.8 %collective-permute-done.62 = bf16[2,64,2048]{2,1,0:T(8,128)(2,1)} collective-permute-done((bf16[2,64,2048]{2,1,0:T(8,128)(2,1)}, bf16[2,64,2048]{2,1,0:T(8,128)(2,1)}, u32[]{:S(2)}, u32[]{:S(2)}) %collective-permute-start.62) | collective-permute-done | bytes 524320 | tf_op jit(solution)/shard_map/ppermute | solution.py:52
  769.2 21.2 %all-to-all-done.2 = bf16[8,64,768]{2,1,0:T(8,128)(2,1)} async-done(((bf16[8,64,768]{2,1,0:T(8,128)(2,1)}), bf16[8,64,768]{2,1,0:T(8,128)(2,1)}, u32[]{:S(2)}, u32[]{:S(2)}) %all-to-all-start.2) | async-done | bytes 786464 | tf_op jit(solution)/shard_map/all_to_all | solution.py:794
  (510 shorter events, 404.1 us)
Async XLA Ops:
  7.2 133.5 %all-gather.11.cloned.1.call-start = ((), (), s32[]{:S(2)}) async-start(), calls=%async_computation.11 | async-start | bytes 1310720 | tf_op jit(solution)/shard_map/all_gather | solution.py:147
  7.9 160.3 %all-gather.9.cloned.1.call-start = ((), (), s32[]{:S(2)}) async-start(), calls=%async_computation.10 | async-start | bytes 9437184 | tf_op jit(solution)/shard_map/all_gather | solution.py:150
  14.5 54.0 %collective-permute-start.5 = (bf16[256,2048]{1,0:T(8,128)(2,1)S(1)}, bf16[256,2048]{1,0:T(8,128)(2,1)}, u32[]{:S(2)}, u32[]{:S(2)}) collective-permute-start(bf16[256,2048]{1,0:T(8,128)(2,1)S(1)} %bitcast.364), channel_id=1, source_target_pairs={{0,16},{8,24},{16,0},{24,8},{1,17},{9,25},{17,1},{25,9},{2,18},{10... | collective-permute-start | bytes 3145736 | tf_op jit(solution)/shard_map/ppermute | solution.py:48
  17.0 52.3 %collective-permute-start.4 = (bf16[256,2048]{1,0:T(8,128)(2,1)S(1)}, bf16[256,2048]{1,0:T(8,128)(2,1)}, u32[]{:S(2)}, u32[]{:S(2)}) collective-permute-start(bf16[256,2048]{1,0:T(8,128)(2,1)S(1)} %bitcast.365), channel_id=1, source_target_pairs={{0,8},{8,0},{16,24},{24,16},{1,9},{9,1},{17,25},{25,17},{2,10},{10... | collective-permute-start | bytes 3145736 | tf_op jit(solution)/shard_map/ppermute | solution.py:48
  25.5 42.9 %collective-permute-start.6 = (bf16[4,64,1024]{2,1,0:T(8,128)(2,1)S(1)}, bf16[4,64,1024]{2,1,0:T(8,128)(2,1)S(1)}, u32[]{:S(2)}, u32[]{:S(2)}) collective-permute-start(bf16[4,64,1024]{2,1,0:T(8,128)(2,1)S(1)} %bitcast.414), channel_id=1, source_target_pairs={{0,2},{2,0},{4,6},{6,4},{1,3},{3,1},{5,7},{7,5},{8,10},{10,8},{12,... | collective-permute-start | bytes 1572872 | tf_op jit(solution)/shard_map/ppermute | solution.py:48
  69.3 159.1 %all-gather.13.cloned.1.call-start = ((), (), s32[]{:S(2)}) async-start(), calls=%async_computation.12 | async-start | bytes 3145728 | tf_op jit(solution)/shard_map/all_gather | solution.py:185
  248.1 82.4 %all-gather.15.cloned.1.call-start = ((), (), s32[]{:S(2)}) async-start(), calls=%async_computation.13 | async-start | bytes 3145728 | tf_op jit(solution)/shard_map/all_gather | solution.py:206
  275.8 458.5 %reduce-scatter.6.cloned.1.call-start = ((), (), s32[]{:S(2)}) async-start(), calls=%async_computation.8 | async-start | bytes 3145728 | tf_op jit(solution)/shard_map/reduce_scatter | solution.py:281
  299.1 46.0 %collective-permute-start.30 = (bf16[256,2048]{1,0:T(8,128)(2,1)}, bf16[256,2048]{1,0:T(8,128)(2,1)}, u32[]{:S(2)}, u32[]{:S(2)}) collective-permute-start(bf16[256,2048]{1,0:T(8,128)(2,1)} %get-tuple-element.194), channel_id=1, source_target_pairs={{0,2},{2,0},{4,6},{6,4},{1,3},{3,1},{5,7},{7,5},{8,10},{10,8},{12,... | collective-permute-start | bytes 3145736 | tf_op jit(solution)/shard_map/ppermute | solution.py:48
  353.5 45.2 %collective-permute-start.34 = (bf16[256,2048]{1,0:T(8,128)(2,1)}, bf16[256,2048]{1,0:T(8,128)(2,1)}, u32[]{:S(2)}, u32[]{:S(2)}) collective-permute-start(bf16[256,2048]{1,0:T(8,128)(2,1)} %collective-permute-done.30), channel_id=1, source_target_pairs={{0,16},{8,24},{16,0},{24,8},{1,17},{9,25},{17,1},{25,9},{2,18},{10... | collective-permute-start | bytes 3145736 | tf_op jit(solution)/shard_map/ppermute | solution.py:48
  354.0 47.3 %collective-permute-start.33 = (bf16[256,2048]{1,0:T(8,128)(2,1)}, bf16[256,2048]{1,0:T(8,128)(2,1)}, u32[]{:S(2)}, u32[]{:S(2)}) collective-permute-start(bf16[256,2048]{1,0:T(8,128)(2,1)} %collective-permute-done.30), channel_id=1, source_target_pairs={{0,8},{8,0},{16,24},{24,16},{1,9},{9,1},{17,25},{25,17},{2,10},{10... | collective-permute-start | bytes 3145736 | tf_op jit(solution)/shard_map/ppermute | solution.py:48
  463.4 36.8 %collective-permute-start.47 = (bf16[2,256,2048]{2,1,0:T(8,128)(2,1)}, bf16[2,256,2048]{2,1,0:T(8,128)(2,1)}, u32[]{:S(2)}, u32[]{:S(2)}) collective-permute-start(bf16[2,256,2048]{2,1,0:T(8,128)(2,1)} %dynamic-slice_bitcast_fusion.1), channel_id=1, source_target_pairs={{0,1},{1,0},{2,3},{3,2},{4,5},{5,4},{6,7},{7,6},{8,9},{9,8},{10,11... | collective-permute-start | bytes 6291464 | tf_op jit(solution)/shard_map/ppermute | solution.py:48
  500.2 37.2 %collective-permute-start.46 = (bf16[256,2048]{1,0:T(8,128)(2,1)}, bf16[256,2048]{1,0:T(8,128)(2,1)}, u32[]{:S(2)}, u32[]{:S(2)}) collective-permute-start(bf16[256,2048]{1,0:T(8,128)(2,1)} %add_convert_fusion), channel_id=1, source_target_pairs={{0,2},{2,0},{4,6},{6,4},{1,3},{3,1},{5,7},{7,5},{8,10},{10,8},{12,... | collective-permute-start | bytes 3145736 | tf_op jit(solution)/shard_map/ppermute | solution.py:48
  505.7 42.0 %collective-permute-start.45 = (bf16[1,256,2048]{2,1,0:T(8,128)(2,1)S(1)}, bf16[1,256,2048]{2,1,0:T(8,128)(2,1)S(1)}, u32[]{:S(2)}, u32[]{:S(2)}) collective-permute-start(bf16[1,256,2048]{2,1,0:T(8,128)(2,1)S(1)} %get-tuple-element.228), channel_id=1, source_target_pairs={{0,16},{8,24},{16,0},{24,8},{1,17},{9,25},{17,1},{25,9},{2,18},{10... | collective-permute-start | bytes 3145736 | tf_op jit(solution)/shard_map/ppermute | solution.py:48
  506.2 41.5 %collective-permute-start.49 = (bf16[1,256,2048]{2,1,0:T(8,128)(2,1)S(1)}, bf16[1,256,2048]{2,1,0:T(8,128)(2,1)S(1)}, u32[]{:S(2)}, u32[]{:S(2)}) collective-permute-start(bf16[1,256,2048]{2,1,0:T(8,128)(2,1)S(1)} %get-tuple-element.229), channel_id=1, source_target_pairs={{0,8},{8,0},{16,24},{24,16},{1,9},{9,1},{17,25},{25,17},{2,10},{10... | collective-permute-start | bytes 3145736 | tf_op jit(solution)/shard_map/ppermute | solution.py:48
  555.9 61.9 %collective-permute-start.53 = (bf16[4,4,64,2048]{3,2,1,0:T(8,128)(2,1)}, bf16[4,4,64,2048]{3,2,1,0:T(8,128)(2,1)}, u32[]{:S(2)}, u32[]{:S(2)}) collective-permute-start(bf16[4,4,64,2048]{3,2,1,0:T(8,128)(2,1)} %dynamic-slice_bitcast_fusion), channel_id=1, source_target_pairs={{0,1},{1,0},{2,3},{3,2},{4,5},{5,4},{6,7},{7,6},{8,9},{9,8},{10,11... | collective-permute-start | bytes 12582920 | tf_op jit(solution)/shard_map/ppermute | solution.py:48
  564.6 47.7 %collective-permute-start.51 = (bf16[2,256,2048]{2,1,0:T(8,128)(2,1)}, bf16[2,256,2048]{2,1,0:T(8,128)(2,1)}, u32[]{:S(2)}, u32[]{:S(2)}) collective-permute-start(bf16[2,256,2048]{2,1,0:T(8,128)(2,1)} %pad_maximum_fusion.2), channel_id=1, source_target_pairs={{0,16},{8,24},{16,0},{24,8},{1,17},{9,25},{17,1},{25,9},{2,18},{10... | collective-permute-start | bytes 6291464 | tf_op jit(solution)/shard_map/ppermute | solution.py:48
  566.3 47.5 %collective-permute-start.50 = (bf16[2,256,2048]{2,1,0:T(8,128)(2,1)}, bf16[2,256,2048]{2,1,0:T(8,128)(2,1)}, u32[]{:S(2)}, u32[]{:S(2)}) collective-permute-start(bf16[2,256,2048]{2,1,0:T(8,128)(2,1)} %pad_maximum_fusion.1), channel_id=1, source_target_pairs={{0,8},{8,0},{16,24},{24,16},{1,9},{9,1},{17,25},{25,17},{2,10},{10... | collective-permute-start | bytes 6291464 | tf_op jit(solution)/shard_map/ppermute | solution.py:48
  567.7 75.9 %all-to-all-start.1 = ((bf16[8,256,256]{2,1,0:T(8,128)(2,1)}), bf16[8,256,256]{2,1,0:T(8,128)(2,1)}, u32[]{:S(2)}, u32[]{:S(2)}) async-start(bf16[8,256,256]{2,1,0:T(8,128)(2,1)} %bitcast.384), calls=%async_computation.1 | async-start | bytes 2097152 | tf_op jit(solution)/shard_map/all_to_all | solution.py:766
  571.9 162.3 %reduce-scatter.8.cloned.1.call-start = ((), (), s32[]{:S(2)}) async-start(), calls=%async_computation.9 | async-start | bytes 3145728 | tf_op jit(solution)/shard_map/reduce_scatter | solution.py:281
  576.8 236.3 %reduce-scatter.4.cloned.1.call-start = ((), (), s32[]{:S(2)}) async-start(), calls=%async_computation.7 | async-start | bytes 9437184 | tf_op jit(solution)/shard_map/reduce_scatter | solution.py:773
  628.2 37.7 %collective-permute-start.52 = (bf16[256,2048]{1,0:T(8,128)(2,1)}, bf16[256,2048]{1,0:T(8,128)(2,1)}, u32[]{:S(2)}, u32[]{:S(2)}) collective-permute-start(bf16[256,2048]{1,0:T(8,128)(2,1)} %fusion.16), channel_id=1, source_target_pairs={{0,2},{2,0},{4,6},{6,4},{1,3},{3,1},{5,7},{7,5},{8,10},{10,8},{12,... | collective-permute-start | bytes 3145736 | tf_op jit(solution)/shard_map/ppermute | solution.py:48
  730.0 39.3 %collective-permute-start.63 = (bf16[2,64,2048]{2,1,0:T(8,128)(2,1)}, bf16[2,64,2048]{2,1,0:T(8,128)(2,1)}, u32[]{:S(2)}, u32[]{:S(2)}) collective-permute-start(bf16[2,64,2048]{2,1,0:T(8,128)(2,1)} %fusion.19), channel_id=1, source_target_pairs={{2,4},{4,2},{3,5},{5,3},{10,12},{12,10},{11,13},{13,11},{18,20},{2... | collective-permute-start | bytes 1572872 | tf_op jit(solution)/shard_map/ppermute | solution.py:52
  737.2 53.3 %all-to-all-start.2 = ((bf16[8,64,768]{2,1,0:T(8,128)(2,1)}), bf16[8,64,768]{2,1,0:T(8,128)(2,1)}, u32[]{:S(2)}, u32[]{:S(2)}) async-start(bf16[8,64,768]{2,1,0:T(8,128)(2,1)} %bitcast.389), calls=%async_computation.3 | async-start | bytes 1572864 | tf_op jit(solution)/shard_map/all_to_all | solution.py:794
  (115 other events, 1864.4 us)
Sparse Core Ops, SparseCore 0:
  9.6 43.6 all-gather.10
  69.4 79.3 all-gather.8
  168.4 56.9 all-gather.12
  275.9 54.6 all-gather.14
  504.0 55.0 reduce-scatter.5
  576.9 67.8 reduce-scatter.7
  682.9 128.9 reduce-scatter.3

commit v5 on v4

--- a/solution.py
+++ b/solution.py
@@ -298,14 +298,14 @@
         theirs = swap(pick(whole, 1 - self.core, 2), "fsdp", 1)
         whole = (pick(whole, self.core, 2).astype(f32) + theirs.astype(f32)).astype(bf16)
         self.out_parts = [pick(whole, self.dp ^ k) for k in range(4)]
-        return after(got, whole)
+        return got
 
     def before_norm(self, grad_qkv):
         own, other = scatter_sum(self.fed, self.fed_two)
         other = swap(other.astype(bf16), "seq", 1)
         self.feed_out = own + other.astype(f32)
         self.out_two = scatter_two(self.out_parts, scatter_one(self.out_parts))
-        return after(grad_qkv, other, *self.out_two)
+        return after(grad_qkv, other)
 
     def last(self, normed, grad_qkv):
         out_parts, out_two = self.out_parts, self.out_two

time: 836 us -> 850 us (1.017)
  waiting for transfers between devices: 299 us -> 322 us
    ppermute x67, waiting for transfers between devices: 238 us -> 272 us  [swap(): lax.ppermute(value, axis, [(i, i ^ mask) for i in range(lax.axis_size(axi...]
    all_to_all x1, waiting for transfers between devices: 21.2 us -> 0.01 us  [on_device(): lax.all_to_all(grad_qkv_w.reshape(n_line, share, 3 * cols), LINE, split_a...]
    all_to_all x1, waiting for transfers between devices: 0.01 us -> 13.6 us  [on_device(): lax.all_to_all(grad_context, LINE, split_axis=0, concat_axis=0, tiled=True)]
    unnamed x150 -> x148, local copies, waits for them, and re-layouts: 58.7 us -> 55.9 us
  transfers between devices with their start and end apart: 80 -> 80, of which waited for: 30 -> 35; matrix products, arithmetic and copies ran while one was open for 33% -> 32% of each run, Pallas kernels for 14% -> 14%
where the time goes in v5:
time: 850 us; the launch traced here: 839 us
  waiting for transfers between devices  322 us (38%)
  local copies, waits for them, and re-layouts  137 us (16%)
  Pallas kernels  128 us (15%)
  other arithmetic  90.6 us (11%)
  starting transfers between devices  86.4 us (10%)
  matrix products  60.5 us (7%)
  between operations  15.7 us (2%)
    ppermute x67, waiting for transfers between devices, swap(): lax.ppermute(value, axis, [(i, i ^ mask) for i in range(lax.axis_size(axi...  272 us
    ppermute x67, starting transfers between devices, swap(): lax.ppermute(value, axis, [(i, i ^ mask) for i in range(lax.axis_size(axi...  66.7 us
    dot_general x7, matrix products, dot(): lax.dot_general(left, right, (dims, ((), ())), preferred_element_type=f32)  60.5 us
    unnamed x148, local copies, waits for them, and re-layouts  55.9 us
    pallas_call x2, Pallas kernels, feed_forward(): call(feed_body, grid=(rows // tile,), in_specs=[part(width), part(width),...  38.4 us
    pallas_call x4, Pallas kernels, assemble(): call(body, in_specs=[pl.BlockSpec(memory_space=pltpu.SMEM)] + [pl.BlockSp...  22.1 us
    all_to_all x1, waiting for transfers between devices, on_device(): lax.all_to_all(context_own, LINE, split_axis=0, concat_axis=0, tiled=True)  21.5 us
    pallas_call x1, Pallas kernels, attend_back(): call(lambda *refs: attend_back_body(score_scale, heads, *refs), grid=(seq...  17.8 us
  transfers between devices with their start and end apart: 80, of which 35 were waited for; matrix products, arithmetic and copies ran while one was open for 32% of the time, Pallas kernels for 14%

profile of v5, /device:TPU:0, one launch (start us, length us, event | category | flops | bytes accessed | tf_op | source)
XLA Modules:
  0.0 839.3 jit_solution(8992003407847946819)
XLA Ops:
  28.6 18.4 %collective-permute-done.1 = bf16[2,80,768]{2,1,0:T(8,128)(2,1)S(1)} collective-permute-done((bf16[2,80,768]{2,1,0:T(8,128)(2,1)S(1)}, bf16[2,80,768]{2,1,0:T(8,128)(2,1)S(1)}, u32[]{:S(2)}, u32[]{:S(2)}) %collective-permute-start.1) | collective-permute-done | bytes 245792 | tf_op jit(solution)/shard_map/ppermute | solution.py:48
  79.2 24.8 %collective-permute-done.10 = bf16[128,2048]{1,0:T(8,128)(2,1)} collective-permute-done((bf16[128,2048]{1,0:T(8,128)(2,1)}, bf16[128,2048]{1,0:T(8,128)(2,1)}, u32[]{:S(2)}, u32[]{:S(2)}) %collective-permute-start.10) | collective-permute-done | bytes 524320 | tf_op jit(solution)/shard_map/ppermute | solution.py:48
  118.2 11.3 %collective-permute-done.11 = bf16[2,64,1024]{2,1,0:T(8,128)(2,1)S(1)} collective-permute-done((bf16[2,64,1024]{2,1,0:T(8,128)(2,1)}, bf16[2,64,1024]{2,1,0:T(8,128)(2,1)S(1)}, u32[]{:S(2)}, u32[]{:S(2)}) %collective-permute-start.11) | collective-permute-done | bytes 262176 | tf_op jit(solution)/shard_map/ppermute | solution.py:48
  148.1 15.3 %collective-permute-done.17 = bf16[4,64,2048]{2,1,0:T(8,128)(2,1)S(1)} collective-permute-done((bf16[4,64,2048]{2,1,0:T(8,128)(2,1)}, bf16[4,64,2048]{2,1,0:T(8,128)(2,1)S(1)}, u32[]{:S(2)}, u32[]{:S(2)}) %collective-permute-start.17) | collective-permute-done | bytes 1048608 | tf_op jit(solution)/shard_map/ppermute | solution.py:48
  175.4 16.0 %shard_map.272 = (bf16[2048,2048]{1,0:T(8,128)(2,1)}, bf16[2048,768]{1,0:T(8,128)(2,1)}) custom-call(bf16[2048,2048]{1,0:T(8,128)(2,1)} %bitcast.352, f32[1,2048]{1,0:T(1,128)} %slice.397.gain_ref, f32[1,2048]{1,0:T(1,128)} %slice.399.beta_ref, bf16[2048,768]{1,0:T(8,128)(2,1)} %bitcast.354, f32[1,768]{1,0:T(1,128)} %fusion.40.bias_ref), custom_call_target="tpu_custom_call" | custom-call | flops 6442450 | bytes 23068 | tf_op jit(solution)/shard_map/pallas_call | solution.py:467
  212.9 15.8 %collective-permute-done.22 = bf16[256,2048]{1,0:T(8,128)(2,1)S(1)} collective-permute-done((bf16[256,2048]{1,0:T(8,128)(2,1)}, bf16[256,2048]{1,0:T(8,128)(2,1)S(1)}, u32[]{:S(2)}, u32[]{:S(2)}) %collective-permute-start.22) | collective-permute-done | bytes 1048608 | tf_op jit(solution)/shard_map/ppermute | solution.py:48
  228.7 13.9 %shard_map.273 = (bf16[8,2,128,256]{3,2,1,0:T(8,128)(2,1)}, f32[2,1024,2]{2,1,0:T(8,128)}) custom-call(f32[1,2]{1,0:T(1,128)} %multiply_exponential_fusion.refs_0_, f32[2,1024,1]{2,1,0:T(8,128)} %copy.167.refs_1_, f32[2,1,1024]{2,1,0:T(1,128)} %bitcast.440, bf16[8,2,128,768]{3,2,1,0:T(8,128)(2,1)} %bitcast.361), custom_call_target="tpu_custom_call" | custom-call | flops 2147483 | bytes 4194 | tf_op jit(solution)/shard_map/pallas_call | solution.py:580
  253.6 21.5 %all-to-all-done = bf16[8,256,256]{1,2,0:T(8,128)(2,1)S(1)} async-done(((bf16[8,256,256]{1,2,0:T(8,128)(2,1)}), bf16[8,256,256]{1,2,0:T(8,128)(2,1)S(1)}, u32[]{:S(2)}, u32[]{:S(2)}) %all-to-all-start) | async-done | bytes 1048608 | tf_op jit(solution)/shard_map/all_to_all | solution.py:746
  304.4 13.3 %collective-permute-done.27 = bf16[256,2048]{1,0:T(8,128)(2,1)S(1)} collective-permute-done((bf16[256,2048]{1,0:T(8,128)(2,1)}, bf16[256,2048]{1,0:T(8,128)(2,1)S(1)}, u32[]{:S(2)}, u32[]{:S(2)}) %collective-permute-start.27) | collective-permute-done | bytes 1048608 | tf_op jit(solution)/shard_map/ppermute | solution.py:48
  332.9 12.5 %collective-permute-done.30 = bf16[256,2048]{1,0:T(8,128)(2,1)} collective-permute-done((bf16[256,2048]{1,0:T(8,128)(2,1)}, bf16[256,2048]{1,0:T(8,128)(2,1)}, u32[]{:S(2)}, u32[]{:S(2)}) %collective-permute-start.30) | collective-permute-done | bytes 1048608 | tf_op jit(solution)/shard_map/ppermute | solution.py:48
  372.8 19.3 %shard_map.277 = (bf16[1024,1024]{1,0:T(8,128)(2,1)}, bf16[1024,1024]{1,0:T(8,128)(2,1)}, bf16[1024,2048]{1,0:T(8,128)(2,1)}) custom-call(bf16[1024,2048]{1,0:T(8,128)(2,1)} %get-tuple-element.275.x_ref, bf16[1024,2048]{1,0:T(8,128)(2,1)} %get-tuple-element.283.dy_ref, bf16[2048,1024]{1,0:T(8,128)(2,1)} %bitcast.349, bf16[1024,2048]{1,0:T(8,128)(2,1)} %bitcast.346, ...), custom_call_target="tpu_custom_call" | custom-call | flops 12884901 | bytes 25165 | tf_op jit(solution)/shard_map/pallas_call | solution.py:670
  425.5 19.1 %shard_map.278 = (bf16[1024,1024]{1,0:T(8,128)(2,1)}, bf16[1024,1024]{1,0:T(8,128)(2,1)}, bf16[1024,2048]{1,0:T(8,128)(2,1)}) custom-call(bf16[1024,2048]{1,0:T(8,128)(2,1)} %get-tuple-element.140.x_ref, bf16[1024,2048]{1,0:T(8,128)(2,1)} %get-tuple-element.279.dy_ref, bf16[2048,1024]{1,0:T(8,128)(2,1)} %bitcast.350, bf16[1024,2048]{1,0:T(8,128)(2,1)} %bitcast.347, ...), custom_call_target="tpu_custom_call" | custom-call | flops 12884901 | bytes 25165 | tf_op jit(solution)/shard_map/pallas_call | solution.py:670
  450.1 11.9 %convolution_convert_fusion.2 = bf16[1024,2048]{1,0:T(8,128)(2,1)S(1)} fusion(bf16[2048,1024]{1,0:T(8,128)(2,1)S(1)} %copy-done.40, bf16[2048,2048]{1,0:T(8,128)(2,1)} %get-tuple-element.278), kind=kOutput, calls=%fused_computation.14 | convolution fusion | flops 8592031744 | bytes 16777216 | tf_op jit(solution)/shard_map/dot_general | solution.py:18
  469.3 10.7 %convolution_convert_fusion.1 = bf16[2048,2048]{1,0:T(8,128)(2,1)S(1)} fusion(bf16[2048,1024]{1,0:T(8,128)(2,1)} %constant_dynamic-update-slice_fusion.20, bf16[1024,2048]{1,0:T(8,128)(2,1)S(1)} %bitcast.348), kind=kOutput, calls=%fused_computation.4 | convolution fusion | flops 8594128896 | bytes 16777216 | tf_op jit(solution)/shard_map/dot_general | solution.py:18
  480.0 14.4 %convolution_convert_fusion.3 = bf16[2048,1024]{1,0:T(8,128)(2,1)S(1)} fusion(bf16[2048,2048]{1,0:T(8,128)(2,1)} %get-tuple-element.270, bf16[2048,1024]{1,0:T(8,128)(2,1)S(1)} %constant_dynamic-update-slice_fusion.42), kind=kOutput, calls=%fused_computation.15 | convolution fusion | flops 8592031744 | bytes 16777216 | tf_op jit(solution)/shard_map/dot_general | solution.py:18
  511.4 32.1 %collective-permute-done.46 = bf16[256,2048]{1,0:T(8,128)(2,1)} collective-permute-done((bf16[256,2048]{1,0:T(8,128)(2,1)}, bf16[256,2048]{1,0:T(8,128)(2,1)}, u32[]{:S(2)}, u32[]{:S(2)}) %collective-permute-start.46) | collective-permute-done | bytes 1048608 | tf_op jit(solution)/shard_map/ppermute | solution.py:48
  568.6 36.5 %collective-permute-done.51 = bf16[2,256,2048]{2,1,0:T(8,128)(2,1)} collective-permute-done((bf16[2,256,2048]{2,1,0:T(8,128)(2,1)}, bf16[2,256,2048]{2,1,0:T(8,128)(2,1)}, u32[]{:S(2)}, u32[]{:S(2)}) %collective-permute-start.51) | collective-permute-done | bytes 2097184 | tf_op jit(solution)/shard_map/ppermute | solution.py:48
  614.5 13.6 %all-to-all-done.1 = bf16[8,256,256]{2,1,0:T(8,128)(2,1)} async-done(((bf16[8,256,256]{2,1,0:T(8,128)(2,1)}), bf16[8,256,256]{2,1,0:T(8,128)(2,1)}, u32[]{:S(2)}, u32[]{:S(2)}) %all-to-all-start.1) | async-done | bytes 1048608 | tf_op jit(solution)/shard_map/all_to_all | solution.py:766
  628.1 17.8 %shard_map.279 = bf16[8,2,128,768]{3,2,1,0:T(8,128)(2,1)} custom-call(f32[1,2]{1,0:T(1,128)} %multiply_exponential_fusion.refs_0_, f32[2,1024,1]{2,1,0:T(8,128)} %copy.167.refs_1_, f32[2,1,1024]{2,1,0:T(1,128)} %bitcast.441, bf16[8,2,128,768]{3,2,1,0:T(8,128)(2,1)} %bitcast.362, bf16[8,2,128,256]{3,2,1,0:T(8,128)(2,1)} %bitcast.99.refs_4_, ...), custom_call_target="tpu_custom_call" | custom-call | flops 5368709 | bytes 7340 | tf_op jit(solution)/shard_map/pallas_call | solution.py:602
  645.9 14.4 %collective-permute-done.52 = bf16[256,2048]{1,0:T(8,128)(2,1)} collective-permute-done((bf16[256,2048]{1,0:T(8,128)(2,1)}, bf16[256,2048]{1,0:T(8,128)(2,1)}, u32[]{:S(2)}, u32[]{:S(2)}) %collective-permute-start.52) | collective-permute-done | bytes 1048608 | tf_op jit(solution)/shard_map/ppermute | solution.py:48
  660.3 17.1 %shard_map.280 = (bf16[2048,2048]{1,0:T(8,128)(2,1)}, f32[1,2048]{1,0:T(1,128)}, f32[1,2048]{1,0:T(1,128)}) custom-call(bf16[2048,768]{1,0:T(8,128)(2,1)} %bitcast.356, bf16[2048,768]{1,0:T(8,128)(2,1)} %bitcast.355, bf16[2048,2048]{1,0:T(8,128)(2,1)} %bitcast.353), custom_call_target="tpu_custom_call" | custom-call | flops 6442450 | bytes 23068 | tf_op jit(solution)/shard_map/pallas_call | solution.py:637
  689.5 11.0 %convolution_convert_fusion.4 = bf16[2048,768]{1,0:T(8,128)(2,1)S(1)} fusion(bf16[2048,2048]{1,0:T(8,128)(2,1)} %get-tuple-element.161, bf16[2048,768]{1,0:T(8,128)(2,1)} %bitcast.357), kind=kOutput, calls=%fused_computation.16 | convolution fusion | flops 6444023808 | bytes 14680064 | tf_op jit(solution)/shard_map/dot_general | solution.py:18
  729.8 11.0 %collective-permute-done.56 = bf16[512,768]{1,0:T(8,128)(2,1)} collective-permute-done((bf16[512,768]{1,0:T(8,128)(2,1)}, bf16[512,768]{1,0:T(8,128)(2,1)}, u32[]{:S(2)}, u32[]{:S(2)}) %collective-permute-start.56) | collective-permute-done | bytes 786464 | tf_op jit(solution)/shard_map/ppermute | solution.py:48
  772.7 12.3 %collective-permute-done.62 = bf16[2,64,2048]{2,1,0:T(8,128)(2,1)S(1)} collective-permute-done((bf16[2,64,2048]{2,1,0:T(8,128)(2,1)S(1)}, bf16[2,64,2048]{2,1,0:T(8,128)(2,1)S(1)}, u32[]{:S(2)}, u32[]{:S(2)}) %collective-permute-start.62) | collective-permute-done | bytes 524320 | tf_op jit(solution)/shard_map/ppermute | solution.py:52
  (508 shorter events, 419.5 us)
Async XLA Ops:
  7.2 133.5 %all-gather.11.cloned.1.call-start = ((), (), s32[]{:S(2)}) async-start(), calls=%async_computation.11 | async-start | bytes 1310720 | tf_op jit(solution)/shard_map/all_gather | solution.py:147
  7.9 160.3 %all-gather.9.cloned.1.call-start = ((), (), s32[]{:S(2)}) async-start(), calls=%async_computation.10 | async-start | bytes 9437184 | tf_op jit(solution)/shard_map/all_gather | solution.py:150
  14.5 54.0 %collective-permute-start.5 = (bf16[256,2048]{1,0:T(8,128)(2,1)S(1)}, bf16[256,2048]{1,0:T(8,128)(2,1)}, u32[]{:S(2)}, u32[]{:S(2)}) collective-permute-start(bf16[256,2048]{1,0:T(8,128)(2,1)S(1)} %bitcast.366), channel_id=1, source_target_pairs={{0,16},{8,24},{16,0},{24,8},{1,17},{9,25},{17,1},{25,9},{2,18},{10... | collective-permute-start | bytes 3145736 | tf_op jit(solution)/shard_map/ppermute | solution.py:48
  17.0 52.3 %collective-permute-start.4 = (bf16[256,2048]{1,0:T(8,128)(2,1)S(1)}, bf16[256,2048]{1,0:T(8,128)(2,1)}, u32[]{:S(2)}, u32[]{:S(2)}) collective-permute-start(bf16[256,2048]{1,0:T(8,128)(2,1)S(1)} %bitcast.367), channel_id=1, source_target_pairs={{0,8},{8,0},{16,24},{24,16},{1,9},{9,1},{17,25},{25,17},{2,10},{10... | collective-permute-start | bytes 3145736 | tf_op jit(solution)/shard_map/ppermute | solution.py:48
  25.5 42.9 %collective-permute-start.6 = (bf16[4,64,1024]{2,1,0:T(8,128)(2,1)S(1)}, bf16[4,64,1024]{2,1,0:T(8,128)(2,1)S(1)}, u32[]{:S(2)}, u32[]{:S(2)}) collective-permute-start(bf16[4,64,1024]{2,1,0:T(8,128)(2,1)S(1)} %bitcast.414), channel_id=1, source_target_pairs={{0,2},{2,0},{4,6},{6,4},{1,3},{3,1},{5,7},{7,5},{8,10},{10,8},{12,... | collective-permute-start | bytes 1572872 | tf_op jit(solution)/shard_map/ppermute | solution.py:48
  69.3 159.4 %all-gather.13.cloned.1.call-start = ((), (), s32[]{:S(2)}) async-start(), calls=%async_computation.12 | async-start | bytes 3145728 | tf_op jit(solution)/shard_map/all_gather | solution.py:185
  248.5 82.4 %all-gather.15.cloned.1.call-start = ((), (), s32[]{:S(2)}) async-start(), calls=%async_computation.13 | async-start | bytes 3145728 | tf_op jit(solution)/shard_map/all_gather | solution.py:206
  276.1 468.8 %reduce-scatter.6.cloned.1.call-start = ((), (), s32[]{:S(2)}) async-start(), calls=%async_computation.8 | async-start | bytes 3145728 | tf_op jit(solution)/shard_map/reduce_scatter | solution.py:281
  299.4 46.0 %collective-permute-start.30 = (bf16[256,2048]{1,0:T(8,128)(2,1)}, bf16[256,2048]{1,0:T(8,128)(2,1)}, u32[]{:S(2)}, u32[]{:S(2)}) collective-permute-start(bf16[256,2048]{1,0:T(8,128)(2,1)} %get-tuple-element.192), channel_id=1, source_target_pairs={{0,2},{2,0},{4,6},{6,4},{1,3},{3,1},{5,7},{7,5},{8,10},{10,8},{12,... | collective-permute-start | bytes 3145736 | tf_op jit(solution)/shard_map/ppermute | solution.py:48
  353.9 44.9 %collective-permute-start.34 = (bf16[256,2048]{1,0:T(8,128)(2,1)}, bf16[256,2048]{1,0:T(8,128)(2,1)}, u32[]{:S(2)}, u32[]{:S(2)}) collective-permute-start(bf16[256,2048]{1,0:T(8,128)(2,1)} %collective-permute-done.30), channel_id=1, source_target_pairs={{0,16},{8,24},{16,0},{24,8},{1,17},{9,25},{17,1},{25,9},{2,18},{10... | collective-permute-start | bytes 3145736 | tf_op jit(solution)/shard_map/ppermute | solution.py:48
  354.5 47.0 %collective-permute-start.33 = (bf16[256,2048]{1,0:T(8,128)(2,1)}, bf16[256,2048]{1,0:T(8,128)(2,1)}, u32[]{:S(2)}, u32[]{:S(2)}) collective-permute-start(bf16[256,2048]{1,0:T(8,128)(2,1)} %collective-permute-done.30), channel_id=1, source_target_pairs={{0,8},{8,0},{16,24},{24,16},{1,9},{9,1},{17,25},{25,17},{2,10},{10... | collective-permute-start | bytes 3145736 | tf_op jit(solution)/shard_map/ppermute | solution.py:48
  463.6 40.1 %collective-permute-start.47 = (bf16[2,256,2048]{2,1,0:T(8,128)(2,1)}, bf16[2,256,2048]{2,1,0:T(8,128)(2,1)}, u32[]{:S(2)}, u32[]{:S(2)}) collective-permute-start(bf16[2,256,2048]{2,1,0:T(8,128)(2,1)} %dynamic-slice_bitcast_fusion.1), channel_id=1, source_target_pairs={{0,1},{1,0},{2,3},{3,2},{4,5},{5,4},{6,7},{7,6},{8,9},{9,8},{10,11... | collective-permute-start | bytes 6291464 | tf_op jit(solution)/shard_map/ppermute | solution.py:48
  497.8 62.3 %collective-permute-start.48 = (bf16[4,2,2,64,1024]{4,3,2,0,1:T(8,128)(2,1)}, bf16[4,2,2,64,1024]{4,3,2,0,1:T(8,128)(2,1)}, u32[]{:S(2)}, u32[]{:S(2)}) collective-permute-start(bf16[4,2,2,64,1024]{4,3,2,0,1:T(8,128)(2,1)} %bitcast.326), channel_id=1, source_target_pairs={{0,1},{1,0},{2,3},{3,2},{4,5},{5,4},{6,7},{7,6},{8,9},{9,8},{10,11... | collective-permute-start | bytes 6291464 | tf_op jit(solution)/shard_map/ppermute | solution.py:48
  503.7 39.9 %collective-permute-start.46 = (bf16[256,2048]{1,0:T(8,128)(2,1)}, bf16[256,2048]{1,0:T(8,128)(2,1)}, u32[]{:S(2)}, u32[]{:S(2)}) collective-permute-start(bf16[256,2048]{1,0:T(8,128)(2,1)} %add_convert_fusion), channel_id=1, source_target_pairs={{0,2},{2,0},{4,6},{6,4},{1,3},{3,1},{5,7},{7,5},{8,10},{10,8},{12,... | collective-permute-start | bytes 3145736 | tf_op jit(solution)/shard_map/ppermute | solution.py:48
  507.5 247.8 %reduce-scatter.8.cloned.1.call-start = ((), (), s32[]{:S(2)}) async-start(), calls=%async_computation.9 | async-start | bytes 3145728 | tf_op jit(solution)/shard_map/reduce_scatter | solution.py:281
  509.5 44.4 %collective-permute-start.45 = (bf16[1,256,2048]{2,1,0:T(8,128)(2,1)S(1)}, bf16[1,256,2048]{2,1,0:T(8,128)(2,1)S(1)}, u32[]{:S(2)}, u32[]{:S(2)}) collective-permute-start(bf16[1,256,2048]{2,1,0:T(8,128)(2,1)S(1)} %get-tuple-element.226), channel_id=1, source_target_pairs={{0,16},{8,24},{16,0},{24,8},{1,17},{9,25},{17,1},{25,9},{2,18},{10... | collective-permute-start | bytes 3145736 | tf_op jit(solution)/shard_map/ppermute | solution.py:48
  510.0 43.9 %collective-permute-start.49 = (bf16[1,256,2048]{2,1,0:T(8,128)(2,1)S(1)}, bf16[1,256,2048]{2,1,0:T(8,128)(2,1)S(1)}, u32[]{:S(2)}, u32[]{:S(2)}) collective-permute-start(bf16[1,256,2048]{2,1,0:T(8,128)(2,1)S(1)} %get-tuple-element.227), channel_id=1, source_target_pairs={{0,8},{8,0},{16,24},{24,16},{1,9},{9,1},{17,25},{25,17},{2,10},{10... | collective-permute-start | bytes 3145736 | tf_op jit(solution)/shard_map/ppermute | solution.py:48
  557.8 47.3 %collective-permute-start.51 = (bf16[2,256,2048]{2,1,0:T(8,128)(2,1)}, bf16[2,256,2048]{2,1,0:T(8,128)(2,1)}, u32[]{:S(2)}, u32[]{:S(2)}) collective-permute-start(bf16[2,256,2048]{2,1,0:T(8,128)(2,1)} %pad_maximum_fusion.2), channel_id=1, source_target_pairs={{0,16},{8,24},{16,0},{24,8},{1,17},{9,25},{17,1},{25,9},{2,18},{10... | collective-permute-start | bytes 6291464 | tf_op jit(solution)/shard_map/ppermute | solution.py:48
  559.3 47.3 %collective-permute-start.50 = (bf16[2,256,2048]{2,1,0:T(8,128)(2,1)}, bf16[2,256,2048]{2,1,0:T(8,128)(2,1)}, u32[]{:S(2)}, u32[]{:S(2)}) collective-permute-start(bf16[2,256,2048]{2,1,0:T(8,128)(2,1)} %pad_maximum_fusion.1), channel_id=1, source_target_pairs={{0,8},{8,0},{16,24},{24,16},{1,9},{9,1},{17,25},{25,17},{2,10},{10... | collective-permute-start | bytes 6291464 | tf_op jit(solution)/shard_map/ppermute | solution.py:48
  564.0 64.1 %all-to-all-start.1 = ((bf16[8,256,256]{2,1,0:T(8,128)(2,1)}), bf16[8,256,256]{2,1,0:T(8,128)(2,1)}, u32[]{:S(2)}, u32[]{:S(2)}) async-start(bf16[8,256,256]{2,1,0:T(8,128)(2,1)} %bitcast.384), calls=%async_computation.1 | async-start | bytes 2097152 | tf_op jit(solution)/shard_map/all_to_all | solution.py:766
  568.3 258.7 %reduce-scatter.4.cloned.1.call-start = ((), (), s32[]{:S(2)}) async-start(), calls=%async_computation.7 | async-start | bytes 9437184 | tf_op jit(solution)/shard_map/reduce_scatter | solution.py:773
  613.8 46.5 %collective-permute-start.52 = (bf16[256,2048]{1,0:T(8,128)(2,1)}, bf16[256,2048]{1,0:T(8,128)(2,1)}, u32[]{:S(2)}, u32[]{:S(2)}) collective-permute-start(bf16[256,2048]{1,0:T(8,128)(2,1)} %fusion.16), channel_id=1, source_target_pairs={{0,2},{2,0},{4,6},{6,4},{1,3},{3,1},{5,7},{7,5},{8,10},{10,8},{12,... | collective-permute-start | bytes 3145736 | tf_op jit(solution)/shard_map/ppermute | solution.py:48
  751.0 51.2 %all-to-all-start.2 = ((bf16[8,64,768]{2,1,0:T(8,128)(2,1)}), bf16[8,64,768]{2,1,0:T(8,128)(2,1)}, u32[]{:S(2)}, u32[]{:S(2)}) async-start(bf16[8,64,768]{2,1,0:T(8,128)(2,1)} %bitcast.389), calls=%async_computation.3 | async-start | bytes 1572864 | tf_op jit(solution)/shard_map/all_to_all | solution.py:794
  757.5 36.7 %collective-permute-start.67 = (bf16[2,64,1024]{2,1,0:T(8,128)(2,1)}, bf16[2,64,1024]{2,1,0:T(8,128)(2,1)}, u32[]{:S(2)}, u32[]{:S(2)}) collective-permute-start(bf16[2,64,1024]{2,1,0:T(8,128)(2,1)} %get-tuple-element.231), channel_id=1, source_target_pairs={{0,24},{8,16},{16,8},{24,0},{1,25},{9,17},{17,9},{25,1},{2,26},{10... | collective-permute-start | bytes 786440 | tf_op jit(solution)/shard_map/ppermute | solution.py:48
  (114 other events, 1979.2 us)
Sparse Core Ops, SparseCore 0:
  9.6 43.6 all-gather.10
  69.4 79.4 all-gather.8
  168.4 56.9 all-gather.12
  276.3 54.5 all-gather.14
  507.6 55.1 reduce-scatter.5
  564.9 76.2 reduce-scatter.7
  677.6 93.0 reduce-scatter.3
